TPU v7x, 32 devices: a whole 2x2x4 slice. The times are simulated.
32 devices in a mesh: shard: 16 (over z, x, core), seq: 2 (over y).
Axes of the slice: x: 2, y: 2, z: 4, core: 2. Of those that a mesh axis runs over, the one named last changes fastest.
Arguments:
- stream: bfloat16 [8192, 1536], P(('shard', 'seq')), may hold values from -6 to 6
- doc_starts: int32 [10], replicated, may hold values from 0 to 8191, as said below
- expert_routes: int32 [8192, 4], P(('shard', 'seq')), may hold values from 0 to 7, all different within a row; in each aligned block of 256 rows (0 to 255, 256 to 511, ...) at most 192 rows name the same one
- attn_gain: bfloat16 [1536], P('shard'), may hold values from 0.5 to 1.5
- w_query: bfloat16 [1536, 1536], P('shard'), may hold values from -0.15625 to 0.15625
- key_projection: bfloat16 [1536, 256], P('shard'), may hold values from -0.15625 to 0.15625
- value_projection: bfloat16 [1536, 256], P('shard'), may hold values from -0.15625 to 0.15625
- w_out: bfloat16 [1536, 1536], P('shard'), may hold values from -3.5 to 3.5
- ffn_gain: bfloat16 [1536], P('shard'), may hold values from 0.5 to 1.5
- w_router: bfloat16 [1536, 8], P('shard'), may hold values from -0.078125 to 0.078125
- w_gate: bfloat16 [8, 1536, 768], P(None, 'shard'), may hold values from -0.15625 to 0.15625
- w_up: bfloat16 [8, 1536, 768], P(None, 'shard'), may hold values from -0.15625 to 0.15625
- w_down: bfloat16 [8, 768, 1536], P(None, 'shard'), may hold values from -1.25 to 1.25
- out_grad: bfloat16 [8192, 1536], P(('shard', 'seq')), may hold values from -6 to 6
Outputs:
- result: bfloat16 [8192, 1536], P(('shard', 'seq'))
- stream_grad: bfloat16 [8192, 1536], P(('shard', 'seq'))
- attn_gain_grad: float32 [1536], P('shard')
- w_query_grad: float32 [1536, 1536], P('shard')
- w_key_grad: float32 [1536, 256], P('shard')
- w_value_grad: float32 [1536, 256], P('shard')
- w_out_grad: float32 [1536, 1536], P('shard')
- ffn_gain_grad: float32 [1536], P('shard')
- w_router_grad: float32 [1536, 8], P('shard')
- w_gate_grad: float32 [8, 1536, 768], P(None, 'shard')
- w_up_grad: float32 [8, 1536, 768], P(None, 'shard')
- w_down_grad: float32 [8, 768, 1536], P(None, 'shard')
Inputs may be any that keep to these rules, and one draw needn't show every extreme that they name: `doc_starts`: strictly increasing starts, the first 0; a document runs from its start to the next start or to the stream's end and holds at most 16384 tokens; the last document is the stream's last token alone. `expert_routes`: each row names 4 different experts; among the 256 rows of one device no expert is named by more than 192 rows, and in every draw some expert is named by exactly 192 rows of some device.
All inputs are finite; a program needn't handle non-finite values.
Results may differ from a plain program's by a relative error of at most 0.02.
Values may be sent and summed in bfloat16 or wider, within the bound.
A program may use at most 448 MiB of HBM per device.

v0:
```python
import jax
import jax.numpy as jnp
from jax import lax
from jax.sharding import PartitionSpec as P

MODEL_WIDTH = 1536
QUERY_HEADS = 12
KEY_VALUE_HEADS = 2
HEAD_SIZE = 128
E = 8
MOST = 192


norm_eps = 1e-06
rope_base = 10000.0
contract_rows = (((0,), (0,)), ((), ()))
contract_cols = (((1,), (1,)), ((), ()))


def rms_scale(values, gain):
    return values * lax.rsqrt(jnp.mean(values * values, axis=-1, keepdims=True) + norm_eps) * gain


def segment_info(tok_index, starts):
    inside = starts[None, :] <= tok_index[:, None]
    segment = jnp.sum(inside.astype(jnp.int32), axis=1) - 1
    doc_first = jnp.max(jnp.where(inside, starts[None, :], 0), axis=1)
    return (segment, tok_index - doc_first)


def rope_angles(position, head_width):
    half_width = head_width // 2
    inv_freq = rope_base ** (-(jnp.arange(half_width, dtype=jnp.float32) * 2.0) / head_width)
    return position.astype(jnp.float32)[:, None] * inv_freq[None, :]


def apply_rotary(values, rotary_angle):
    half_width = values.shape[-1] // 2
    cosine = jnp.cos(rotary_angle)[:, None, :]
    sine_part = jnp.sin(rotary_angle)[:, None, :]
    lower, second = (values[..., :half_width], values[..., half_width:])
    return jnp.concatenate(
        [lower * cosine - second * sine_part, second * cosine + lower * sine_part], axis=-1
    )


def invert_rotary(grads_in, rotary_angle):
    half_width = grads_in.shape[-1] // 2
    cosine = jnp.cos(rotary_angle)[:, None, :]
    sine_part = jnp.sin(rotary_angle)[:, None, :]
    lower, second = (grads_in[..., :half_width], grads_in[..., half_width:])
    return jnp.concatenate(
        [lower * cosine + second * sine_part, second * cosine - lower * sine_part], axis=-1
    )


def gelu_product(gate_pre, up_pre):
    return jax.nn.gelu(gate_pre, approximate=False) * up_pre


def sub_rows(row_count):
    for block_size in (1024, 512):
        return block_size
    return row_count


def keep_state(fold_carry):
    return fold_carry


def local(
    stream,
    doc_starts,
    expert_routes,
    attn_gain,
    w_query,
    key_projection,
    value_projection,
    w_out,
    ffn_gain,
    w_router,
    w_gate,
    w_up,
    w_down,
    out_grad,
):
    tokens_per_device = stream.shape[0]
    sequence_count = lax.axis_size("seq")
    shard_count = lax.axis_size("shard")
    shard_place = lax.axis_index("shard")
    seq_place = lax.axis_index("seq")
    local_key_value = KEY_VALUE_HEADS // sequence_count
    query_group = QUERY_HEADS // KEY_VALUE_HEADS
    head_rows = tokens_per_device * sequence_count
    score_scale = HEAD_SIZE ** (-0.5)
    gain_a, query_w, key_matrix, value_w, out_w, gain_f, router_w, gate_w, up_w, down_w = (
        lax.all_gather(attn_gain, "shard", axis=0, tiled=True),
        lax.all_gather(w_query, "shard", axis=0, tiled=True),
        lax.all_gather(key_projection, "shard", axis=0, tiled=True),
        lax.all_gather(value_projection, "shard", axis=0, tiled=True),
        lax.all_gather(w_out, "shard", axis=0, tiled=True),
        lax.all_gather(ffn_gain, "shard", axis=0, tiled=True),
        lax.all_gather(w_router, "shard", axis=0, tiled=True),
        lax.all_gather(w_gate, "shard", axis=1, tiled=True),
        lax.all_gather(w_up, "shard", axis=1, tiled=True),
        lax.all_gather(w_down, "shard", axis=1, tiled=True),
    )
    own_index = (shard_place * sequence_count + seq_place) * tokens_per_device + jnp.arange(
        tokens_per_device, dtype=jnp.int32
    )
    own_segment, own_position = segment_info(own_index, doc_starts)
    rotary_angle = rope_angles(own_position, HEAD_SIZE)
    stream_f = stream.astype(jnp.float32)
    normed_f, attn_norm_pull = jax.vjp(rms_scale, stream_f, gain_a.astype(jnp.float32))
    normalized_input = normed_f.astype(jnp.bfloat16)
    query_raw = jnp.dot(normalized_input, query_w, preferred_element_type=jnp.float32).reshape(
        tokens_per_device, QUERY_HEADS, HEAD_SIZE
    )
    rotated_query = (
        apply_rotary(query_raw, rotary_angle)
        .astype(jnp.bfloat16)
        .reshape(tokens_per_device, QUERY_HEADS * HEAD_SIZE)
    )
    unrotated_key = jnp.dot(
        normalized_input, key_matrix, preferred_element_type=jnp.float32
    ).reshape(tokens_per_device, KEY_VALUE_HEADS, HEAD_SIZE)
    rotated_key = (
        apply_rotary(unrotated_key, rotary_angle)
        .astype(jnp.bfloat16)
        .reshape(tokens_per_device, KEY_VALUE_HEADS * HEAD_SIZE)
    )
    value_low = jnp.dot(normalized_input, value_w, preferred_element_type=jnp.float32).astype(
        jnp.bfloat16
    )
    head_query, head_key, head_value = (
        lax.all_to_all(rotated_query, "seq", split_axis=1, concat_axis=0, tiled=True),
        lax.all_to_all(rotated_key, "seq", split_axis=1, concat_axis=0, tiled=True),
        lax.all_to_all(value_low, "seq", split_axis=1, concat_axis=0, tiled=True),
    )
    query_four = head_query.reshape(head_rows, local_key_value, query_group, HEAD_SIZE)
    query_index = shard_place * head_rows + jnp.arange(head_rows, dtype=jnp.int32)
    query_segment, ignored = segment_info(query_index, doc_starts)

    def block_scores(key_block, key_start):
        row_count = key_block.shape[0]
        key_index = key_start + jnp.arange(row_count, dtype=jnp.int32)
        key_segment, unused_pos = segment_info(key_index, doc_starts)
        raw_scores = jnp.einsum(
            "qkgd,tkd->kgqt", query_four, key_block, preferred_element_type=jnp.float32
        )
        allowed = (key_index[None, :] <= query_index[:, None]) & (
            key_segment[None, :] == query_segment[:, None]
        )
        return (raw_scores * score_scale, allowed)

    def reachable(key_start, row_count):
        last_segment = jnp.sum((doc_starts <= key_start + row_count - 1).astype(jnp.int32)) - 1
        return (key_start <= query_index[head_rows - 1]) & (last_segment >= query_segment[0])

    start_top = jnp.full((local_key_value, query_group, head_rows), -1e30, jnp.float32)
    start_total = jnp.zeros((local_key_value, query_group, head_rows), jnp.float32)
    start_summed = jnp.zeros((local_key_value, query_group, head_rows, HEAD_SIZE), jnp.float32)
    fold_state = (start_top, start_total, start_summed)
    key_all = lax.all_gather(head_key, "shard", axis=0, tiled=True)
    value_all = lax.all_gather(head_value, "shard", axis=0, tiled=True)
    row_count = key_all.shape[0]
    block_size = sub_rows(row_count)
    key_steps = key_all.reshape(row_count // block_size, block_size, local_key_value, HEAD_SIZE)
    value_steps = value_all.reshape(row_count // block_size, block_size, local_key_value, HEAD_SIZE)
    offsets = jnp.arange(row_count // block_size, dtype=jnp.int32) * block_size

    def forward_key_step(fold_carry, block_item):
        key_block, value_block, offset = block_item
        key_start = offset

        def forward_update(acc_state):
            row_top, row_total, summed = acc_state
            scores, allowed = block_scores(key_block, key_start)
            masked = jnp.where(allowed, scores, -1e30)
            new_top = jnp.maximum(row_top, jnp.max(masked, axis=-1))
            weights = jnp.where(allowed, jnp.exp(masked - new_top[..., None]), 0.0)
            factor = jnp.exp(row_top - new_top)
            row_total = row_total * factor + jnp.sum(weights, axis=-1)
            summed = summed * factor[..., None] + jnp.einsum(
                "kgqt,tkd->kgqd",
                weights.astype(jnp.bfloat16),
                value_block,
                preferred_element_type=jnp.float32,
            )
            return (new_top, row_total, summed)

        return (
            lax.cond(reachable(key_start, block_size), forward_update, keep_state, fold_carry),
            None,
        )

    fold_state, unused_out = lax.scan(
        forward_key_step, fold_state, (key_steps, value_steps, offsets)
    )
    row_top, row_total, summed = fold_state
    attended_f = summed / row_total[..., None]
    head_out = (
        attended_f.transpose(2, 0, 1, 3)
        .reshape(head_rows, local_key_value * query_group * HEAD_SIZE)
        .astype(jnp.bfloat16)
    )
    mixed_heads = lax.all_to_all(head_out, "seq", split_axis=0, concat_axis=1, tiled=True)
    middle = stream_f + jnp.dot(mixed_heads, out_w, preferred_element_type=jnp.float32)
    normed_ffn_f, ffn_norm_pull = jax.vjp(rms_scale, middle, gain_f.astype(jnp.float32))
    normed_ffn = normed_ffn_f.astype(jnp.bfloat16)
    logits = jnp.dot(normed_ffn, router_w, preferred_element_type=jnp.float32)
    router_probs = jax.nn.softmax(logits, axis=-1)
    expert_ids = jnp.arange(E, dtype=jnp.int32)
    chosen = jnp.sum(
        (expert_routes[:, :, None] == expert_ids[None, None, :]).astype(jnp.int32), axis=1
    )
    slot_rank = jnp.cumsum(chosen, axis=0) - 1
    slot_ids = jnp.arange(MOST, dtype=jnp.int32)
    dispatch = (
        (slot_rank.T[:, None, :] == slot_ids[None, :, None]) & (chosen.T[:, None, :] == 1)
    ).astype(jnp.int32)
    token_ids = jnp.arange(tokens_per_device, dtype=jnp.int32)
    slot_token = jnp.sum(dispatch * token_ids[None, None, :], axis=-1)
    slot_valid = jnp.sum(dispatch, axis=-1).astype(jnp.float32)
    flat_token = slot_token.reshape(E * MOST)
    flat_expert = jnp.broadcast_to(expert_ids[:, None], (E, MOST)).reshape(E * MOST)
    chosen_f = chosen.astype(jnp.float32)
    slot_rows = jnp.take(normed_ffn, flat_token, axis=0).reshape(E, MOST, MODEL_WIDTH) * slot_valid[
        ..., None
    ].astype(jnp.bfloat16)
    gate_table = (router_probs * chosen_f).T
    slot_gates = jnp.take_along_axis(gate_table, slot_token, axis=1) * slot_valid
    gate_pre = jnp.einsum("ecd,edf->ecf", slot_rows, gate_w, preferred_element_type=jnp.float32)
    up_pre = jnp.einsum("ecd,edf->ecf", slot_rows, up_w, preferred_element_type=jnp.float32)
    active_f, gelu_pull = jax.vjp(gelu_product, gate_pre, up_pre)
    active = active_f.astype(jnp.bfloat16)
    expert_out = jnp.einsum("ecf,efd->ecd", active, down_w, preferred_element_type=jnp.float32)
    mixture = (
        jnp.zeros((tokens_per_device, MODEL_WIDTH), jnp.float32)
        .at[flat_token]
        .add((expert_out * slot_gates[..., None]).reshape(E * MOST, MODEL_WIDTH))
    )
    result = (middle + mixture).astype(jnp.bfloat16)
    grad_result = out_grad.astype(jnp.float32)
    slot_grad = jnp.take(grad_result, flat_token, axis=0).reshape(E, MOST, MODEL_WIDTH)
    expert_grad = (slot_grad * slot_gates[..., None]).astype(jnp.bfloat16)
    slot_gate_grad = jnp.sum(slot_grad * expert_out, axis=-1) * slot_valid
    prob_grad = (
        jnp.zeros((tokens_per_device, E), jnp.float32)
        .at[flat_token, flat_expert]
        .add(slot_gate_grad.reshape(E * MOST))
        * chosen_f
    )
    logit_grad = (
        router_probs * (prob_grad - jnp.sum(prob_grad * router_probs, axis=-1, keepdims=True))
    ).astype(jnp.bfloat16)
    router_grad = lax.dot_general(
        normed_ffn, logit_grad, contract_rows, preferred_element_type=jnp.float32
    )
    ffn_in_grad = lax.dot_general(
        logit_grad, router_w, contract_cols, preferred_element_type=jnp.float32
    )
    down_grad = jnp.einsum("ecf,ecd->efd", active, expert_grad, preferred_element_type=jnp.float32)
    active_grad = jnp.einsum(
        "ecd,efd->ecf", expert_grad, down_w, preferred_element_type=jnp.float32
    )
    gate_pre_grad, up_pre_grad = gelu_pull(active_grad)
    gate_pre_low = gate_pre_grad.astype(jnp.bfloat16)
    up_pre_low = up_pre_grad.astype(jnp.bfloat16)
    gate_grad = jnp.einsum(
        "ecd,ecf->edf", slot_rows, gate_pre_low, preferred_element_type=jnp.float32
    )
    up_grad = jnp.einsum("ecd,ecf->edf", slot_rows, up_pre_low, preferred_element_type=jnp.float32)
    slot_in_grad = jnp.einsum(
        "ecf,edf->ecd", gate_pre_low, gate_w, preferred_element_type=jnp.float32
    ) + jnp.einsum("ecf,edf->ecd", up_pre_low, up_w, preferred_element_type=jnp.float32)
    ffn_in_grad = ffn_in_grad.at[flat_token].add(
        (slot_in_grad * slot_valid[..., None]).reshape(E * MOST, MODEL_WIDTH)
    )
    middle_add, ffn_gain_grad = ffn_norm_pull(ffn_in_grad)
    middle_grad = grad_result + middle_add
    middle_low = middle_grad.astype(jnp.bfloat16)
    out_grad_w = lax.dot_general(
        mixed_heads, middle_low, contract_rows, preferred_element_type=jnp.float32
    )
    mixed_grad = lax.dot_general(
        middle_low, out_w, contract_cols, preferred_element_type=jnp.float32
    ).astype(jnp.bfloat16)
    head_grad = lax.all_to_all(mixed_grad, "seq", split_axis=1, concat_axis=0, tiled=True)
    head_grad_f = (
        head_grad.astype(jnp.float32)
        .reshape(head_rows, local_key_value, query_group, HEAD_SIZE)
        .transpose(1, 2, 0, 3)
    )
    total_shift = -jnp.sum(head_grad_f * attended_f, axis=-1) / row_total
    summed_grad = (head_grad_f / row_total[..., None]).astype(jnp.bfloat16)
    all_rows = shard_count * head_rows
    start_query = jnp.zeros((local_key_value, query_group, head_rows, HEAD_SIZE), jnp.float32)
    start_keys = jnp.zeros((all_rows, local_key_value * HEAD_SIZE), jnp.float32)
    start_values = jnp.zeros((all_rows, local_key_value * HEAD_SIZE), jnp.float32)
    fold_state = (start_query, start_keys, start_values)
    key_all = lax.all_gather(head_key, "shard", axis=0, tiled=True)
    value_all = lax.all_gather(head_value, "shard", axis=0, tiled=True)
    row_count = key_all.shape[0]
    backward_block_size = sub_rows(row_count)
    key_steps = key_all.reshape(
        row_count // backward_block_size, backward_block_size, local_key_value, HEAD_SIZE
    )
    value_steps = value_all.reshape(
        row_count // backward_block_size, backward_block_size, local_key_value, HEAD_SIZE
    )
    offsets = jnp.arange(row_count // backward_block_size, dtype=jnp.int32) * backward_block_size

    def backward_key_step(fold_carry, block_item):
        key_block, value_block, offset = block_item
        key_start = offset

        def backward_update(acc_state):
            query_acc, key_acc, value_acc = acc_state
            scores, allowed = block_scores(key_block, key_start)
            weights = jnp.where(
                allowed, jnp.exp(jnp.where(allowed, scores, -1e30) - row_top[..., None]), 0.0
            )
            value_part = jnp.einsum(
                "kgqt,kgqd->tkd",
                weights.astype(jnp.bfloat16),
                summed_grad,
                preferred_element_type=jnp.float32,
            )
            weight_shift = (
                jnp.einsum(
                    "kgqd,tkd->kgqt", summed_grad, value_block, preferred_element_type=jnp.float32
                )
                + total_shift[..., None]
            )
            score_grad = (weights * weight_shift).astype(jnp.bfloat16)
            query_acc = query_acc + score_scale * jnp.einsum(
                "kgqt,tkd->kgqd", score_grad, key_block, preferred_element_type=jnp.float32
            )
            key_part = score_scale * jnp.einsum(
                "kgqt,qkgd->tkd", score_grad, query_four, preferred_element_type=jnp.float32
            )
            key_acc = lax.dynamic_update_slice_in_dim(
                key_acc,
                key_part.reshape(backward_block_size, local_key_value * HEAD_SIZE),
                key_start,
                0,
            )
            value_acc = lax.dynamic_update_slice_in_dim(
                value_acc,
                value_part.reshape(backward_block_size, local_key_value * HEAD_SIZE),
                key_start,
                0,
            )
            return (query_acc, key_acc, value_acc)

        return (
            lax.cond(
                reachable(key_start, backward_block_size), backward_update, keep_state, fold_carry
            ),
            None,
        )

    fold_state, unused_out = lax.scan(
        backward_key_step, fold_state, (key_steps, value_steps, offsets)
    )
    query_acc, key_acc, value_acc = fold_state
    own_key_grad, own_value_grad = (
        lax.psum_scatter(key_acc, "shard", scatter_dimension=0, tiled=True),
        lax.psum_scatter(value_acc, "shard", scatter_dimension=0, tiled=True),
    )
    query_grad = (
        query_acc.transpose(2, 0, 1, 3)
        .reshape(head_rows, local_key_value * query_group * HEAD_SIZE)
        .astype(jnp.bfloat16)
    )
    tok_query_grad, token_key_gradient, tok_value_grad = (
        lax.all_to_all(query_grad, "seq", split_axis=0, concat_axis=1, tiled=True),
        lax.all_to_all(
            own_key_grad.astype(jnp.bfloat16), "seq", split_axis=0, concat_axis=1, tiled=True
        ),
        lax.all_to_all(
            own_value_grad.astype(jnp.bfloat16), "seq", split_axis=0, concat_axis=1, tiled=True
        ),
    )
    query_raw_grad = (
        invert_rotary(
            tok_query_grad.astype(jnp.float32).reshape(tokens_per_device, QUERY_HEADS, HEAD_SIZE),
            rotary_angle,
        )
        .reshape(tokens_per_device, QUERY_HEADS * HEAD_SIZE)
        .astype(jnp.bfloat16)
    )
    key_raw_grad = (
        invert_rotary(
            token_key_gradient.astype(jnp.float32).reshape(
                tokens_per_device, KEY_VALUE_HEADS, HEAD_SIZE
            ),
            rotary_angle,
        )
        .reshape(tokens_per_device, KEY_VALUE_HEADS * HEAD_SIZE)
        .astype(jnp.bfloat16)
    )
    query_grad_w = lax.dot_general(
        normalized_input, query_raw_grad, contract_rows, preferred_element_type=jnp.float32
    )
    key_grad_w = lax.dot_general(
        normalized_input, key_raw_grad, contract_rows, preferred_element_type=jnp.float32
    )
    value_grad_w = lax.dot_general(
        normalized_input, tok_value_grad, contract_rows, preferred_element_type=jnp.float32
    )
    normed_grad = lax.dot_general(
        query_raw_grad, query_w, contract_cols, preferred_element_type=jnp.float32
    )
    normed_grad = normed_grad + lax.dot_general(
        key_raw_grad, key_matrix, contract_cols, preferred_element_type=jnp.float32
    )
    normed_grad = normed_grad + lax.dot_general(
        tok_value_grad, value_w, contract_cols, preferred_element_type=jnp.float32
    )
    stream_add, attn_gain_grad = attn_norm_pull(normed_grad)
    stream_grad = (middle_grad + stream_add).astype(jnp.bfloat16)
    (
        gain_a_part,
        query_part,
        key_part_w,
        value_part_w,
        out_part,
        gain_f_part,
        router_part,
        gate_part,
        up_part,
        down_part,
    ) = (
        lax.psum_scatter(attn_gain_grad, "shard", scatter_dimension=0, tiled=True),
        lax.psum_scatter(query_grad_w, "shard", scatter_dimension=0, tiled=True),
        lax.psum_scatter(key_grad_w, "shard", scatter_dimension=0, tiled=True),
        lax.psum_scatter(value_grad_w, "shard", scatter_dimension=0, tiled=True),
        lax.psum_scatter(out_grad_w, "shard", scatter_dimension=0, tiled=True),
        lax.psum_scatter(ffn_gain_grad, "shard", scatter_dimension=0, tiled=True),
        lax.psum_scatter(router_grad, "shard", scatter_dimension=0, tiled=True),
        lax.psum_scatter(gate_grad, "shard", scatter_dimension=1, tiled=True),
        lax.psum_scatter(up_grad, "shard", scatter_dimension=1, tiled=True),
        lax.psum_scatter(down_grad, "shard", scatter_dimension=1, tiled=True),
    )
    (
        gain_a_own,
        query_own,
        key_own,
        value_own,
        out_own,
        gain_f_own,
        router_own,
        gate_own,
        up_own,
        down_own,
    ) = (
        lax.psum(gain_a_part.astype(jnp.bfloat16), "seq").astype(jnp.float32),
        lax.psum(query_part.astype(jnp.bfloat16), "seq").astype(jnp.float32),
        lax.psum(key_part_w.astype(jnp.bfloat16), "seq").astype(jnp.float32),
        lax.psum(value_part_w.astype(jnp.bfloat16), "seq").astype(jnp.float32),
        lax.psum(out_part.astype(jnp.bfloat16), "seq").astype(jnp.float32),
        lax.psum(gain_f_part.astype(jnp.bfloat16), "seq").astype(jnp.float32),
        lax.psum(router_part.astype(jnp.bfloat16), "seq").astype(jnp.float32),
        lax.psum(gate_part.astype(jnp.bfloat16), "seq").astype(jnp.float32),
        lax.psum(up_part.astype(jnp.bfloat16), "seq").astype(jnp.float32),
        lax.psum(down_part.astype(jnp.bfloat16), "seq").astype(jnp.float32),
    )
    return (
        result,
        stream_grad,
        gain_a_own,
        query_own,
        key_own,
        value_own,
        out_own,
        gain_f_own,
        router_own,
        gate_own,
        up_own,
        down_own,
    )


def solution(mesh):
    in_specs = (
        P(("shard", "seq"), None),
        P(),
        P(("shard", "seq"), None),
        P("shard"),
        P("shard", None),
        P("shard", None),
        P("shard", None),
        P("shard", None),
        P("shard"),
        P("shard", None),
        P(None, "shard", None),
        P(None, "shard", None),
        P(None, "shard", None),
        P(("shard", "seq"), None),
    )
    out_specs = (
        P(("shard", "seq"), None),
        P(("shard", "seq"), None),
        P("shard"),
        P("shard", None),
        P("shard", None),
        P("shard", None),
        P("shard", None),
        P("shard"),
        P("shard", None),
        P(None, "shard", None),
        P(None, "shard", None),
        P(None, "shard", None),
    )
    return jax.shard_map(local, mesh=mesh, in_specs=in_specs, out_specs=out_specs, check_vma=False)
```

profile of v0, /device:TPU:0, one launch (start us, length us, event | category | flops | bytes accessed | tf_op | source)
XLA Modules:
  0.0 2754.4 jit_solution(670745606099352188)
XLA Ops:
  11.8 35.9 %all-reduce.5 = (bf16[1536]{0:T(1024)(128)(2,1)S(1)}, bf16[1536]{0:T(1024)(128)(2,1)S(1)}) all-reduce(bf16[1536]{0:T(1024)(128)(2,1)S(1)} %dynamic-update-slice, bf16[1536]{0:T(1024)(128)(2,1)S(1)} %dynamic-update-slice.1), channel_id=1, replica_groups=mesh['shard'=16,'seq'=2] {'shard'}, use_global_device_ids=true, to_apply=%add | all-reduce | flops 3072 | bytes 12288
  49.1 22.8 all_gather.39
  75.7 7.6 all_to_all.119
  83.4 21.6 all_gather.42
  106.6 7.6 all_to_all.120
  129.1 17.9 all-gather
  147.2 6.7 gather_fusion.1
  156.9 8.9 all-gather.13.cloned.1.call-done
  167.0 59.2 %while.38 = (s32[]{:T(128)}, f32[1,6,512]{2,1,0:T(8,128)S(1)}, f32[1,6,512]{2,1,0:T(8,128)S(1)}, f32[1,6,512,128]{3,2,1,0:T(8,128)}, s32[8]{0:T(128)S(1)}, /*ind...) while((s32[]{:T(128)}, f32[1,6,512]{2,1,0:T(8,128)S(1)}, ...), condition=%wide.region_10.11_spmd, body=%wide.region_3.10_spmd.sunk | while | flops 1653907456 | bytes 57116160 | solution.py:197
  172.6 14.3 conditional.4
  180.6 5.1 bitcast_add_fusion
  236.4 11.2 all-to-all-done.3
  253.2 6.3 gather_fusion
  259.9 9.9 gather_fusion.2
  269.9 48.9 %all-gather.17.cloned.1.call-done = bf16[8,1536,768]{2,1,0:T(8,128)(2,1)} async-done(((bf16[8,96,768]{2,1,0:T(8,128)(2,1)}), bf16[8,1536,768]{2,1,0:T(8,128)(2,1)}) %all-gather.17.cloned.1.call-update) | async-done | bytes 18874384 | tf_op jit(solution)/shard_map/all_gather | solution.py:104
  318.9 14.5 fusion.78
  333.4 85.9 %all-gather.21.cloned.1.call-done = bf16[8,768,1536]{2,1,0:T(8,128)(2,1)} async-done(((bf16[8,48,1536]{2,1,0:T(8,128)(2,1)}), bf16[8,768,1536]{2,1,0:T(8,128)(2,1)}) %all-gather.21.cloned.1.call-update) | async-done | bytes 18874384 | tf_op jit(solution)/shard_map/all_gather | solution.py:106
  419.3 23.0 multiply_convert_fusion.1
  442.2 77.5 %all-gather.19.cloned.1.call-done = bf16[8,1536,768]{2,1,0:T(8,128)(2,1)} async-done(((bf16[8,96,768]{2,1,0:T(8,128)(2,1)}), bf16[8,1536,768]{2,1,0:T(8,128)(2,1)}) %all-gather.19.cloned.1.call-update) | async-done | bytes 18874384 | tf_op jit(solution)/shard_map/all_gather | solution.py:105
  519.8 18.4 add_convert_fusion
  538.2 15.8 multiply_reduce_fusion
  554.0 11.1 scatter_custom_fusion.2
  565.7 13.1 fusion.115
  578.7 15.2 add_multiply_fusion
  594.0 17.6 scatter_fusion.1
  619.4 14.1 all_to_all.121
  645.0 74.4 %while.39 = (s32[]{:T(128)}, f32[1,6,512,128]{3,2,1,0:T(8,128)S(1)}, f32[8192,128]{1,0:T(8,128)}, f32[8192,128]{1,0:T(8,128)}, s32[8]{0:T(128)S(1)}, /*index=5*/...) while((s32[]{:T(128)}, ...), condition=%wide.region_31.32_spmd, body=%wide.region_26.31_spmd.sunk | while | flops 4066802688 | bytes 121968728 | solution.py:364
  650.8 29.4 %conditional.5 = ((f32[1,6,512,128]{3,2,1,0:T(8,128)S(1)}, f32[8192,128]{1,0:T(8,128)}, f32[8192,128]{1,0:T(8,128)})) conditional(s32[]{:T(128)} %convert_element_type.464, (f32[1,6,512,128]{3,2,1,0:T(8,128)S(1)}, f32[8192,128]{1,0:T(8,128)}, f32[8192,128]{1,0:T(8,128)}) %tuple.147, (s32[]{:T(128)}, s32[512]{0:T(512)S(1)}, s32[10]{0:T(128)S(1)}, ...), branch_computations={%region_28.28_spmd, %region_29.30_spmd} | conditional | flops 4066802688 | bytes 121968304 | solution.py:358
  655.3 5.8 fusion.28
  670.9 6.4 fusion.32
  720.3 274.4 %reduce-scatter.13.cloned.1.call-done = f32[512,128]{1,0:T(8,128)} async-done(((f32[8192,128]{1,0:T(8,128)}), f32[512,128]{1,0:T(8,128)}) %reduce-scatter.13.cloned.1.call-update) | async-done | bytes 262160 | tf_op jit(solution)/shard_map/reduce_scatter | solution.py:369
  1006.4 64.2 %reduce-scatter.15.cloned.1.call-done = f32[512,128]{1,0:T(8,128)} async-done(((f32[8192,128]{1,0:T(8,128)}), f32[512,128]{1,0:T(8,128)}) %reduce-scatter.15.cloned.1.call-update) | async-done | bytes 262160 | tf_op jit(solution)/shard_map/reduce_scatter | solution.py:370
  1071.6 7.0 all_to_all.122
  1080.8 6.4 fusion.79
  1088.0 10.5 all_to_all.123
  1099.8 5.1 fusion.101
  1106.6 18.5 fusion.73
  1126.7 18.7 fusion.72
  1147.1 18.9 fusion.76
  1174.5 58.0 %all-reduce.4 = (bf16[1536]{0:T(1024)(128)(2,1)S(1)}, bf16[1536]{0:T(1024)(128)(2,1)S(1)}) all-reduce(f32[1536]{0:T(1024)S(1)} %get-tuple-element.953, f32[1536]{0:T(1024)S(1)} %copy-done.66), channel_id=4, replica_groups=mesh['shard'=16,'seq'=2] {'shard'}, use_global_device_ids=true, to_apply=%region_36.37.clone | all-reduce | flops 3072 | bytes 18432
  1235.2 19.7 reduce-scatter.21.cloned.1.call-done
  1256.4 113.5 %reduce-scatter.23.cloned.1.call-done = f32[96,1536]{1,0:T(8,128)} async-done(((f32[1536,1536]{1,0:T(8,128)}), f32[96,1536]{1,0:T(8,128)}) %reduce-scatter.23.cloned.1.call-update) | async-done | bytes 589840 | tf_op jit(solution)/shard_map/reduce_scatter | solution.py:440
  1371.8 113.3 %reduce-scatter.17.cloned.1.call-done = f32[96,1536]{1,0:T(8,128)} async-done(((f32[1536,1536]{1,0:T(8,128)}), f32[96,1536]{1,0:T(8,128)}) %reduce-scatter.17.cloned.1.call-update) | async-done | bytes 589840 | tf_op jit(solution)/shard_map/reduce_scatter | solution.py:437
  1486.9 370.5 %reduce-scatter.25.cloned.1.call-done = f32[8,96,768]{2,1,0:T(8,128)} async-done(((f32[8,1536,768]{2,1,0:T(8,128)}), f32[8,96,768]{2,1,0:T(8,128)}) %reduce-scatter.25.cloned.1.call-update) | async-done | bytes 2359312 | tf_op jit(solution)/shard_map/reduce_scatter | solution.py:443
  1860.2 368.9 %reduce-scatter.27.cloned.1.call-done = f32[8,96,768]{2,1,0:T(8,128)} async-done(((f32[8,1536,768]{2,1,0:T(8,128)}), f32[8,96,768]{2,1,0:T(8,128)}) %reduce-scatter.27.cloned.1.call-update) | async-done | bytes 2359312 | tf_op jit(solution)/shard_map/reduce_scatter | solution.py:444
  2231.9 368.9 %reduce-scatter.29.cloned.1.call-done = f32[8,48,1536]{2,1,0:T(8,128)} async-done(((f32[8,768,1536]{2,1,0:T(8,128)}), f32[8,48,1536]{2,1,0:T(8,128)}) %reduce-scatter.29.cloned.1.call-update) | async-done | bytes 2359312 | tf_op jit(solution)/shard_map/reduce_scatter | solution.py:445
  2603.7 17.2 scatter_fusion
  2631.7 105.9 %all-reduce.13.cloned.1.call-done = (bf16[96,1536]{1,0:T(8,128)(2,1)}, bf16[96,1536]{1,0:T(8,128)(2,1)}, bf16[8,96,768]{2,1,0:T(8,128)(2,1)}, bf16[8,96,768]{2,1,0:T(8,128)(2,1)}, bf16[8,48,1536]{2,1,0:T(8,128)(2,1)}) async-done(((bf16[96,1536]{1,0:T(8,128)(2,1)}, bf16[96,1536]{1,0:T(8,128)(2,1)}, bf16[8,96,768]{2,1,0:T(8,128)(2,1)}, bf16[8,96,768]{2,1,0:T(8,128)(2,1)}, bf16[8,48,1536]{2,1,0:T(8,128)(2,1)}), ...) | async-done | bytes 4128784 | tf_op jit(solution)/shard_map/psum | solution.py:460
  (438 shorter events, 194.5 us)
Async XLA Ops:
  7.2 98.7 %copy-start.8 = (bf16[256,1536]{1,0:T(8,128)(2,1)S(1)}, bf16[256,1536]{1,0:T(8,128)(2,1)}, u32[]{:S(2)}) copy-start(bf16[256,1536]{1,0:T(8,128)(2,1)} %param.22) | copy-start | bytes 2359300
  7.2 67.6 %copy-start.59 = (s32[10]{0:T(128)S(1)}, s32[10]{0:T(128)}, u32[]{:S(2)}) copy-start(s32[10]{0:T(128)} %param.23) | copy-start | bytes 124
  7.2 76.2 %copy-start.63 = (bf16[96,256]{1,0:T(8,128)(2,1)S(1)}, bf16[96,256]{1,0:T(8,128)(2,1)}, u32[]{:S(2)}) copy-start(bf16[96,256]{1,0:T(8,128)(2,1)} %param.28) | copy-start | bytes 147460
  7.2 111.7 %all-gather.11.cloned.1.call-start = ((), (), s32[]{:S(2)}) async-start(), calls=%async_computation.19 | async-start | bytes 5013504 | tf_op jit(solution)/shard_map/all_gather | solution.py:98
  7.9 148.9 %all-gather.9.cloned.1.call-start = ((), (), s32[]{:S(2)}) async-start(), calls=%async_computation.18 | async-start | bytes 2228224 | tf_op jit(solution)/shard_map/all_gather | solution.py:164
  47.7 71.2 %copy-start.48 = (f32[1536]{0:T(1024)}, f32[1536]{0:T(1024)S(1)}, u32[]{:S(2)}) copy-start(f32[1536]{0:T(1024)S(1)} %convert_element_type.297) | copy-start | bytes 18436
  49.1 57.4 %copy-start.69 = (f32[256]{0:T(256)}, f32[256]{0:T(256)S(1)}, u32[]{:S(2)}) copy-start(f32[256]{0:T(256)S(1)} %fusion.67) | copy-start | bytes 3076
  49.1 69.8 %copy-start.61 = (f32[256]{0:T(256)}, f32[256]{0:T(256)S(1)}, u32[]{:S(2)}) copy-start(f32[256]{0:T(256)S(1)} %fusion.89) | copy-start | bytes 3076
  75.2 48.1 %copy-start.37 = (f32[256,64]{0,1:T(8,128)}, f32[256,64]{0,1:T(8,128)S(1)}, u32[]{:S(2)}) copy-start(f32[256,64]{0,1:T(8,128)S(1)} %get-tuple-element.1049) | copy-start | bytes 196612
  75.3 48.1 %copy-start.39 = (f32[256,64]{0,1:T(8,128)}, f32[256,64]{0,1:T(8,128)S(1)}, u32[]{:S(2)}) copy-start(f32[256,64]{0,1:T(8,128)S(1)} %get-tuple-element.1050) | copy-start | bytes 196612
  75.4 41.4 %copy-start.33 = (f32[256,64]{1,0:T(8,128)}, f32[256,64]{1,0:T(8,128)S(1)}, u32[]{:S(2)}) copy-start(f32[256,64]{1,0:T(8,128)S(1)} %copy.136) | copy-start | bytes 196612
  75.5 42.0 %copy-start.35 = (f32[256,64]{1,0:T(8,128)}, f32[256,64]{1,0:T(8,128)S(1)}, u32[]{:S(2)}) copy-start(f32[256,64]{1,0:T(8,128)S(1)} %copy.134) | copy-start | bytes 196612
  75.5 41.4 %copy-start.73 = (s32[256,4]{0,1:T(4,128)S(1)}, s32[256,4]{0,1:T(4,128)}, u32[]{:S(2)}) copy-start(s32[256,4]{0,1:T(4,128)} %param.24) | copy-start | bytes 12292
  75.5 43.2 %copy-start.76 = (s32[2]{0:T(128)S(1)}, s32[2]{0:T(128)}, u32[]{:S(2)}) copy-start(s32[2]{0:T(128)} %constant.312) | copy-start | bytes 28
  83.3 82.4 %all-gather.13.cloned.1.call-start = ((), (), s32[]{:S(2)}) async-start(), calls=%async_computation.20 | async-start | bytes 2228224 | tf_op jit(solution)/shard_map/all_gather | solution.py:165
  114.2 122.1 %all-gather.15.cloned.1.call-start = ((), (), s32[]{:S(2)}) async-start(), calls=%async_computation.21 | async-start | bytes 5013504 | tf_op jit(solution)/shard_map/all_gather | solution.py:101
  114.8 204.1 %all-gather.17.cloned.1.call-start = ((), (), s32[]{:S(2)}) async-start(), calls=%async_computation.22 | async-start | bytes 20054016 | tf_op jit(solution)/shard_map/all_gather | solution.py:104
  115.4 303.8 %all-gather.21.cloned.1.call-start = ((), (), s32[]{:S(2)}) async-start(), calls=%async_computation.24 | async-start | bytes 20054016 | tf_op jit(solution)/shard_map/all_gather | solution.py:106
  116.0 403.8 %all-gather.19.cloned.1.call-start = ((), (), s32[]{:S(2)}) async-start(), calls=%async_computation.23 | async-start | bytes 20054016 | tf_op jit(solution)/shard_map/all_gather | solution.py:105
  124.6 29.4 %all-to-all-start.1 = ((bf16[256,2,768]{0,2,1:T(8,128)(2,1)}), bf16[256,2,768]{0,2,1:T(8,128)(2,1)}, u32[]{:S(2)}, u32[]{:S(2)}) async-start(bf16[256,2,768]{0,2,1:T(8,128)(2,1)} %bitcast.43), calls=%async_computation.1 | async-start | bytes 1572864 | tf_op jit(solution)/shard_map/all_to_all | solution.py:136
  129.1 122.8 %copy-start.54 = (f32[1536]{0:T(1024)}, f32[1536]{0:T(1024)S(1)}, u32[]{:S(2)}) copy-start(f32[1536]{0:T(1024)S(1)} %convert_element_type.306) | copy-start | bytes 18436
  232.5 15.0 all-to-all-start.3
  236.1 758.6 %reduce-scatter.13.cloned.1.call-start = ((), (), s32[]{:S(2)}) async-start(), calls=%async_computation.25 | async-start | bytes 4456448 | tf_op jit(solution)/shard_map/reduce_scatter | solution.py:369
  236.3 283.4 %copy-start.46 = (bf16[8,192]{1,0:T(8,128)(2,1)}, bf16[8,192]{1,0:T(8,128)(2,1)S(1)}, u32[]{:S(2)}) copy-start(bf16[8,192]{1,0:T(8,128)(2,1)S(1)} %get-tuple-element.1048) | copy-start | bytes 9220
  269.9 268.2 %copy-start.42 = (f32[8,192]{1,0:T(8,128)}, f32[8,192]{1,0:T(8,128)S(1)}, u32[]{:S(2)}) copy-start(f32[8,192]{1,0:T(8,128)S(1)} %get-tuple-element.1025) | copy-start | bytes 18436
  269.9 268.2 %copy-start.44 = (pred[8,192]{1,0:T(8,128)(4,1)}, pred[8,192]{1,0:T(8,128)(4,1)S(1)}, u32[]{:S(2)}) copy-start(pred[8,192]{1,0:T(8,128)(4,1)S(1)} %get-tuple-element.1026) | copy-start | bytes 4612
  719.5 280.3 %copy-start.4 = (bf16[256,1536]{1,0:T(8,128)(2,1)S(1)}, bf16[256,1536]{1,0:T(8,128)(2,1)}, u32[]{:S(2)}) copy-start(bf16[256,1536]{1,0:T(8,128)(2,1)} %copy-done.3) | copy-start | bytes 2359300
  719.5 280.3 %copy-start.65 = (bf16[256,8]{0,1:T(8,128)(2,1)S(1)}, bf16[256,8]{0,1:T(8,128)(2,1)}, u32[]{:S(2)}) copy-start(bf16[256,8]{0,1:T(8,128)(2,1)} %copy-done.64) | copy-start | bytes 12292
  719.5 284.7 %copy-start.34 = (f32[256,64]{1,0:T(8,128)S(1)}, f32[256,64]{1,0:T(8,128)}, u32[]{:S(2)}) copy-start(f32[256,64]{1,0:T(8,128)} %copy-done.33) | copy-start | bytes 196612
  719.5 284.7 %copy-start.36 = (f32[256,64]{1,0:T(8,128)S(1)}, f32[256,64]{1,0:T(8,128)}, u32[]{:S(2)}) copy-start(f32[256,64]{1,0:T(8,128)} %copy-done.35) | copy-start | bytes 196612
  719.6 285.1 %copy-start.9 = (bf16[256,1536]{1,0:T(8,128)(2,1)S(1)}, bf16[256,1536]{1,0:T(8,128)(2,1)}, u32[]{:S(2)}) copy-start(bf16[256,1536]{1,0:T(8,128)(2,1)} %param.22) | copy-start | bytes 2359300
  719.6 285.1 %copy-start.49 = (f32[1536]{0:T(1024)S(1)}, f32[1536]{0:T(1024)}, u32[]{:S(2)}) copy-start(f32[1536]{0:T(1024)} %copy-done.48) | copy-start | bytes 18436
  719.6 285.1 %copy-start.62 = (f32[256]{0:T(256)S(1)}, f32[256]{0:T(256)}, u32[]{:S(2)}) copy-start(f32[256]{0:T(256)} %copy-done.61) | copy-start | bytes 3076
  719.6 351.0 %reduce-scatter.15.cloned.1.call-start = ((), (), s32[]{:S(2)}) async-start(), calls=%async_computation.26 | async-start | bytes 4456448 | tf_op jit(solution)/shard_map/reduce_scatter | solution.py:370
  996.4 7.8 all-to-all-start.6
  999.7 167.1 %reduce-scatter.31.cloned.1.call-start = ((), (), s32[]{:S(2)}) async-start(), calls=%async_computation.34 | async-start | bytes 835584
  1001.1 232.5 %reduce-scatter.19.cloned.1.call-start = ((), (), s32[]{:S(2)}) async-start(), calls=%async_computation.28 | async-start | bytes 1671168 | tf_op jit(solution)/shard_map/reduce_scatter | solution.py:438
  1004.5 76.3 %copy-start.17 = (bf16[2,256,768]{1,2,0:T(8,128)(2,1)S(1)}, bf16[2,256,768]{1,2,0:T(8,128)(2,1)}, u32[]{:S(2)}) copy-start(bf16[2,256,768]{1,2,0:T(8,128)(2,1)} %copy-done.16) | copy-start | bytes 2359300
  1006.4 248.5 %reduce-scatter.21.cloned.1.call-start = ((), (), s32[]{:S(2)}) async-start(), calls=%async_computation.29 | async-start | bytes 1671168 | tf_op jit(solution)/shard_map/reduce_scatter | solution.py:439
  1080.4 289.6 %reduce-scatter.23.cloned.1.call-start = ((), (), s32[]{:S(2)}) async-start(), calls=%async_computation.30 | async-start | bytes 10027008 | tf_op jit(solution)/shard_map/reduce_scatter | solution.py:440
  1087.3 397.8 %reduce-scatter.17.cloned.1.call-start = ((), (), s32[]{:S(2)}) async-start(), calls=%async_computation.27 | async-start | bytes 10027008 | tf_op jit(solution)/shard_map/reduce_scatter | solution.py:437
  1104.9 752.4 %reduce-scatter.25.cloned.1.call-start = ((), (), s32[]{:S(2)}) async-start(), calls=%async_computation.31 | async-start | bytes 40108032 | tf_op jit(solution)/shard_map/reduce_scatter | solution.py:443
  1125.1 1104.0 %reduce-scatter.27.cloned.1.call-start = ((), (), s32[]{:S(2)}) async-start(), calls=%async_computation.32 | async-start | bytes 40108032 | tf_op jit(solution)/shard_map/reduce_scatter | solution.py:444
  1145.4 1455.3 %reduce-scatter.29.cloned.1.call-start = ((), (), s32[]{:S(2)}) async-start(), calls=%async_computation.33 | async-start | bytes 40108032 | tf_op jit(solution)/shard_map/reduce_scatter | solution.py:445
  1166.1 1459.2 %all-reduce.11.cloned.1.call-start = ((), (), s32[]{:S(2)}) async-start(), calls=%async_computation.35 | async-start | bytes 202752 | tf_op jit(solution)/shard_map/psum | solution.py:459
  1256.4 1481.2 %all-reduce.13.cloned.1.call-start = ((), (), s32[]{:S(2)}) async-start(), calls=%async_computation.36 | async-start | bytes 8257536 | tf_op jit(solution)/shard_map/psum | solution.py:460
  2231.9 371.8 %copy-start.2 = (f32[256,1536]{1,0:T(8,128)S(1)}, f32[256,1536]{1,0:T(8,128)}, u32[]{:S(2)}) copy-start(f32[256,1536]{1,0:T(8,128)} %copy-done) | copy-start | bytes 4718596
  2231.9 371.8 %copy-start.58 = (s32[1536]{0:T(1024)S(1)}, s32[1536]{0:T(1024)}, u32[]{:S(2)}) copy-start(s32[1536]{0:T(1024)} %copy-done.56) | copy-start | bytes 18436
  (53 other events, 354.4 us)
Sparse Core Ops, SparseCore 0:
  10.3 61.5 all-gather.10
  83.5 39.9 all-gather.8
  125.7 40.0 all-gather.12
  167.9 52.0 all-gather.14
  221.4 97.4 all-gather.16
  320.3 98.9 all-gather.20
  420.8 98.9 all-gather.18
  719.6 275.0 reduce-scatter.12
  999.1 71.4 reduce-scatter.14
  1074.6 55.5 reduce-scatter.30
  1134.3 58.5 reduce-scatter.18
  1196.3 58.4 reduce-scatter.20
  1259.5 110.4 reduce-scatter.22
  1373.9 111.1 reduce-scatter.16
  1489.7 367.5 reduce-scatter.24
  1862.0 366.9 reduce-scatter.26
  2233.7 366.9 reduce-scatter.28
  2604.5 20.7 all-reduce.10
  2629.5 108.0 all-reduce.12
where the time goes:
time: 2760 us; the launch traced here: 2750 us
  waiting for transfers between devices  2040 us (74%)
  matrix products  222 us (8%)
  blocking collectives  203 us (7%)
  other arithmetic  113 us (4%)
  local copies, waits for them, and re-layouts  93.1 us (3%)
  loops' own time  55 us (2%)
    reduce_scatter x1, waiting for transfers between devices, local(): lax.psum_scatter(gate_grad, 'shard', scatter_dimension=1, tiled=True)  370 us
    reduce_scatter x1, waiting for transfers between devices, local(): lax.psum_scatter(up_grad, 'shard', scatter_dimension=1, tiled=True)  369 us
    reduce_scatter x1, waiting for transfers between devices, local(): lax.psum_scatter(down_grad, 'shard', scatter_dimension=1, tiled=True)  369 us
    reduce_scatter x1, waiting for transfers between devices, local(): lax.psum_scatter(key_acc, 'shard', scatter_dimension=0, tiled=True)  274 us
    reduce_scatter x1, waiting for transfers between devices, local(): lax.psum_scatter(out_grad_w, 'shard', scatter_dimension=0, tiled=True)  114 us
    reduce_scatter x1, waiting for transfers between devices, local(): lax.psum_scatter(query_grad_w, 'shard', scatter_dimension=0, tiled=True)  113 us
    psum x1, waiting for transfers between devices, local(): lax.psum(query_part.astype(jnp.bfloat16), 'seq').astype(jnp.float32)  106 us
    unnamed x2, blocking collectives  93.9 us
  transfers between devices with their start and end apart: 22, of which 16 were waited for; matrix products, arithmetic and copies ran while one was open for 9% of the time, Pallas kernels for 0%

commit v1 on v0

v1 whole, which is shorter than its diff:
```python
import jax
import jax.numpy as jnp
from jax import lax
from jax.experimental import pallas as pl
from jax.experimental.pallas import tpu as pltpu
from jax.sharding import Mesh, PartitionSpec as P

WIDTH = 1536
HEADS = 12
KV_HEADS = 2
HEAD = 128
FF = 768
E = 8
MOST = 192
SEQ = KV_HEADS
GROUP = HEADS // KV_HEADS
INNER = E // SEQ
QCOLS = GROUP * HEAD
QKV = QCOLS + 2 * HEAD
EXTRA = 128
PACK = QKV + EXTRA + WIDTH
EPS = 1e-06
ROPE_BASE = 10000.0
SCALE = HEAD**-0.5
LOG2E = 1.4426950408889634
LN2 = 0.6931471805599453
NEG = -1e30
AXES = ("outer", "inner", "seq")
MESH = pl.DeviceIdType.MESH
NN = (((1,), (0,)), ((), ()))
NT = (((1,), (1,)), ((), ()))
TN = (((0,), (0,)), ((), ()))
BF = jnp.bfloat16
F32 = jnp.float32


def dot(a, b, dims=NN):
    return lax.dot_general(a, b, dims, preferred_element_type=F32)


class Net:
    def __init__(self, depth):
        self.depth = depth
        self.z = lax.axis_index("outer")
        self.i = lax.axis_index("inner")
        self.y = lax.axis_index("seq")
        self.core = lax.rem(self.i, 2)
        self.x = lax.div(self.i, 2)
        self.xp = self.dev(i=lax.rem(self.i + 2, INNER))
        self.cp = self.dev(i=self.i + 1 - 2 * self.core)
        self.yp = self.dev(y=1 - self.y)

    def dev(self, z=None, i=None, y=None):
        return {
            "outer": self.z if z is None else z,
            "inner": self.i if i is None else i,
            "seq": self.y if y is None else y,
        }

    def zoff(self, dz):
        return lax.rem(self.z + dz, self.depth)

    def zpeers(self):
        return [self.dev(z=self.zoff(dz)) for dz in range(1, self.depth)]

    def plane(self):
        out = []
        for di in range(INNER):
            for dy in range(SEQ):
                if di or dy:
                    out.append(
                        self.dev(i=lax.rem(self.i + di, INNER), y=lax.rem(self.y + dy, SEQ))
                    )
        return out


def greet(devices):
    barrier = pltpu.get_barrier_semaphore()
    for device in devices:
        pl.semaphore_signal(barrier, inc=1, device_id=device, device_id_type=MESH)
    pl.semaphore_wait(barrier, len(devices))


def remote(src, dst, ssem, rsem, device):
    return pltpu.make_async_remote_copy(
        src_ref=src, dst_ref=dst, send_sem=ssem, recv_sem=rsem, device_id=device, device_id_type=MESH
    )


class Sends:
    def __init__(self):
        self.items = []

    def start(self, src, dst, ssem, rsem, device):
        copy = remote(src, dst, ssem, rsem, device)
        copy.start()
        self.items.append(copy)

    def finish(self):
        for copy in self.items:
            copy.wait_send()


def arrived(dst, ssem, rsem, device):
    remote(dst, dst, ssem, rsem, device).wait_recv()


def dma_sems(*counts):
    return [pltpu.SemaphoreType.DMA((n,)) for n in counts]


class ShardGather:
    def __init__(self, net, sends, src, out, sems):
        self.net, self.sends, self.src, self.out = net, sends, src, out
        self.sz, self.rz, self.sx, self.rx, self.sc, self.rc = sems

    @staticmethod
    def sems(depth):
        return dma_sems(*([max(depth - 1, 1)] * 2 + [depth] * 2 + [2 * depth] * 2))

    def slot(self, dz, i):
        return self.out.at[lax.rem(self.net.z - dz + self.net.depth, self.net.depth) * INNER + i]

    def begin(self):
        net, me = self.net, self.slot(0, self.net.i)
        for n, device in enumerate(net.zpeers()):
            self.sends.start(self.src, me, self.sz.at[n], self.rz.at[n], device)
        self.sends.start(self.src, me, self.sx.at[0], self.rx.at[0], net.xp)
        self.sends.start(self.src, me, self.sc.at[0], self.rc.at[0], net.cp)

    def end(self):
        net, depth = self.net, self.net.depth
        xi = lax.rem(net.i + 2, INNER)
        for dz in range(1, depth):
            block = self.slot(dz, net.i)
            arrived(block, self.sz.at[dz - 1], self.rz.at[dz - 1], net.zpeers()[dz - 1])
            self.sends.start(block, block, self.sx.at[dz], self.rx.at[dz], net.xp)
            self.sends.start(block, block, self.sc.at[dz], self.rc.at[dz], net.cp)
        for dz in range(depth):
            block = self.slot(dz, xi)
            arrived(block, self.sx.at[dz], self.rx.at[dz], net.xp)
            self.sends.start(
                block, block, self.sc.at[depth + dz], self.rc.at[depth + dz], net.cp
            )
        ci = net.i + 1 - 2 * net.core
        for dz in range(depth):
            arrived(self.slot(dz, ci), self.sc.at[dz], self.rc.at[dz], net.cp)
        for dz in range(depth):
            arrived(
                self.slot(dz, lax.rem(ci + 2, INNER)),
                self.sc.at[depth + dz],
                self.rc.at[depth + dz],
                net.cp,
            )


def hbm():
    return pl.BlockSpec(memory_space=pltpu.HBM)


def vmem():
    return pl.BlockSpec(memory_space=pltpu.VMEM)


def smem():
    return pl.BlockSpec(memory_space=pltpu.SMEM)


def comm_params(cid, limit=56 << 20):
    return pltpu.CompilerParams(
        collective_id=cid, has_side_effects=True, vmem_limit_bytes=limit
    )


def opening(pack, moe, stream, chosen, depth):
    rows = pack.shape[0]

    def kernel(pack_ref, moe_ref, st_ref, ch_ref, pack_out, moe_out, st_out, ch_out, *sems):
        net = Net(depth)
        sends = Sends()
        gather = ShardGather(net, sends, pack_ref, pack_out, sems[:6])
        sm, rm, sy, ry, sp, rp, own = sems[6:]
        locals_ = [
            pltpu.make_async_copy(pack_ref, gather.slot(0, net.i), own.at[0]),
            pltpu.make_async_copy(moe_ref.at[net.i * SEQ + net.y], moe_out.at[net.i], own.at[1]),
            pltpu.make_async_copy(st_ref, st_out.at[net.y], own.at[2]),
            pltpu.make_async_copy(ch_ref, ch_out.at[net.i * SEQ + net.y], own.at[3]),
        ]
        greet(net.zpeers() + net.plane())
        gather.begin()
        sends.start(st_ref, st_out.at[net.y], sy.at[0], ry.at[0], net.yp)
        for n, device in enumerate(net.plane()):
            sends.start(ch_ref, ch_out.at[net.i * SEQ + net.y], sp.at[n], rp.at[n], device)
        for di in range(1, INNER):
            other = lax.rem(net.i + di, INNER)
            sends.start(
                moe_ref.at[other * SEQ + net.y],
                moe_out.at[net.i],
                sm.at[di - 1],
                rm.at[di - 1],
                net.dev(i=other),
            )
        for copy in locals_:
            copy.start()
        gather.end()
        arrived(st_out.at[1 - net.y], sy.at[0], ry.at[0], net.yp)
        n = 0
        for di in range(INNER):
            for dy in range(SEQ):
                if di or dy:
                    frm = lax.rem(net.i - di + INNER, INNER) * SEQ + lax.rem(net.y + dy, SEQ)
                    arrived(ch_out.at[frm], sp.at[n], rp.at[n], net.yp)
                    n += 1
        for di in range(1, INNER):
            frm = lax.rem(net.i - di + INNER, INNER)
            arrived(moe_out.at[frm], sm.at[di - 1], rm.at[di - 1], net.yp)
        sends.finish()
        for copy in locals_:
            copy.wait()

    return pl.pallas_call(
        kernel,
        out_shape=(
            jax.ShapeDtypeStruct((depth * INNER,) + pack.shape, BF),
            jax.ShapeDtypeStruct((INNER,) + moe.shape[1:], BF),
            jax.ShapeDtypeStruct((SEQ,) + stream.shape, BF),
            jax.ShapeDtypeStruct((E,) + chosen.shape, F32),
        ),
        in_specs=[hbm()] * 4,
        out_specs=(hbm(),) * 4,
        scratch_shapes=ShardGather.sems(depth) + dma_sems(3, 3, 1, 1, E - 1, E - 1, 4),
        compiler_params=comm_params(1),
        name="opening",
    )(pack, moe, stream, chosen)


def gather_keys(kv, depth):
    def kernel(src, out, *sems):
        net = Net(depth)
        sends = Sends()
        gather = ShardGather(net, sends, src, out, sems[:6])
        own = pltpu.make_async_copy(src, gather.slot(0, net.i), sems[6].at[0])
        greet(net.zpeers() + [net.xp, net.cp])
        gather.begin()
        own.start()
        gather.end()
        sends.finish()
        own.wait()

    return pl.pallas_call(
        kernel,
        out_shape=jax.ShapeDtypeStruct((depth * INNER,) + kv.shape, BF),
        in_specs=[hbm()],
        out_specs=hbm(),
        scratch_shapes=ShardGather.sems(depth) + dma_sems(1),
        compiler_params=comm_params(2),
        name="gather_keys",
    )(kv)


def gather_plane(rows, depth, cid):
    half = rows.shape[0] // 2

    def kernel(src, out, sx, rx, sy, ry, sc, rc, own):
        net = Net(depth)
        sends = Sends()

        def place(i, y):
            return i * SEQ + y

        xi = lax.rem(net.i + 2, INNER)
        me, xb = place(net.i, net.y), place(xi, net.y)
        yb, db = place(net.i, 1 - net.y), place(xi, 1 - net.y)
        lo, hi = pl.ds(0, half), pl.ds(half, half)
        mine = pltpu.make_async_copy(src, out.at[me], own.at[0])
        greet([net.xp, net.yp, net.cp])
        sends.start(src, out.at[me], sx.at[0], rx.at[0], net.xp)
        sends.start(src, out.at[me], sy.at[0], ry.at[0], net.yp)
        sends.start(src, out.at[me], sc.at[0], rc.at[0], net.cp)
        mine.start()
        arrived(out.at[yb], sy.at[0], ry.at[0], net.yp)
        sends.start(out.at[yb, lo], out.at[yb, lo], sx.at[1], rx.at[1], net.xp)
        sends.start(out.at[yb], out.at[yb], sc.at[1], rc.at[1], net.cp)
        arrived(out.at[xb], sx.at[0], rx.at[0], net.xp)
        sends.start(out.at[xb, hi], out.at[xb, hi], sy.at[1], ry.at[1], net.yp)
        sends.start(out.at[xb], out.at[xb], sc.at[2], rc.at[2], net.cp)
        arrived(out.at[db, lo], sx.at[1], rx.at[1], net.xp)
        sends.start(out.at[db, lo], out.at[db, lo], sc.at[3], rc.at[3], net.cp)
        arrived(out.at[db, hi], sy.at[1], ry.at[1], net.yp)
        sends.start(out.at[db, hi], out.at[db, hi], sc.at[4], rc.at[4], net.cp)
        ci = net.i + 1 - 2 * net.core
        cx = lax.rem(ci + 2, INNER)
        arrived(out.at[place(ci, net.y)], sc.at[0], rc.at[0], net.cp)
        arrived(out.at[place(ci, 1 - net.y)], sc.at[1], rc.at[1], net.cp)
        arrived(out.at[place(cx, net.y)], sc.at[2], rc.at[2], net.cp)
        arrived(out.at[place(cx, 1 - net.y), lo], sc.at[3], rc.at[3], net.cp)
        arrived(out.at[place(cx, 1 - net.y), hi], sc.at[4], rc.at[4], net.cp)
        sends.finish()
        mine.wait()

    return pl.pallas_call(
        kernel,
        out_shape=jax.ShapeDtypeStruct((E,) + rows.shape, BF),
        in_specs=[hbm()],
        out_specs=hbm(),
        scratch_shapes=dma_sems(2, 2, 2, 2, 5, 5, 1),
        compiler_params=comm_params(cid),
        name="gather_plane",
    )(rows)


def add_into(dst, sources, rows, chunk):
    def body(n, carry):
        at = pl.ds(pl.multiple_of(n * chunk, chunk), chunk)
        total = sources[0][at, :].astype(F32)
        for source in sources[1:]:
            total = total + source[at, :].astype(F32)
        dst[at, :] = total.astype(dst.dtype)
        return carry

    lax.fori_loop(0, rows // chunk, body, 0)


def chunk_of(rows):
    for size in (32, 16, 8):
        if rows % size == 0:
            return size
    return rows


def scatter_plane(part, depth):
    rows, cols = part.shape[1:]
    half = rows // 2

    def kernel(part_ref, out, bc, mid, bx, by, second, b2, ssem, rsem):
        net = Net(depth)
        sends = Sends()

        def place(fx, fy, core):
            x = 1 - net.x if fx else net.x
            y = 1 - net.y if fy else net.y
            return (x * 2 + core) * SEQ + y

        greet([net.xp, net.yp, net.cp])
        order = ((1, 1), (1, 0), (0, 1), (0, 0))
        for n, (fx, fy) in enumerate(order):
            sends.start(
                part_ref.at[place(fx, fy, 1 - net.core)], bc.at[n], ssem.at[n], rsem.at[n], net.cp
            )
        ch = chunk_of(half)
        lo, hi = pl.ds(0, half), pl.ds(half, half)
        for n, (fx, fy) in enumerate(order):
            arrived(bc.at[n], ssem.at[n], rsem.at[n], net.cp)
            add_into(mid.at[n], [part_ref.at[place(fx, fy, net.core)], bc.at[n]], rows, ch)
            if n == 0:
                sends.start(mid.at[0, lo], bx.at[0], ssem.at[4], rsem.at[4], net.xp)
                sends.start(mid.at[0, hi], by.at[0], ssem.at[5], rsem.at[5], net.yp)
            if n == 1:
                sends.start(mid.at[1, lo], bx.at[1], ssem.at[6], rsem.at[6], net.xp)
            if n == 2:
                sends.start(mid.at[2, hi], by.at[1], ssem.at[7], rsem.at[7], net.yp)
        arrived(bx.at[0], ssem.at[4], rsem.at[4], net.xp)
        add_into(second.at[0], [mid.at[2, lo], bx.at[0]], half, ch)
        sends.start(second.at[0], b2.at[0], ssem.at[8], rsem.at[8], net.yp)
        arrived(by.at[0], ssem.at[5], rsem.at[5], net.yp)
        add_into(second.at[1], [mid.at[1, hi], by.at[0]], half, ch)
        sends.start(second.at[1], b2.at[1], ssem.at[9], rsem.at[9], net.xp)
        arrived(bx.at[1], ssem.at[6], rsem.at[6], net.xp)
        arrived(by.at[1], ssem.at[7], rsem.at[7], net.yp)
        arrived(b2.at[0], ssem.at[8], rsem.at[8], net.yp)
        add_into(out.at[lo], [mid.at[3, lo], bx.at[1], b2.at[0]], half, ch)
        arrived(b2.at[1], ssem.at[9], rsem.at[9], net.xp)
        add_into(out.at[hi], [mid.at[3, hi], by.at[1], b2.at[1]], half, ch)
        sends.finish()

    return pl.pallas_call(
        kernel,
        out_shape=jax.ShapeDtypeStruct((rows, cols), F32),
        in_specs=[vmem()],
        out_specs=vmem(),
        scratch_shapes=[pltpu.VMEM((4, rows, cols), BF)] * 2
        + [pltpu.VMEM((2, half, cols), BF)] * 4
        + dma_sems(10, 10),
        compiler_params=comm_params(4),
        name="scatter_plane",
    )(part)


class ShardScatter:
    @staticmethod
    def scratch(depth, rows, cols):
        far = max(depth - 1, 1)
        shapes = [(2 * depth, rows, cols)] + [(depth, rows, cols)] * 2 + [(far, rows, cols)] * 2
        return [pltpu.VMEM(s, BF) for s in shapes] + dma_sems(
            2 * depth, 2 * depth, depth, depth, far, far
        )

    def __init__(self, net, sends, part, scratch):
        self.net, self.sends, self.part = net, sends, part
        self.bc, self.sx, self.bx, self.sz, self.bz = scratch[:5]
        self.ssc, self.rsc, self.ssx, self.rsx, self.ssz, self.rsz = scratch[5:]
        depth = net.depth
        self.order = sorted(range(1, depth), key=lambda d: -min(d, depth - d)) + [0]
        self.rows = part.shape[1]
        self.chunk = chunk_of(self.rows)

    def block(self, dz, fx, core):
        x = 1 - self.net.x if fx else self.net.x
        return self.part.at[self.net.zoff(dz) * INNER + x * 2 + core]

    def begin(self):
        net = self.net
        for dz in self.order:
            for fx in (1, 0):
                n = dz * 2 + fx
                self.sends.start(
                    self.block(dz, fx, 1 - net.core),
                    self.bc.at[n],
                    self.ssc.at[n],
                    self.rsc.at[n],
                    net.cp,
                )

    def end(self, out):
        net, sends = self.net, self.sends
        for dz in self.order:
            n = dz * 2 + 1
            arrived(self.bc.at[n], self.ssc.at[n], self.rsc.at[n], net.cp)
            add_into(
                self.sx.at[dz], [self.block(dz, 1, net.core), self.bc.at[n]], self.rows, self.chunk
            )
            sends.start(self.sx.at[dz], self.bx.at[dz], self.ssx.at[dz], self.rsx.at[dz], net.xp)
        for dz in self.order:
            n = dz * 2
            arrived(self.bc.at[n], self.ssc.at[n], self.rsc.at[n], net.cp)
            arrived(self.bx.at[dz], self.ssx.at[dz], self.rsx.at[dz], net.xp)
            terms = [self.block(dz, 0, net.core), self.bc.at[n], self.bx.at[dz]]
            if dz:
                add_into(self.sz.at[dz - 1], terms, self.rows, self.chunk)
                sends.start(
                    self.sz.at[dz - 1],
                    self.bz.at[dz - 1],
                    self.ssz.at[dz - 1],
                    self.rsz.at[dz - 1],
                    net.dev(z=net.zoff(dz)),
                )
            else:
                for far in range(net.depth - 1):
                    arrived(self.bz.at[far], self.ssz.at[far], self.rsz.at[far], net.xp)
                    terms.append(self.bz.at[far])
                add_into(out, terms, self.rows, self.chunk)


def scatter_keys(part, depth):
    rows, cols = part.shape[1:]

    def kernel(part_ref, out, *scratch):
        net = Net(depth)
        sends = Sends()
        greet(net.zpeers() + [net.xp, net.cp])
        work = ShardScatter(net, sends, part_ref, scratch)
        work.begin()
        work.end(out)
        sends.finish()

    return pl.pallas_call(
        kernel,
        out_shape=jax.ShapeDtypeStruct((rows, cols), F32),
        in_specs=[vmem()],
        out_specs=vmem(),
        scratch_shapes=ShardScatter.scratch(depth, rows, cols),
        compiler_params=comm_params(5),
        name="scatter_keys",
    )(part)


def closing(part, moe, depth):
    rows, cols = part.shape[1:]

    def kernel(part_ref, moe_ref, own_out, pair_out, moe_out, low, sm, rm, sy, ry, ls, *scratch):
        net = Net(depth)
        sends = Sends()
        me = net.i * SEQ + net.y
        mine = pltpu.make_async_copy(moe_ref.at[net.i], moe_out.at[me], ls.at[0])
        greet(net.zpeers() + net.plane())
        work = ShardScatter(net, sends, part_ref, scratch)
        work.begin()
        n = 0
        for di in range(INNER):
            for dy in range(SEQ):
                if di or dy:
                    i = lax.rem(net.i + di, INNER)
                    device = net.dev(i=i, y=lax.rem(net.y + dy, SEQ))
                    sends.start(moe_ref.at[i], moe_out.at[me], sm.at[n], rm.at[n], device)
                    n += 1
        mine.start()
        work.end(own_out)
        low[...] = own_out[...].astype(BF)
        sends.start(low, pair_out, sy.at[0], ry.at[0], net.yp)
        n = 0
        for di in range(INNER):
            for dy in range(SEQ):
                if di or dy:
                    frm = lax.rem(net.i - di + INNER, INNER) * SEQ + lax.rem(net.y + dy, SEQ)
                    arrived(moe_out.at[frm], sm.at[n], rm.at[n], net.yp)
                    n += 1
        arrived(pair_out, sy.at[0], ry.at[0], net.yp)
        sends.finish()
        mine.wait()

    return pl.pallas_call(
        kernel,
        out_shape=(
            jax.ShapeDtypeStruct((rows, cols), F32),
            jax.ShapeDtypeStruct((rows, cols), BF),
            jax.ShapeDtypeStruct((E,) + moe.shape[1:], BF),
        ),
        in_specs=[vmem(), hbm()],
        out_specs=(vmem(), vmem(), hbm()),
        scratch_shapes=[pltpu.VMEM((rows, cols), BF)]
        + dma_sems(E - 1, E - 1, 1, 1, 1)
        + ShardScatter.scratch(depth, rows, cols),
        compiler_params=comm_params(6),
        name="closing",
    )(part, moe)


def turn(values, cosine, sine):
    return values * cosine + pltpu.roll(values, HEAD // 2, 1) * sine


def project(stream, gain, weights, cosine, sine):
    rows = stream.shape[0]
    wide = 2 * HEAD

    def kernel(s_ref, g_ref, w_ref, c_ref, n_ref, h_ref, o_ref):
        n = pl.program_id(0)

        @pl.when(n == 0)
        def _():
            x = s_ref[...].astype(F32)
            scale = lax.rsqrt(jnp.mean(x * x, axis=-1, keepdims=True) + EPS)
            h_ref[...] = (x * scale * g_ref[...]).astype(BF)

        r = dot(h_ref[...], w_ref[...])
        first = turn(r[:, :HEAD], c_ref[...], n_ref[...])

        @pl.when(n < 3)
        def _():
            o_ref[:, :HEAD] = (first * (SCALE * LOG2E)).astype(BF)
            second = turn(r[:, HEAD:], c_ref[...], n_ref[...])
            o_ref[:, HEAD:] = (second * (SCALE * LOG2E)).astype(BF)

        @pl.when(n == 3)
        def _():
            o_ref[:, :HEAD] = first.astype(BF)
            o_ref[:, HEAD:] = r[:, HEAD:].astype(BF)

    fixed = lambda shape: pl.BlockSpec(shape, lambda n: (0, 0))
    return pl.pallas_call(
        kernel,
        grid=(QKV // wide,),
        in_specs=[
            fixed((rows, WIDTH)),
            fixed((1, WIDTH)),
            pl.BlockSpec((WIDTH, wide), lambda n: (0, n)),
            fixed((rows, HEAD)),
            fixed((rows, HEAD)),
        ],
        out_specs=(fixed((rows, WIDTH)), pl.BlockSpec((rows, wide), lambda n: (0, n))),
        out_shape=(
            jax.ShapeDtypeStruct((rows, WIDTH), BF),
            jax.ShapeDtypeStruct((rows, QKV), BF),
        ),
        compiler_params=pltpu.CompilerParams(vmem_limit_bytes=32 << 20),
        name="project",
    )(stream, gain, weights, cosine, sine)


def unturn(dq, dkv, cosine, sine):
    rows = dq.shape[0]

    def kernel(dq_ref, dkv_ref, c_ref, n_ref, o_ref):
        c, s = c_ref[...], -n_ref[...]
        for h in range(GROUP):
            at = slice(h * HEAD, (h + 1) * HEAD)
            o_ref[:, at] = turn(dq_ref[:, at].astype(F32), c, s).astype(BF)
        dk = dkv_ref[:, :HEAD].astype(BF).astype(F32)
        o_ref[:, QCOLS : QCOLS + HEAD] = turn(dk, c, s).astype(BF)
        o_ref[:, QCOLS + HEAD :] = dkv_ref[:, HEAD:].astype(BF)

    return pl.pallas_call(
        kernel,
        in_specs=[vmem()] * 4,
        out_specs=vmem(),
        out_shape=jax.ShapeDtypeStruct((rows, QKV), BF),
        compiler_params=pltpu.CompilerParams(vmem_limit_bytes=32 << 20),
        name="unturn",
    )(dq, dkv, cosine, sine)


def attend_forward(q, kv, lo, info, tile=512):
    block = q.shape[1]

    def kernel(info_ref, q_ref, kv_ref, lo_ref, o_ref, m_ref, l_ref, acc, top, total):
        for j in range(2):
            base = info_ref[j] * block
            first = info_ref[2 + j] // tile
            last = (base + block - 1) // tile
            acc[...] = jnp.zeros_like(acc)
            top[...] = jnp.full_like(top, NEG)
            total[...] = jnp.zeros_like(total)

            def step(t, masked):
                start = pl.multiple_of(t * tile, tile)
                k = kv_ref[pl.ds(start, tile), :HEAD]
                vt = kv_ref[pl.ds(start, tile), HEAD:].T
                if masked:
                    key = start + lax.broadcasted_iota(jnp.int32, (tile, block), 0)
                    query = base + lax.broadcasted_iota(jnp.int32, (tile, block), 1)
                    ok = (key <= query) & (key >= lo_ref[j])
                for h in range(GROUP):
                    s = dot(k, q_ref[j, :, h * HEAD : (h + 1) * HEAD], NT)
                    if masked:
                        s = jnp.where(ok, s, NEG)
                    m0 = top[h : h + 1, :]
                    m1 = jnp.maximum(m0, jnp.max(s, axis=0, keepdims=True))
                    p = jnp.exp2(s - m1)
                    f = jnp.exp2(m0 - m1)
                    top[h : h + 1, :] = m1
                    total[h : h + 1, :] = total[h : h + 1, :] * f + jnp.sum(
                        p, axis=0, keepdims=True
                    )
                    acc[h] = acc[h] * f + dot(vt, p.astype(BF))

            free_from = jnp.minimum((info_ref[4 + j] + tile - 1) // tile, last + 1)
            free_to = jnp.maximum(base // tile, free_from)

            def run(a, b, masked):
                lax.fori_loop(a, b, lambda t, c: (step(t, masked), c)[1], 0)

            run(first, free_from, True)
            run(free_from, free_to, False)
            run(jnp.maximum(free_to, first), last + 1, True)
            for h in range(GROUP):
                o_ref[j, :, h * HEAD : (h + 1) * HEAD] = (
                    (acc[h] / total[h : h + 1, :]).T.astype(BF)
                )
            m_ref[j] = top[...]
            l_ref[j] = total[...]

    stat = jax.ShapeDtypeStruct((2, 8, block), F32)
    return pl.pallas_call(
        kernel,
        out_shape=(jax.ShapeDtypeStruct(q.shape, BF), stat, stat),
        in_specs=[smem()] + [vmem()] * 3,
        out_specs=(vmem(),) * 3,
        scratch_shapes=[
            pltpu.VMEM((GROUP, HEAD, block), F32),
            pltpu.VMEM((8, block), F32),
            pltpu.VMEM((8, block), F32),
        ],
        compiler_params=pltpu.CompilerParams(vmem_limit_bytes=48 << 20),
        cost_estimate=pl.CostEstimate(
            flops=int(1e10), bytes_accessed=6 << 20, transcendentals=13 << 20
        ),
        name="attend_forward",
    )(info, q, kv, lo)


def attend_backward(q, kv, lo, info, m, l, dob, ob, tile=512):
    block = q.shape[1]
    keys = kv.shape[0]
    tiles = keys // tile

    def kernel(info_ref, q_ref, kv_ref, lo_ref, m_ref, l_ref, do_ref, ob_ref, dq_ref, dkv_ref, da, dl, acc):
        acc[...] = jnp.zeros_like(acc)
        for j in range(2):
            for h in range(GROUP):
                c = slice(h * HEAD, (h + 1) * HEAD)
                d = do_ref[j, :, c].astype(F32)
                o = ob_ref[j, :, c].astype(F32)
                inv = 1.0 / l_ref[j, h : h + 1, :]
                da[j, h] = (d.T * inv).T.astype(BF)
                dl[j, h : h + 1, :] = -jnp.sum((d * o).T, axis=0, keepdims=True) * inv
        low = jnp.minimum(info_ref[2], info_ref[3]) // tile
        high = (info_ref[1] * block + block - 1) // tile

        def clear(t, carry):
            dkv_ref[pl.ds(pl.multiple_of(t * tile, tile), tile), :] = jnp.zeros((tile, 2 * HEAD), BF)
            return carry

        lax.fori_loop(0, low, clear, 0)
        lax.fori_loop(high + 1, tiles, clear, 0)

        def piece(t, j, masked):
            start = pl.multiple_of(t * tile, tile)
            base = info_ref[j] * block
            k = kv_ref[pl.ds(start, tile), :HEAD]
            v = kv_ref[pl.ds(start, tile), HEAD:]
            kt = k.T
            if masked:
                key = start + lax.broadcasted_iota(jnp.int32, (tile, block), 0)
                query = base + lax.broadcasted_iota(jnp.int32, (tile, block), 1)
                ok = (key <= query) & (key >= lo_ref[j])
            dk = dv = None
            for h in range(GROUP):
                qh = q_ref[j, :, h * HEAD : (h + 1) * HEAD]
                s = dot(k, qh, NT) - m_ref[j, h : h + 1, :]
                if masked:
                    s = jnp.where(ok, s, NEG)
                p = jnp.exp2(s)
                dah = da[j, h]
                dvh = dot(p.astype(BF), dah)
                dp = dot(v, dah, NT) + dl[j, h : h + 1, :]
                ds = (p * dp).astype(BF)
                dkh = dot(ds, qh)
                acc[j, h] += dot(kt, ds)
                dk = dkh if dk is None else dk + dkh
                dv = dvh if dv is None else dv + dvh
            return dk * LN2, dv

        def tile_step(t, carry):
            start = pl.multiple_of(t * tile, tile)
            rows = pl.ds(start, tile)

            def put(j, masked):
                dk, dv = piece(t, j, masked)
                if j == 0:
                    dk = dk + dkv_ref[rows, :HEAD].astype(F32)
                    dv = dv + dkv_ref[rows, HEAD:].astype(F32)
                dkv_ref[rows, :HEAD] = dk.astype(BF)
                dkv_ref[rows, HEAD:] = dv.astype(BF)

            for j in (1, 0):
                base = info_ref[j] * block
                live = (start <= base + block - 1) & (start + tile > info_ref[2 + j])
                free = (start + tile - 1 <= base) & (start >= info_ref[4 + j])
                if j == 1:

                    @pl.when(jnp.logical_not(live))
                    def _():
                        clear(t, 0)

                @pl.when(live & free)
                def _():
                    put(j, False)

                @pl.when(live & jnp.logical_not(free))
                def _():
                    put(j, True)

            return carry

        lax.fori_loop(low, high + 1, tile_step, 0)
        for j in range(2):
            for h in range(GROUP):
                dq_ref[j, :, h * HEAD : (h + 1) * HEAD] = (acc[j, h] * SCALE).T.astype(BF)

    return pl.pallas_call(
        kernel,
        out_shape=(jax.ShapeDtypeStruct(q.shape, BF), jax.ShapeDtypeStruct(kv.shape, BF)),
        in_specs=[smem()] + [vmem()] * 7,
        out_specs=(vmem(),) * 2,
        scratch_shapes=[
            pltpu.VMEM((2, GROUP, block, HEAD), BF),
            pltpu.VMEM((2, 8, block), F32),
            pltpu.VMEM((2, GROUP, HEAD, block), F32),
        ],
        compiler_params=pltpu.CompilerParams(vmem_limit_bytes=60 << 20),
        cost_estimate=pl.CostEstimate(
            flops=int(2.5e10), bytes_accessed=12 << 20, transcendentals=13 << 20
        ),
        name="attend_backward",
    )(info, q, kv, lo, m, l, dob, ob)


def rms_parts(x):
    scale = lax.rsqrt(jnp.mean(x * x, axis=-1, keepdims=True) + EPS)
    return x * scale, scale


def rms_pull(normed, scale, grad, gain):
    inner = grad * gain
    return scale * (inner - normed * jnp.mean(inner * normed, axis=-1, keepdims=True))


def document_first(index, starts):
    return jnp.max(jnp.where(starts <= index[..., None], starts, 0), axis=-1)


def gelu_product(gate_pre, up_pre):
    return jax.nn.gelu(gate_pre, approximate=False) * up_pre


class Zigzag:
    def __init__(self, shards):
        last = 2 * shards - 1
        home = lambda b: b if b < shards else last - b
        self.rows = [
            [(s * 2 + y, home(2 * s + k) * 2 + y) for s in range(shards) for y in range(2)]
            for k in range(2)
        ]
        self.heads = [
            [
                (s * 2 + g, s if (g == 0) == (k == 0) else last - s)
                for s in range(shards)
                for g in range(2)
            ]
            for k in range(2)
        ]

    @staticmethod
    def move(x, pairs, back=False):
        return lax.ppermute(x, AXES, [(b, a) for a, b in pairs] if back else pairs)


def pick(flag, a, b):
    return jnp.where(flag, a, b), jnp.where(flag, b, a)


def experts(h2, out_grad, chosen, router_w, moe_w, rows_in, rows_out, me):
    blocks, tokens = h2.shape[:2]
    logits = dot(h2.reshape(blocks * tokens, WIDTH), router_w)
    probs = jax.nn.softmax(logits, axis=-1)
    mine = (jnp.arange(E) == me).astype(F32)
    named = jnp.sum(chosen * mine[None, :, None], axis=1)
    gate_tok = jnp.sum(probs * mine[None, :], axis=-1).reshape(blocks, tokens) * named
    upper = (jnp.arange(tokens)[:, None] <= jnp.arange(tokens)[None, :]).astype(BF)
    rank = dot(named.astype(BF), upper) - 1.0
    pick_slot = (
        rank[:, None, :] == jnp.arange(MOST, dtype=F32)[None, :, None]
    ) & (named[:, None, :] > 0.5)
    onehot = pick_slot.astype(BF)
    slots = blocks * MOST
    gate = jnp.sum(jnp.where(pick_slot, gate_tok[:, None, :], 0.0), axis=-1).reshape(slots, 1)
    spread = lambda v: lax.dot_general(
        onehot, v, (((2,), (1,)), ((0,), (0,))), preferred_element_type=F32
    )
    collect = lambda v: lax.dot_general(
        onehot, v, (((1,), (1,)), ((0,), (0,))), preferred_element_type=F32
    )
    rows = spread(h2).astype(BF).reshape(slots, WIDTH)
    slot_grad = spread(out_grad).astype(BF).reshape(slots, WIDTH)
    gate_w = moe_w[:, :rows_in, :FF].reshape(WIDTH, FF)
    up_w = moe_w[:, :rows_in, FF:].reshape(WIDTH, FF)
    down_w = moe_w[:, rows_in:, :].reshape(FF, WIDTH)
    gate_pre = dot(rows, gate_w)
    up_pre = dot(rows, up_w)
    active_f, pull = jax.vjp(gelu_product, gate_pre, up_pre)
    active = active_f.astype(BF)
    out = dot(active, down_w)
    slot_gf = slot_grad.astype(F32)
    gate_grad = jnp.sum(slot_gf * out, axis=-1).reshape(blocks, MOST)
    mixture = collect((out * gate).astype(BF).reshape(blocks, MOST, WIDTH)).astype(BF)
    expert_grad = (slot_gf * gate).astype(BF)
    active_grad = dot(expert_grad, down_w, NT)
    g_low, u_low = (v.astype(BF) for v in pull(active_grad))
    back = dot(g_low, gate_w, NT) + dot(u_low, up_w, NT)
    back_tok = collect(back.astype(BF).reshape(blocks, MOST, WIDTH)).astype(BF)
    gate_back = jnp.sum(jnp.where(pick_slot, gate_grad[:, :, None], 0.0), axis=1)
    lanes = (jnp.arange(EXTRA) == me).astype(F32)
    back_tok = jnp.concatenate(
        [back_tok, (gate_back[:, :, None] * lanes[None, None, :]).astype(BF)], axis=-1
    )
    shards = WIDTH // rows_in
    grads = jnp.concatenate(
        [
            jnp.concatenate(
                [
                    dot(rows, g_low, TN).astype(BF).reshape(shards, rows_in, FF),
                    dot(rows, u_low, TN).astype(BF).reshape(shards, rows_in, FF),
                ],
                axis=-1,
            ),
            dot(active, expert_grad, TN).astype(BF).reshape(shards, rows_out, WIDTH),
        ],
        axis=1,
    )
    return mixture, back_tok, grads


def local(depth, stream, doc_starts, routes, attn_gain, w_query, w_key, w_value, w_out, ffn_gain, w_router, w_gate, w_up, w_down, out_grad):
    tokens = stream.shape[0]
    rows_in, rows_out = w_gate.shape[1], w_down.shape[1]
    shards = depth * INNER
    z, i, y = (lax.axis_index(a) for a in AXES)
    shard = z * INNER + i
    own_block = shard * SEQ + y
    me = i * SEQ + y
    zig = Zigzag(shards)

    cut = lambda w, width: lax.dynamic_slice_in_dim(w, y * width, width, 1)
    extra = jnp.concatenate(
        [
            attn_gain[:, None],
            ffn_gain[:, None],
            w_router,
            jnp.zeros((rows_in, EXTRA - 2 - E), BF),
        ],
        axis=1,
    )
    pack = jnp.concatenate(
        [cut(w_query, QCOLS), cut(w_key, HEAD), cut(w_value, HEAD), extra, w_out], axis=1
    )
    moe_pack = jnp.concatenate([jnp.concatenate([w_gate, w_up], axis=2), w_down], axis=1)
    chosen_t = jnp.any(
        routes.T[:, None, :] == jnp.arange(E, dtype=jnp.int32)[None, :, None], axis=0
    ).astype(F32)
    weights, moe_part, stream_pair, chosen_all = opening(pack, moe_pack, stream, chosen_t, depth)
    grad_plane = lax.all_gather(out_grad, ("inner", "seq"), axis=0, tiled=False)
    moe_w = lax.all_gather(moe_part, "outer", axis=0, tiled=True)
    weights = weights.reshape(WIDTH, PACK)
    extra_w = weights[:, QKV : QKV + EXTRA]
    gains = extra_w[:, :2].astype(F32).T
    gain_a, gain_f = gains[0:1], gains[1:2]
    router_w = extra_w[:, 2 : 2 + E]
    qkv_w = weights[:, :QKV]
    out_w = weights[:, QKV + EXTRA :]

    pair_index = shard * SEQ * tokens + jnp.arange(SEQ * tokens, dtype=jnp.int32)
    position = pair_index - document_first(pair_index, doc_starts)
    freq = ROPE_BASE ** (-(jnp.arange(HEAD // 2, dtype=F32) * 2.0) / HEAD)
    angle = position.astype(F32)[:, None] * freq[None, :]
    cos_half, sin_half = jnp.cos(angle), jnp.sin(angle)
    cosine = jnp.concatenate([cos_half, cos_half], axis=1)
    sine = jnp.concatenate([-sin_half, sin_half], axis=1)

    pair = stream_pair.reshape(SEQ * tokens, WIDTH)
    h1, qkv = project(pair, gain_a, qkv_w, cosine, sine)
    even = lax.rem(shard, 2) == 0
    q_pair = qkv[:, :QCOLS].reshape(SEQ, tokens, QCOLS)
    q_low, q_high = pick(even, *(zig.move(q_pair[k], zig.rows[k]) for k in range(2)))
    q = jnp.stack([q_low, q_high])
    kv = gather_keys(qkv[:, QCOLS:], depth).reshape(shards * SEQ * tokens, 2 * HEAD)

    block_ids = jnp.stack([shard, 2 * shards - 1 - shard]).astype(jnp.int32)
    query_index = block_ids[:, None] * tokens + jnp.arange(tokens, dtype=jnp.int32)[None, :]
    lo = document_first(query_index, doc_starts).astype(jnp.int32)
    info = jnp.concatenate([block_ids, lo[:, 0], lo[:, -1], jnp.zeros((2,), jnp.int32)])
    lo = lo[:, None, :]
    ob, top, total = attend_forward(q, kv, lo, info)

    head_zero = y == 0
    ob_a, ob_b = pick(head_zero, ob[0], ob[1])
    low_half = own_block < shards
    half_0, half_1 = pick(
        low_half, zig.move(ob_a, zig.heads[0]), zig.move(ob_b, zig.heads[1])
    )
    mixed = jnp.concatenate([half_0, half_1], axis=1)
    x1 = stream.astype(F32) + dot(mixed, out_w)
    normed, scale = rms_parts(x1)
    h2 = (normed * gain_f).astype(BF)
    h2_plane = gather_plane(h2, depth, 3)

    mixture_part, back_part, moe_grads = experts(
        h2_plane, grad_plane, chosen_all, router_w, moe_w, rows_in, rows_out, me
    )
    back = scatter_plane(back_part, depth)
    mixture = lax.psum_scatter(mixture_part, ("inner", "seq"), scatter_dimension=0, tiled=False)
    moe_own = lax.psum_scatter(
        moe_grads.reshape(depth, INNER, rows_in + rows_out, WIDTH),
        "outer",
        scatter_dimension=0,
        tiled=False,
    )
    result = (x1 + mixture.astype(F32)).astype(BF)

    chosen = chosen_t.T
    probs = jax.nn.softmax(dot(h2, router_w), axis=-1)
    dp = back[:, WIDTH : WIDTH + E] * chosen
    dz = (probs * (dp - jnp.sum(dp * probs, axis=-1, keepdims=True))).astype(BF)
    router_part = dot(h2, dz, TN)
    dh2 = back[:, :WIDTH] + dot(dz, router_w, NT)
    grad_f = out_grad.astype(F32)
    dx1 = grad_f + rms_pull(normed, scale, dh2, gain_f)
    gain_f_part = jnp.sum(dh2 * normed, axis=0)
    dx1_low = dx1.astype(BF)
    out_part = dot(mixed, dx1_low, TN)
    dob = dot(dx1_low, out_w, NT).astype(BF)

    dob_a, dob_b = pick(low_half, dob[:, :QCOLS], dob[:, QCOLS:])
    dob_low, dob_high = pick(
        head_zero,
        zig.move(dob_a, zig.heads[0], True),
        zig.move(dob_b, zig.heads[1], True),
    )
    dob_zig = jnp.stack([dob_low, dob_high])
    dq, dkv_part = attend_backward(q, kv, lo, info, top, total, dob_zig, ob)
    dq_a, dq_b = pick(even, dq[0], dq[1])
    dq_pair = jnp.concatenate(
        [zig.move(dq_a, zig.rows[0], True), zig.move(dq_b, zig.rows[1], True)], axis=0
    )
    dkv = scatter_keys(dkv_part.reshape(shards, SEQ * tokens, 2 * HEAD), depth)
    raw = unturn(dq_pair, dkv, cosine, sine)
    qkv_part = dot(h1, raw, TN)
    dh1 = dot(raw, qkv_w, NT)

    normed_pair, scale_pair = rms_parts(pair.astype(F32))
    gain_a_part = jnp.sum(dh1 * normed_pair, axis=0)
    dh1 = dh1.reshape(SEQ, tokens, WIDTH)
    mine, other = pick(head_zero, dh1[0], dh1[1])
    theirs = lax.ppermute(other.astype(BF), "seq", [(0, 1), (1, 0)])
    normed_s, scale_s = rms_parts(stream.astype(F32))
    stream_grad = (
        dx1 + rms_pull(normed_s, scale_s, mine + theirs.astype(F32), gain_a)
    ).astype(BF)

    small = jnp.concatenate(
        [
            gain_a_part[:, None],
            gain_f_part[:, None],
            router_part,
            jnp.zeros((WIDTH, EXTRA - 2 - E), F32),
        ],
        axis=1,
    )
    dense = jnp.concatenate([qkv_part, small, out_part], axis=1).astype(BF)
    own, peer, moe_out = closing(dense.reshape(shards, rows_in, PACK), moe_own, depth)
    peer = peer.astype(F32)

    def halves(a, b):
        return jnp.concatenate(
            pick(head_zero, own[:, a:b], peer[:, a:b]), axis=1
        )

    both = own[:, QKV:] + peer[:, QKV:]
    moe_out = moe_out.astype(F32)
    return (
        result,
        stream_grad,
        both[:, 0],
        halves(0, QCOLS),
        halves(QCOLS, QCOLS + HEAD),
        halves(QCOLS + HEAD, QKV),
        both[:, EXTRA:],
        both[:, 1],
        both[:, 2 : 2 + E],
        moe_out[:, :rows_in, :FF],
        moe_out[:, :rows_in, FF:],
        moe_out[:, rows_in:, :],
    )


def solution(mesh):
    shards = mesh.shape["shard"]
    depth = shards // INNER
    fine = Mesh(mesh.devices.reshape(depth, INNER, SEQ), AXES)
    shard = ("outer", "inner")
    tokens = P(AXES, None)
    in_specs = (
        tokens,
        P(),
        tokens,
        P(shard),
        P(shard, None),
        P(shard, None),
        P(shard, None),
        P(shard, None),
        P(shard),
        P(shard, None),
        P(None, shard, None),
        P(None, shard, None),
        P(None, shard, None),
        tokens,
    )
    out_specs = (
        tokens,
        tokens,
        P(shard),
        P(shard, None),
        P(shard, None),
        P(shard, None),
        P(shard, None),
        P(shard),
        P(shard, None),
        P(None, shard, None),
        P(None, shard, None),
        P(None, shard, None),
    )

    def run(*args):
        return local(depth, *args)

    return jax.shard_map(run, mesh=fine, in_specs=in_specs, out_specs=out_specs, check_vma=False)
```

time: 2760 us -> 890 us (0.32)
  waiting for transfers between devices: 2040 us -> 55.7 us
  Pallas kernels: 0 us -> 467 us
  blocking collectives: 203 us -> 0 us
  matrix products: 222 us -> 117 us
  starting transfers between devices: 12.8 us -> 112 us
  other arithmetic: 113 us -> 53.3 us
  loops' own time: 55 us -> 0 us
  local copies, waits for them, and re-layouts: 93.1 us -> 59.1 us
    reduce_scatter x9 -> x2, waiting for transfers between devices: 1690 us -> 0.01 us  [the longest x1 0.01 us: local(): lax.psum_scatter(mixture_part, ('inner', 'seq'), scatter_dimension=0, til...]
    pallas_call x0 -> x10, Pallas kernels: none -> 467 us  [the longest x1 119 us: closing(): pl.pallas_call(kernel, out_shape=(jax.ShapeDtypeStruct((rows, cols), F32)...]
    all_gather x7 -> x2, waiting for transfers between devices: 221 us -> 0.01 us  [the longest x1 0.01 us: local(): moe_w = lax.all_gather(moe_part, 'outer', axis=0, tiled=True)]
    ppermute x0 -> x9, starting transfers between devices: none -> 112 us  [the longest x8 111 us: move(): return lax.ppermute(x, AXES, [(b, a) for a, b in pairs] if back else pairs)]
    psum x2 -> x0, waiting for transfers between devices: 106 us -> none  [the longest x1 106 us: local(): lax.psum(query_part.astype(jnp.bfloat16), 'seq').astype(jnp.float32)]
    dot_general x30 -> x23, matrix products: 220 us -> 117 us  [the longest x19 97.7 us: dot(): return lax.dot_general(a, b, dims, preferred_element_type=F32)]
    unnamed x2 -> x0, blocking collectives: 93.9 us -> none
    all_gather x3 -> x0, blocking collectives: 62.3 us -> none  [the longest x1 22.8 us: local(): lax.all_gather(key_projection, 'shard', axis=0, tiled=True)]
  transfers between devices with their start and end apart: 22 -> 13, of which waited for: 16 -> 2; matrix products, arithmetic and copies ran while one was open for 9% -> 19% of each run, Pallas kernels for 0% -> 31%
where the time goes in v1:
time: 890 us; the launch traced here: 880 us
  Pallas kernels  467 us (52%)
  matrix products  117 us (13%)
  starting transfers between devices  112 us (13%)
  local copies, waits for them, and re-layouts  59.1 us (7%)
  waiting for transfers between devices  55.7 us (6%)
  other arithmetic  53.3 us (6%)
  between operations  15.1 us (2%)
    pallas_call x1, Pallas kernels, closing(): pl.pallas_call(kernel, out_shape=(jax.ShapeDtypeStruct((rows, cols), F32)...  119 us
    ppermute x8, starting transfers between devices, move(): return lax.ppermute(x, AXES, [(b, a) for a, b in pairs] if back else pairs)  111 us
    dot_general x19, matrix products, dot(): return lax.dot_general(a, b, dims, preferred_element_type=F32)  97.7 us
    pallas_call x1, Pallas kernels, opening(): pl.pallas_call(kernel, out_shape=(jax.ShapeDtypeStruct((depth * INNER,) +...  73.6 us
    pallas_call x1, Pallas kernels, gather_keys(): pl.pallas_call(kernel, out_shape=jax.ShapeDtypeStruct((depth * INNER,) +...  68.6 us
    ppermute x8, waiting for transfers between devices, move(): return lax.ppermute(x, AXES, [(b, a) for a, b in pairs] if back else pairs)  54.9 us
    pallas_call x1, Pallas kernels, attend_backward(): pl.pallas_call(kernel, out_shape=(jax.ShapeDtypeStruct(q.shape, BF), jax....  49.4 us
    pallas_call x1, Pallas kernels, attend_forward(): pl.pallas_call(kernel, out_shape=(jax.ShapeDtypeStruct(q.shape, BF), stat...  44.9 us
  transfers between devices with their start and end apart: 13, of which 2 were waited for; matrix products, arithmetic and copies ran while one was open for 19% of the time, Pallas kernels for 31%

profile of v1, /device:TPU:0, one launch (start us, length us, event | category | flops | bytes accessed | tf_op | source)
XLA Modules:
  0.0 879.6 jit_solution(6965324735298559099)
XLA Ops:
  12.3 3.3 pad_maximum_fusion.2.moe_ref
  16.6 73.6 %opening.1 = (bf16[16,96,2688]{2,1,0:T(8,128)(2,1)}, bf16[4,144,1536]{2,1,0:T(8,128)(2,1)}, bf16[2,256,1536]{2,1,0:T(8,128)(2,1)}, f32[8,8,256]{2,1,0:T(8,128)}) custom-call(bf16[96,2688]{1,0:T(8,128)(2,1)} %concatenate.71.pack_ref, bf16[8,144,1536]{2,1,0:T(8,128)(2,1)} %pad_maximum_fusion.2.moe_ref, bf16[256,1536]{1,0:T(8,128)(2,1)} %st_ref.1, ...), custom_call_target="tpu_custom_call" | custom-call | tf_op jit(solution)/shard_map/opening/pallas_call | solution.py:221
  93.0 2.2 slice.170.w_ref
  95.2 3.2 slice_reduce_fusion.5
  103.0 4.3 project.1
  110.1 3.8 collective-permute-start.1
  115.8 68.6 %gather_keys.1 = bf16[16,512,256]{2,1,0:T(8,128)(2,1)} custom-call(bf16[512,256]{1,0:T(8,128)(2,1)} %slice.134.src), custom_call_target="tpu_custom_call" | custom-call | tf_op jit(solution)/shard_map/gather_keys/pallas_call | solution.py:250
  185.0 2.5 copy-done.4
  187.5 44.9 %attend_forward.1 = (bf16[2,256,768]{2,1,0:T(8,128)(2,1)S(1)}, f32[2,8,256]{2,1,0:T(8,128)S(1)}, f32[2,8,256]{2,1,0:T(8,128)S(1)}) custom-call(s32[8]{0:T(128)S(1)} %concatenate.70.info_ref, bf16[2,256,768]{2,1,0:T(8,128)(2,1)S(1)} %pad_maximum_fusion.3.q_ref, bf16[8192,256]{1,0:T(8,128)(2,1)S(1)} %bitcast.95, s32[2,1,256]{2,1,0:T(1,128)S(1)} %broadcast_in_dim.51.lo_ref), custom_call_target="tpu_custom_call" | custom-call | flops 10000000000 | bytes 6291456 | tf_op jit(solution)/shard_map/attend_forward/pallas_call | solution.py:653
  233.2 62.7 %collective-permute-start.3 = (bf16[256,768]{1,0:T(8,128)(2,1)S(1)}, bf16[256,768]{1,0:T(8,128)(2,1)S(1)}, u32[]{:S(2)}, u32[]{:S(2)}) collective-permute-start(bf16[256,768]{1,0:T(8,128)(2,1)S(1)} %get-tuple-element.138), channel_id=1, source_target_pairs={{0,31},{1,0},{2,30},{3,1},{4,29},{5,2},{6,28},{7,3},{8,27},{9,4},{... | collective-permute-start | bytes 1179656 | tf_op jit(solution)/shard_map/ppermute | solution.py:815
  296.1 18.8 %collective-permute-done.3 = bf16[256,768]{1,0:T(8,128)(2,1)S(1)} collective-permute-done((bf16[256,768]{1,0:T(8,128)(2,1)S(1)}, bf16[256,768]{1,0:T(8,128)(2,1)S(1)}, u32[]{:S(2)}, u32[]{:S(2)}) %collective-permute-start.3) | collective-permute-done | bytes 393248 | tf_op jit(solution)/shard_map/ppermute | solution.py:815
  315.0 4.1 multiply_reduce_fusion.4
  321.4 32.1 %gather_plane.1 = bf16[8,256,1536]{2,1,0:T(8,128)(2,1)} custom-call(bf16[256,1536]{1,0:T(8,128)(2,1)} %multiply_convert_fusion.3.src), custom_call_target="tpu_custom_call" | custom-call | tf_op jit(solution)/shard_map/gather_plane/pallas_call | solution.py:301
  353.5 4.6 fusion.63
  358.3 6.3 convolution_convert_fusion.4
  366.6 2.8 fusion.60
  369.4 3.8 fusion.65
  375.4 14.9 %multiply_convert_fusion.2 = (bf16[1536,768]{1,0:T(8,128)(2,1)}, f32[1536,768]{1,0:T(8,128)}, f32[1536,768]{1,0:T(8,128)}) fusion(f32[1536,768]{1,0:T(8,128)S(1)} %fusion.65, bf16[1536,1536]{1,0:T(8,128)(2,1)S(1)} %bitcast.103, bf16[1536,768]{1,0:T(8,128)(2,1)S(1)} %bitcast.125), kind=kOutput, calls=%fused_computation.17 | convolution fusion | flops 3701735424 | bytes 23592960 | tf_op jit(solution)/shard_map/dot_general | solution.py:38
  390.3 4.3 convolution_convert_fusion.3
  394.6 6.3 fusion.1
  401.9 11.1 %fusion.2 = (bf16[1536,1536]{1,0:T(8,128)(2,1)}, bf16[1536,1536]{1,0:T(8,128)(2,1)}) fusion(bf16[8,192,1536]{2,1,0:T(8,128)(2,1)} %copy-done.19, f32[1536]{0:T(1024)S(1)} %mul.286, f32[1536,1536]{1,0:T(8,128)} %get-tuple-element.150), kind=kLoop, calls=%fused_computation.5 | loop fusion | flops 11796480 | bytes 23599104 | tf_op jit(solution)/shard_map/convert_element_type | solution.py:856
  413.0 6.9 convolution_convert_fusion.2
  420.0 3.3 fusion
  423.4 7.1 convolution_convert_fusion.6
  430.5 10.2 %multiply_convert_fusion.1 = (bf16[1536,768]{1,0:T(8,128)(2,1)}, bf16[1536,768]{1,0:T(8,128)(2,1)S(1)}) fusion(f32[1536,768]{1,0:T(8,128)} %get-tuple-element.111, f32[1536,768]{1,0:T(8,128)} %copy-done.53, f32[1536,768]{1,0:T(8,128)} %get-tuple-element.148, bf16[1536,1536]{1,0:T(8,128)(2,1)S(1)} %bitcast.108, bf16[768,1536]{1,0:T(8,128)(2,1)S(1)} %bitcast.124), kind=kOutput, calls=%fused_computation.15 | convolution fusion | flops 3645112320 | bytes 25952256 | tf_op jit(solution)/shard_map/dot_general | solution.py:38
  440.7 4.2 convolution_convert_fusion.8
  444.9 4.2 convolution_convert_fusion.7
  449.1 3.4 pad_maximum_fusion
  455.8 10.1 %fusion.66 = f32[1536,1536]{1,0:T(8,128)} fusion(bf16[1536,768]{1,0:T(8,128)(2,1)} %copy-done.52, bf16[1536,768]{1,0:T(8,128)(2,1)} %bitcast.128), kind=kOutput, calls=%fused_computation.170 | convolution fusion | flops 3623878656 | bytes 14155776 | tf_op jit(solution)/shard_map/dot_general | solution.py:38
  465.9 7.5 add_convert_fusion
  475.3 3.4 pad_maximum_fusion.1.part_ref
  478.6 38.4 %scatter_plane.1 = f32[256,1664]{1,0:T(8,128)} custom-call(bf16[8,256,1664]{2,1,0:T(8,128)(2,1)} %pad_maximum_fusion.1.part_ref), custom_call_target="tpu_custom_call" | custom-call | tf_op jit(solution)/shard_map/scatter_plane/pallas_call | solution.py:376
  519.3 3.4 multiply_reduce_fusion.2
  522.7 3.2 multiply_add_fusion
  526.0 4.4 fusion.16
  531.1 3.1 collective-permute-start.5
  534.8 36.2 %collective-permute-done.5 = bf16[256,768]{1,0:T(8,128)(2,1)S(1)} collective-permute-done((bf16[256,768]{1,0:T(8,128)(2,1)S(1)}, bf16[256,768]{1,0:T(8,128)(2,1)S(1)}, u32[]{:S(2)}, u32[]{:S(2)}) %collective-permute-start.5) | collective-permute-done | bytes 393248 | tf_op jit(solution)/shard_map/ppermute | solution.py:815
  572.0 49.4 %attend_backward.1 = (bf16[2,256,768]{2,1,0:T(8,128)(2,1)}, bf16[8192,256]{1,0:T(8,128)(2,1)}) custom-call(s32[8]{0:T(128)} %copy-done.14, bf16[2,256,768]{2,1,0:T(8,128)(2,1)} %copy-done.11, bf16[8192,256]{1,0:T(8,128)(2,1)} %bitcast.94, s32[2,1,256]{2,1,0:T(1,128)} %copy-done.13, f32[2,8,256]{2,1,0:T(8,128)} %copy-done.17, f32[2,8,256]{2,1,0:T(8,128)} %copy-done.18, ...), custom_call_target="tpu_custom_call" | custom-call | flops 24999999488 | bytes 12582912 | tf_op jit(solution)/shard_map/attend_backward/pallas_call | solution.py:760
  623.4 4.5 collective-permute-start.6
  627.9 34.8 %collective-permute-start.7 = (bf16[256,768]{1,0:T(8,128)(2,1)S(1)}, bf16[256,768]{1,0:T(8,128)(2,1)}, u32[]{:S(2)}, u32[]{:S(2)}) collective-permute-start(bf16[256,768]{1,0:T(8,128)(2,1)S(1)} %get-tuple-element.129), channel_id=1, source_target_pairs={{2,0},{3,1},{6,2},{7,3},{10,4},{11,5},{14,6},{15,7},{18,8},{19,9},... | collective-permute-start | bytes 1179656 | tf_op jit(solution)/shard_map/ppermute | solution.py:815
  665.4 36.2 %scatter_keys.1.dkv_ref = f32[512,256]{1,0:T(8,128)} custom-call(bf16[16,512,256]{2,1,0:T(8,128)(2,1)} %bitcast.110), custom_call_target="tpu_custom_call" | custom-call | tf_op jit(solution)/shard_map/scatter_keys/pallas_call | solution.py:466
  704.4 3.9 multiply_reduce_fusion
  711.8 3.6 convolution_convert_fusion
  716.9 3.5 convolution_convert_fusion.5
  721.2 13.9 %concatenate.84.part_ref = bf16[16,96,2688]{2,1,0:T(8,128)(2,1)} concatenate(bf16[16,96,1024]{2,1,0:T(8,128)(2,1)} %bitcast.111, bf16[16,96,1]{2,1,0:T(8,128)(2,1)} %concatenate.93, bf16[16,96,1]{2,1,0:T(8,128)(2,1)} %concatenate.94, bf16[16,96,8]{2,1,0:T(8,128)(2,1)} %bitcast.130, bf16[16,96,118]{2,1,0:T(8,128)(2,1)} %broadcast_in_dim.56, bf16[16,96,1536]{2,1,0:T(8,128)(2,1)} %bitcast.97), dimensions={2} | concatenate | bytes 16515072 | tf_op jit(solution)/shard_map/concatenate | solution.py:1018
  737.2 2.6 fusion.25
  739.8 119.4 %closing.1 = (f32[96,2688]{1,0:T(8,128)}, bf16[96,2688]{1,0:T(8,128)(2,1)}, bf16[8,144,1536]{2,1,0:T(8,128)(2,1)}) custom-call(bf16[16,96,2688]{2,1,0:T(8,128)(2,1)} %concatenate.84.part_ref, bf16[4,144,1536]{2,1,0:T(8,128)(2,1)} %bitcast.129), custom_call_target="tpu_custom_call" | custom-call | tf_op jit(solution)/shard_map/closing/pallas_call | solution.py:511
  862.2 4.5 fusion.61
  (229 shorter events, 61.1 us)
Async XLA Ops:
  7.2 8.5 copy-start.40
  7.2 357.4 %all-gather.4.cloned.1.call-start = ((), (), s32[]{:S(2)}) async-start(), calls=%async_computation.2 | async-start | bytes 8847360 | tf_op jit(solution)/shard_map/all_gather | solution.py:912
  90.3 300.0 %all-gather.6.cloned.1.call-start = ((), (), s32[]{:S(2)}) async-start(), calls=%async_computation.5 | async-start | bytes 7077888 | tf_op jit(solution)/shard_map/all_gather | solution.py:911
  91.0 431.7 %reduce-scatter.3.cloned.1.call-start = ((), (), s32[]{:S(2)}) async-start(), calls=%async_computation.3 | async-start | bytes 7077888 | tf_op jit(solution)/shard_map/reduce_scatter | solution.py:960
  93.0 6.9 copy-start.49
  98.5 220.7 %copy-start.41 = (f32[1536]{0:T(1024)}, f32[1536]{0:T(1024)S(1)}, u32[]{:S(2)}) copy-start(f32[1536]{0:T(1024)S(1)} %get-tuple-element.103) | copy-start | bytes 18436
  101.3 6.0 copy-start.5
  101.3 7.2 copy-start.7
  103.0 81.7 %copy-start.44 = (f32[8,8,256]{2,1,0:T(8,128)S(1)}, f32[8,8,256]{2,1,0:T(8,128)}, u32[]{:S(2)}) copy-start(f32[8,8,256]{2,1,0:T(8,128)} %get-tuple-element.30) | copy-start | bytes 196612
  109.4 75.4 %collective-permute-start = (bf16[256,768]{1,0:T(8,128)(2,1)S(1)}, bf16[256,768]{1,0:T(8,128)(2,1)S(1)}, u32[]{:S(2)}, u32[]{:S(2)}) collective-permute-start(bf16[256,768]{1,0:T(8,128)(2,1)S(1)} %get-tuple-element.126), channel_id=1, source_target_pairs={{0,0},{1,1},{2,4},{3,5},{4,8},{5,9},{6,12},{7,13},{8,16},{9,17},{1... | collective-permute-start | bytes 1179656 | tf_op jit(solution)/shard_map/ppermute | solution.py:815
  110.1 74.7 %collective-permute-start.1 = (bf16[256,768]{1,0:T(8,128)(2,1)S(1)}, bf16[256,768]{1,0:T(8,128)(2,1)S(1)}, u32[]{:S(2)}, u32[]{:S(2)}) collective-permute-start(bf16[256,768]{1,0:T(8,128)(2,1)S(1)} %get-tuple-element.127), channel_id=1, source_target_pairs={{0,2},{1,3},{2,6},{3,7},{4,10},{5,11},{6,14},{7,15},{8,18},{9,19},... | collective-permute-start | bytes 1179656 | tf_op jit(solution)/shard_map/ppermute | solution.py:815
  184.4 48.0 %copy-start.13 = (s32[2,1,256]{2,1,0:T(1,128)}, s32[2,1,256]{2,1,0:T(1,128)S(1)}, u32[]{:S(2)}) copy-start(s32[2,1,256]{2,1,0:T(1,128)S(1)} %broadcast_in_dim.51.lo_ref) | copy-start | bytes 6148
  184.7 47.7 %copy-start.14 = (s32[8]{0:T(128)}, s32[8]{0:T(128)S(1)}, u32[]{:S(2)}) copy-start(s32[8]{0:T(128)S(1)} %concatenate.70.info_ref) | copy-start | bytes 100
  185.0 47.4 %copy-start.11 = (bf16[2,256,768]{2,1,0:T(8,128)(2,1)}, bf16[2,256,768]{2,1,0:T(8,128)(2,1)S(1)}, u32[]{:S(2)}) copy-start(bf16[2,256,768]{2,1,0:T(8,128)(2,1)S(1)} %pad_maximum_fusion.3.q_ref) | copy-start | bytes 2359300
  187.5 127.5 %copy-start.28 = (bf16[256,1536]{1,0:T(8,128)(2,1)S(1)}, bf16[256,1536]{1,0:T(8,128)(2,1)}, u32[]{:S(2)}) copy-start(bf16[256,1536]{1,0:T(8,128)(2,1)} %st_ref.1) | copy-start | bytes 2359300
  232.4 86.7 %copy-start.12 = (bf16[2,256,768]{2,1,0:T(8,128)(2,1)}, bf16[2,256,768]{2,1,0:T(8,128)(2,1)S(1)}, u32[]{:S(2)}) copy-start(bf16[2,256,768]{2,1,0:T(8,128)(2,1)S(1)} %get-tuple-element.29.ob_ref) | copy-start | bytes 2359300
  232.4 86.7 %copy-start.17 = (f32[2,8,256]{2,1,0:T(8,128)}, f32[2,8,256]{2,1,0:T(8,128)S(1)}, u32[]{:S(2)}) copy-start(f32[2,8,256]{2,1,0:T(8,128)S(1)} %get-tuple-element.32.m_ref) | copy-start | bytes 49156
  232.5 86.7 %copy-start.18 = (f32[2,8,256]{2,1,0:T(8,128)}, f32[2,8,256]{2,1,0:T(8,128)S(1)}, u32[]{:S(2)}) copy-start(f32[2,8,256]{2,1,0:T(8,128)S(1)} %get-tuple-element.33.l_ref) | copy-start | bytes 49156
  232.5 63.6 %collective-permute-start.2 = (bf16[256,768]{1,0:T(8,128)(2,1)S(1)}, bf16[256,768]{1,0:T(8,128)(2,1)S(1)}, u32[]{:S(2)}, u32[]{:S(2)}) collective-permute-start(bf16[256,768]{1,0:T(8,128)(2,1)S(1)} %get-tuple-element.137), channel_id=1, source_target_pairs={{0,0},{1,31},{2,1},{3,30},{4,2},{5,29},{6,3},{7,28},{8,4},{9,27},{... | collective-permute-start | bytes 1179656 | tf_op jit(solution)/shard_map/ppermute | solution.py:815
  233.2 81.7 %collective-permute-start.3 = (bf16[256,768]{1,0:T(8,128)(2,1)S(1)}, bf16[256,768]{1,0:T(8,128)(2,1)S(1)}, u32[]{:S(2)}, u32[]{:S(2)}) collective-permute-start(bf16[256,768]{1,0:T(8,128)(2,1)S(1)} %get-tuple-element.138), channel_id=1, source_target_pairs={{0,31},{1,0},{2,30},{3,1},{4,29},{5,2},{6,28},{7,3},{8,27},{9,4},{... | collective-permute-start | bytes 1179656 | tf_op jit(solution)/shard_map/ppermute | solution.py:815
  319.2 34.4 %copy-start.47 = (f32[256]{0:T(256)}, f32[256]{0:T(256)S(1)}, u32[]{:S(2)}) copy-start(f32[256]{0:T(256)S(1)} %add_rsqrt_fusion.1) | copy-start | bytes 3076
  364.6 4.8 slice-start
  394.6 6.3 copy-start.19
  420.0 319.8 %reduce-scatter.5.cloned.1.call-start = ((), (), s32[]{:S(2)}) async-start(), calls=%async_computation.4 | async-start | bytes 8847360 | tf_op jit(solution)/shard_map/reduce_scatter | solution.py:961
  423.4 17.3 %slice-start.2 = ((s8[4718592]{0:T(1024)(128)(4,1)}), s8[4194304]{0:T(1024)(128)(4,1)S(1)}, s32[]{:S(2)}) async-start(s8[4718592]{0:T(1024)(128)(4,1)} %bitcast.104), calls=%async_computation.8 | async-start | bytes 8388608
  430.5 10.2 %slice-start.3 = ((s8[4718592]{0:T(1024)(128)(4,1)}), s8[524288]{0:T(1024)(128)(4,1)S(1)}, s32[]{:S(2)}) async-start(s8[4718592]{0:T(1024)(128)(4,1)} %bitcast.104), calls=%async_computation.9 | async-start | bytes 1048576
  455.8 10.1 %copy-start.33 = (bf16[16,96,768]{2,1,0:T(8,128)(2,1)S(1)}, bf16[16,96,768]{2,1,0:T(8,128)(2,1)}, u32[]{:S(2)}) copy-start(bf16[16,96,768]{2,1,0:T(8,128)(2,1)} %copy-done.32) | copy-start | bytes 7077892
  455.8 10.1 %copy-start.55 = (bf16[1536,768]{1,0:T(8,128)(2,1)S(1)}, bf16[1536,768]{1,0:T(8,128)(2,1)}, u32[]{:S(2)}) copy-start(bf16[1536,768]{1,0:T(8,128)(2,1)} %get-tuple-element.112) | copy-start | bytes 7077892
  478.6 40.7 %copy-start.27 = (f32[256,1536]{1,0:T(8,128)S(1)}, f32[256,1536]{1,0:T(8,128)}, u32[]{:S(2)}) copy-start(f32[256,1536]{1,0:T(8,128)} %copy-done.26) | copy-start | bytes 4718596
  478.6 40.7 %copy-start.42 = (f32[1536]{0:T(1024)S(1)}, f32[1536]{0:T(1024)}, u32[]{:S(2)}) copy-start(f32[1536]{0:T(1024)} %copy-done.41) | copy-start | bytes 18436
  478.6 40.7 %copy-start.48 = (f32[256]{0:T(256)S(1)}, f32[256]{0:T(256)}, u32[]{:S(2)}) copy-start(f32[256]{0:T(256)} %copy-done.47) | copy-start | bytes 3076
  526.0 8.2 copy-start.3
  526.0 8.6 copy-start.29
  530.4 4.4 collective-permute-start.4
  531.1 39.9 %collective-permute-start.5 = (bf16[256,768]{1,0:T(8,128)(2,1)S(1)}, bf16[256,768]{1,0:T(8,128)(2,1)S(1)}, u32[]{:S(2)}, u32[]{:S(2)}) collective-permute-start(bf16[256,768]{1,0:T(8,128)(2,1)S(1)} %get-tuple-element.133), channel_id=1, source_target_pairs={{31,0},{0,1},{30,2},{1,3},{29,4},{2,5},{28,6},{3,7},{27,8},{4,9},{... | collective-permute-start | bytes 1179656 | tf_op jit(solution)/shard_map/ppermute | solution.py:815
  621.4 81.3 %copy-start.6 = (f32[512,128]{1,0:T(8,128)S(1)}, f32[512,128]{1,0:T(8,128)}, u32[]{:S(2)}) copy-start(f32[512,128]{1,0:T(8,128)} %copy-done.5) | copy-start | bytes 786436
  621.4 81.3 %copy-start.8 = (f32[512,128]{1,0:T(8,128)S(1)}, f32[512,128]{1,0:T(8,128)}, u32[]{:S(2)}) copy-start(f32[512,128]{1,0:T(8,128)} %copy-done.7) | copy-start | bytes 786436
  623.4 78.2 %collective-permute-start.6 = (bf16[256,768]{1,0:T(8,128)(2,1)}, bf16[256,768]{1,0:T(8,128)(2,1)}, u32[]{:S(2)}, u32[]{:S(2)}) collective-permute-start(bf16[256,768]{1,0:T(8,128)(2,1)} %get-tuple-element.128), channel_id=1, source_target_pairs={{0,0},{1,1},{4,2},{5,3},{8,4},{9,5},{12,6},{13,7},{16,8},{17,9},{2... | collective-permute-start | bytes 1179656 | tf_op jit(solution)/shard_map/ppermute | solution.py:815
  627.9 73.7 %collective-permute-start.7 = (bf16[256,768]{1,0:T(8,128)(2,1)S(1)}, bf16[256,768]{1,0:T(8,128)(2,1)}, u32[]{:S(2)}, u32[]{:S(2)}) collective-permute-start(bf16[256,768]{1,0:T(8,128)(2,1)S(1)} %get-tuple-element.129), channel_id=1, source_target_pairs={{2,0},{3,1},{6,2},{7,3},{10,4},{11,5},{14,6},{15,7},{18,8},{19,9},... | collective-permute-start | bytes 1179656 | tf_op jit(solution)/shard_map/ppermute | solution.py:815
  704.3 7.4 copy-start.23
  704.3 7.4 copy-start.36
  704.3 7.4 copy-start.38
  710.9 5.9 copy-start.16
  710.9 24.2 %collective-permute-start.8 = (bf16[256,1536]{1,0:T(8,128)(2,1)}, bf16[256,1536]{1,0:T(8,128)(2,1)}, u32[]{:S(2)}, u32[]{:S(2)}) collective-permute-start(bf16[256,1536]{1,0:T(8,128)(2,1)} %select_convert_fusion), channel_id=1, source_target_pairs={{0,1},{1,0},{2,3},{3,2},{4,5},{5,4},{6,7},{7,6},{8,9},{9,8},{10,11... | collective-permute-start | bytes 2359304 | tf_op jit(solution)/shard_map/ppermute | solution.py:1003
  721.2 13.9 %copy-start.21 = (f32[512,1536]{1,0:T(8,128)S(1)}, f32[512,1536]{1,0:T(8,128)}, u32[]{:S(2)}) copy-start(f32[512,1536]{1,0:T(8,128)} %copy-done.20) | copy-start | bytes 9437188
  721.2 13.9 %copy-start.43 = (f32[1536]{0:T(1024)S(1)}, f32[1536]{0:T(1024)}, u32[]{:S(2)}) copy-start(f32[1536]{0:T(1024)} %get-tuple-element.102) | copy-start | bytes 18436
  862.2 6.2 copy-start.39
  862.2 10.7 %copy-start.1 = (bf16[96,1536]{1,0:T(8,128)(2,1)S(1)}, bf16[96,1536]{1,0:T(8,128)(2,1)}, u32[]{:S(2)}) copy-start(bf16[96,1536]{1,0:T(8,128)(2,1)} %param.18) | copy-start | bytes 884740
  (25 other events, 67.3 us)
Sparse Core Ops, SparseCore 0:
  90.4 169.4 all-gather.3
  261.7 57.8 all-gather.5
  420.1 59.5 reduce-scatter.2
  482.0 138.1 reduce-scatter.4

commit v2 on v1

--- a/solution.py
+++ b/solution.py
@@ -18,6 +18,7 @@
 QCOLS = GROUP * HEAD
 QKV = QCOLS + 2 * HEAD
 EXTRA = 128
+FIRST = QKV + EXTRA
 PACK = QKV + EXTRA + WIDTH
 EPS = 1e-06
 ROPE_BASE = 10000.0
@@ -91,14 +92,16 @@
     def __init__(self):
         self.items = []
 
-    def start(self, src, dst, ssem, rsem, device):
-        copy = remote(src, dst, ssem, rsem, device)
-        copy.start()
-        self.items.append(copy)
+    def start(self, *refs):
+        self.later(lambda: refs)
+
+    def later(self, refs):
+        remote(*refs()).start()
+        self.items.append(refs)
 
     def finish(self):
-        for copy in self.items:
-            copy.wait_send()
+        for refs in self.items:
+            remote(*refs()).wait_send()
 
 
 def arrived(dst, ssem, rsem, device):
@@ -107,12 +110,25 @@
 
 def dma_sems(*counts):
     return [pltpu.SemaphoreType.DMA((n,)) for n in counts]
+
+
+class FlatSlots:
+    class At:
+        def __init__(self, ref, rows):
+            self.ref, self.rows = ref, rows
+
+        def __getitem__(self, n):
+            return self.ref.at[pl.ds(pl.multiple_of(n * self.rows, self.rows), self.rows)]
+
+    def __init__(self, ref, rows):
+        self.at = self.At(ref, rows)
 
 
 class ShardGather:
     def __init__(self, net, sends, src, out, sems):
         self.net, self.sends, self.src, self.out = net, sends, src, out
         self.sz, self.rz, self.sx, self.rx, self.sc, self.rc = sems
+        self.xi = lax.rem(net.i + 2, INNER)
 
     @staticmethod
     def sems(depth):
@@ -128,20 +144,27 @@
         self.sends.start(self.src, me, self.sx.at[0], self.rx.at[0], net.xp)
         self.sends.start(self.src, me, self.sc.at[0], self.rc.at[0], net.cp)
 
-    def end(self):
+    def pass_on(self, dz, i, ssem, rsem, n, device):
+        self.sends.later(
+            lambda: (self.slot(dz, i), self.slot(dz, i), ssem.at[n], rsem.at[n], device)
+        )
+
+    def after_z(self):
+        net = self.net
+        for dz in range(1, net.depth):
+            block = self.slot(dz, net.i)
+            arrived(block, self.sz.at[dz - 1], self.rz.at[dz - 1], net.xp)
+            self.pass_on(dz, net.i, self.sx, self.rx, dz, net.xp)
+            self.pass_on(dz, net.i, self.sc, self.rc, dz, net.cp)
+
+    def after_x(self):
         net, depth = self.net, self.net.depth
-        xi = lax.rem(net.i + 2, INNER)
-        for dz in range(1, depth):
-            block = self.slot(dz, net.i)
-            arrived(block, self.sz.at[dz - 1], self.rz.at[dz - 1], net.zpeers()[dz - 1])
-            self.sends.start(block, block, self.sx.at[dz], self.rx.at[dz], net.xp)
-            self.sends.start(block, block, self.sc.at[dz], self.rc.at[dz], net.cp)
         for dz in range(depth):
-            block = self.slot(dz, xi)
-            arrived(block, self.sx.at[dz], self.rx.at[dz], net.xp)
-            self.sends.start(
-                block, block, self.sc.at[depth + dz], self.rc.at[depth + dz], net.cp
-            )
+            arrived(self.slot(dz, self.xi), self.sx.at[dz], self.rx.at[dz], net.xp)
+            self.pass_on(dz, self.xi, self.sc, self.rc, depth + dz, net.cp)
+
+    def last(self):
+        net, depth = self.net, self.net.depth
         ci = net.i + 1 - 2 * net.core
         for dz in range(depth):
             arrived(self.slot(dz, ci), self.sc.at[dz], self.rc.at[dz], net.cp)
@@ -152,6 +175,26 @@
                 self.rc.at[depth + dz],
                 net.cp,
             )
+
+    def end(self):
+        self.after_z()
+        self.after_x()
+        self.last()
+
+    def one_x(self, dz):
+        net, block, n = self.net, self.slot(dz, self.xi), self.net.depth + dz
+        arrived(block, self.sx.at[dz], self.rx.at[dz], net.xp)
+        remote(block, block, self.sc.at[n], self.rc.at[n], net.cp).start()
+
+    def one_c(self, n, place):
+        block = self.out.at[place]
+        arrived(block, self.sc.at[n], self.rc.at[n], self.net.cp)
+
+    def sent_loop(self):
+        net, depth = self.net, self.net.depth
+        for dz in range(depth):
+            block = self.slot(dz, self.xi)
+            remote(block, block, self.sc.at[depth + dz], self.rc.at[depth + dz], net.cp).wait_send()
 
 
 def hbm():
@@ -773,6 +816,535 @@
         ),
         name="attend_backward",
     )(info, q, kv, lo, m, l, dob, ob)
+
+
+class PlaneGather:
+    @staticmethod
+    def sems():
+        return dma_sems(2, 2, 2, 2, 5, 5)
+
+    def __init__(self, net, sends, src, out, sems, rows):
+        self.net, self.sends, self.src, self.out = net, sends, src, out
+        self.sx, self.rx, self.sy, self.ry, self.sc, self.rc = sems
+        half = rows // 2
+        self.lo, self.hi = pl.ds(0, half), pl.ds(half, half)
+        xi = lax.rem(net.i + 2, INNER)
+        ci = net.i + 1 - 2 * net.core
+        cx = lax.rem(ci + 2, INNER)
+        place = lambda i, y: i * SEQ + y
+        self.me, self.xb = place(net.i, net.y), place(xi, net.y)
+        self.yb, self.db = place(net.i, 1 - net.y), place(xi, 1 - net.y)
+        self.core_blocks = [place(ci, net.y), place(ci, 1 - net.y), place(cx, net.y)]
+        self.core_diag = place(cx, 1 - net.y)
+
+    def begin(self):
+        self.begin_y()
+        self.begin_x()
+
+    def begin_y(self):
+        net, out, src = self.net, self.out, self.src
+        self.sends.start(src, out.at[self.me], self.sy.at[0], self.ry.at[0], net.yp)
+        self.sends.start(src, out.at[self.me], self.sc.at[0], self.rc.at[0], net.cp)
+
+    def begin_x(self):
+        net, out, src = self.net, self.out, self.src
+        self.sends.start(src, out.at[self.me], self.sx.at[0], self.rx.at[0], net.xp)
+
+    def pass_on(self, block, part, ssem, rsem, n, device):
+        def refs():
+            at = self.out.at[block] if part is None else self.out.at[block, part]
+            return at, at, ssem.at[n], rsem.at[n], device
+
+        self.sends.later(refs)
+
+    def middle(self):
+        net, out = self.net, self.out
+        arrived(out.at[self.yb], self.sy.at[0], self.ry.at[0], net.yp)
+        self.pass_on(self.yb, self.lo, self.sx, self.rx, 1, net.xp)
+        self.pass_on(self.yb, None, self.sc, self.rc, 1, net.cp)
+        arrived(out.at[self.xb], self.sx.at[0], self.rx.at[0], net.xp)
+        self.pass_on(self.xb, self.hi, self.sy, self.ry, 1, net.yp)
+        self.pass_on(self.xb, None, self.sc, self.rc, 2, net.cp)
+
+    def end(self):
+        net, out = self.net, self.out
+        arrived(out.at[self.db, self.lo], self.sx.at[1], self.rx.at[1], net.xp)
+        self.pass_on(self.db, self.lo, self.sc, self.rc, 3, net.cp)
+        arrived(out.at[self.db, self.hi], self.sy.at[1], self.ry.at[1], net.yp)
+        self.pass_on(self.db, self.hi, self.sc, self.rc, 4, net.cp)
+
+    def last(self):
+        net, out = self.net, self.out
+        for n, block in enumerate(self.core_blocks):
+            arrived(out.at[block], self.sc.at[n], self.rc.at[n], net.cp)
+        arrived(out.at[self.core_diag, self.lo], self.sc.at[3], self.rc.at[3], net.cp)
+        arrived(out.at[self.core_diag, self.hi], self.sc.at[4], self.rc.at[4], net.cp)
+
+
+class Route:
+    def __init__(self, net, sends_to, comes_from):
+        self.net = net
+        me = net.z * INNER + net.i
+        self.local = (sends_to[0] == me) & (sends_to[1] == net.y)
+        self.kept = (comes_from[0] == me) & (comes_from[1] == net.y)
+        self.to, self.frm = self.device(sends_to), self.device(comes_from)
+
+    def device(self, place):
+        shard, y = place
+        return self.net.dev(z=lax.div(shard, INNER), i=lax.rem(shard, INNER), y=y)
+
+    def hello(self):
+        @pl.when(jnp.logical_not(self.kept))
+        def _():
+            pl.semaphore_signal(
+                pltpu.get_barrier_semaphore(), inc=1, device_id=self.frm, device_id_type=MESH
+            )
+
+        return jnp.where(self.local, 0, 1)
+
+    def send(self, refs):
+        @pl.when(self.local)
+        def _():
+            src, dst, _, _ = refs()
+            dst[...] = src[...]
+
+        @pl.when(jnp.logical_not(self.local))
+        def _():
+            remote(*refs(), self.to).start()
+
+    def sent(self, refs):
+        @pl.when(jnp.logical_not(self.local))
+        def _():
+            remote(*refs(), self.to).wait_send()
+
+    def arrive(self, refs):
+        @pl.when(jnp.logical_not(self.kept))
+        def _():
+            dst, ssem, rsem = refs()
+            remote(dst, dst, ssem, rsem, self.to).wait_recv()
+
+
+class Mirror:
+    def __init__(self, net):
+        self.net = net
+        self.n = net.depth * INNER
+        self.last = 2 * self.n - 1
+        self.me = net.z * INNER + net.i
+
+    def home(self, block):
+        return jnp.where(block < self.n, block, self.last - block)
+
+    def blocks(self):
+        return self.me, self.last - self.me
+
+    def slot(self, block):
+        return jnp.where(block < self.n, 0, 1)
+
+    def rows_out(self, k):
+        block = 2 * self.me + k
+        come = self.blocks()[k]
+        return Route(
+            self.net, (self.home(block), self.net.y), (lax.div(come, 2), self.net.y)
+        ), self.slot(block)
+
+    def rows_back(self, k):
+        block = self.blocks()[k]
+        come = 2 * self.me + k
+        return Route(
+            self.net, (lax.div(block, 2), self.net.y), (self.home(come), self.net.y)
+        ), lax.rem(block, 2)
+
+    def heads_back(self, k):
+        block = self.blocks()[k]
+        own = 2 * self.me + self.net.y
+        return Route(self.net, (lax.div(block, 2), lax.rem(block, 2)), (self.home(own), k))
+
+    def heads_out(self, k):
+        own = 2 * self.me + self.net.y
+        come = self.blocks()[k]
+        return Route(
+            self.net, (self.home(own), k), (lax.div(come, 2), lax.rem(come, 2))
+        ), self.slot(own)
+
+
+class Chain:
+    @staticmethod
+    def sems(depth):
+        return dma_sems(*[max(depth - 1, 1) * INNER] * 4)
+
+    def __init__(self, net, out, sems):
+        self.net, self.out = net, out
+        self.su, self.ru, self.sd, self.rd = sems
+        self.steps = (net.depth - 1) * INNER
+        self.up = net.dev(z=jnp.minimum(net.z + 1, net.depth - 1))
+        self.down = net.dev(z=jnp.maximum(net.z - 1, 0))
+
+    def piece(self, z, q):
+        return self.out.at[z * INNER + q]
+
+    def refs(self, hop, q, way):
+        net = self.net
+        n = (hop + 1) * INNER + q
+        z = net.z - 1 - hop if way == 0 else net.z + 1 + hop
+        ssem, rsem, device = (
+            (self.su.at[n], self.ru.at[n], self.up)
+            if way == 0
+            else (self.sd.at[n], self.rd.at[n], self.down)
+        )
+        return self.piece(z, q), ssem, rsem, device
+
+    def begin(self, ready):
+        def body(q, carry):
+            ready(q)
+            for way in range(2):
+
+                @pl.when(self.net.z < self.net.depth - 1 if way == 0 else self.net.z > 0)
+                def _():
+                    dst, ssem, rsem, device = self.refs(-1, q, way)
+                    remote(dst, dst, ssem, rsem, device).start()
+
+            return carry
+
+        lax.fori_loop(0, INNER, body, 0)
+
+    def step(self, n):
+        net = self.net
+        hop, q = lax.div(n, INNER), lax.rem(n, INNER)
+        for way in range(2):
+            z = net.z - 1 - hop if way == 0 else net.z + 1 + hop
+            here = z >= 0 if way == 0 else z <= net.depth - 1
+            further = net.z < net.depth - 1 if way == 0 else net.z > 0
+
+            @pl.when(here)
+            def _():
+                block = self.piece(z, q)
+                if way == 0:
+                    arrived(block, self.su.at[n], self.ru.at[n], self.up)
+                else:
+                    arrived(block, self.sd.at[n], self.rd.at[n], self.down)
+
+            @pl.when(here & further)
+            def _():
+                dst, ssem, rsem, device = self.refs(hop, q, way)
+                remote(dst, dst, ssem, rsem, device).start()
+
+    def run(self, a, b):
+        def body(n, carry):
+            self.step(n)
+            return carry
+
+        lax.fori_loop(a, min(b, self.steps), body, 0)
+
+    def finish(self):
+        def body(n, carry):
+            hop, q = lax.div(n, INNER) - 1, lax.rem(n, INNER)
+            for way in range(2):
+                z = self.net.z - 1 - hop if way == 0 else self.net.z + 1 + hop
+                here = z >= 0 if way == 0 else z <= self.net.depth - 1
+                further = self.net.z < self.net.depth - 1 if way == 0 else self.net.z > 0
+
+                @pl.when(here & further)
+                def _():
+                    dst, ssem, rsem, device = self.refs(hop, q, way)
+                    remote(dst, dst, ssem, rsem, device).wait_send()
+
+            return carry
+
+        lax.fori_loop(0, self.steps, body, 0)
+
+
+def seg_tile(start, rows, st, en):
+    key = start + lax.broadcasted_iota(jnp.int32, (rows, HEAD), 0)
+    return ((key >= st) & (key < en)).astype(F32).astype(BF)
+
+
+def front(stream, pack, moe, chosen, cosine, sine, w_out, out_grad, qseg, starts, depth):
+    block = stream.shape[0]
+    rows = block * SEQ
+    shards = depth * INNER
+    part = w_out.shape[0]
+
+    def kernel(
+        st_ref, pk_ref, mo_ref, ch_ref, c_ref, n_ref, wo_ref, og_ref, qs_ref, sg_ref,
+        s_out, w_full, ch_out, h1_out, q_out, kv_out, o_out, m_out, l_out, mix_out, x1_out, h2_out,
+        wf_out, og_out, mo_out,
+        qp, acc, top, total, h2_own, gains, own, sq, rq, so, ro, sy, ry, sp, rp, sm, rm, *sems,
+    ):
+        net = Net(depth)
+        sends = Sends()
+        mirror = Mirror(net)
+        gp = ShardGather(net, sends, pk_ref, FlatSlots(w_full, part), sems[28:34])
+        gk = ShardGather(net, sends, None, kv_out, sems[:6])
+        gk.src = gk.slot(0, net.i)
+        gw = ShardGather(net, sends, wo_ref, FlatSlots(wf_out, part), sems[6:12])
+        gg = PlaneGather(net, sends, og_ref, og_out, sems[12:18], block)
+        gh = PlaneGather(net, sends, h2_own, h2_out, sems[18:24], block)
+        chain = Chain(net, mo_out, sems[24:28])
+        rows_out = [mirror.rows_out(k) for k in range(2)]
+        heads = [mirror.heads_back(k) for k in range(2)]
+        barrier = pltpu.get_barrier_semaphore()
+        for device in net.zpeers() + net.plane():
+            pl.semaphore_signal(barrier, inc=1, device_id=device, device_id_type=MESH)
+        count = depth - 1 + E - 1
+        for route in [r for r, _ in rows_out] + heads:
+            count = count + route.hello()
+        here = lambda y: s_out.at[pl.ds(pl.multiple_of(y * block, block), block)]
+        mine_p = pltpu.make_async_copy(pk_ref, gp.slot(0, net.i), own.at[4])
+        mine_s = pltpu.make_async_copy(st_ref, here(net.y), own.at[5])
+        mine_m = pltpu.make_async_copy(
+            mo_ref.at[net.i * SEQ + net.y], mo_out.at[net.z * INNER + net.i], own.at[3]
+        )
+        mine_c = pltpu.make_async_copy(ch_ref, ch_out.at[net.i * SEQ + net.y], own.at[6])
+        mine_g = pltpu.make_async_copy(og_ref, og_out.at[gg.me], own.at[0])
+        mine_w = pltpu.make_async_copy(wo_ref, gw.slot(0, net.i), own.at[1])
+        for copy in (mine_p, mine_s, mine_m, mine_c, mine_g, mine_w):
+            copy.start()
+        pl.semaphore_wait(barrier, count)
+        gp.begin()
+        sends.start(st_ref, here(net.y), sy.at[0], ry.at[0], net.yp)
+        for n, device in enumerate(net.plane()):
+            sends.start(ch_ref, ch_out.at[net.i * SEQ + net.y], sp.at[n], rp.at[n], device)
+        gw.begin()
+        gp.end()
+        for di in range(1, INNER):
+            other = lax.rem(net.i + di, INNER)
+            sends.start(
+                mo_ref.at[other * SEQ + net.y],
+                mo_out.at[net.z * INNER + net.i],
+                sm.at[di - 1],
+                rm.at[di - 1],
+                net.dev(i=other),
+            )
+        gg.begin_y()
+
+        def moe_ready(q):
+            di = lax.rem(net.i - q + INNER, INNER)
+
+            @pl.when(di > 0)
+            def _():
+                arrived(mo_out.at[net.z * INNER + q], sm.at[di - 1], rm.at[di - 1], net.xp)
+
+        arrived(here(1 - net.y), sy.at[0], ry.at[0], net.yp)
+        mine_s.wait()
+        mine_p.wait()
+        tail = w_full[:, QKV:].astype(F32).T
+        gains[...] = tail[:8, :]
+
+        step = 64
+
+        def norm(n, carry):
+            at = pl.ds(pl.multiple_of(n * step, step), step)
+            x = s_out[at, :].astype(F32)
+            scale = lax.rsqrt(jnp.mean(x * x, axis=-1, keepdims=True) + EPS)
+            h1_out[at, :] = (x * scale * gains[0:1, :]).astype(BF)
+            return carry
+
+        lax.fori_loop(0, rows // step, norm, 0)
+        h1 = h1_out[...]
+        cos, sin = c_ref[...], n_ref[...]
+        r = dot(h1, w_full[:, QCOLS:QKV])
+        me = net.z * INNER + net.i
+        kv_out[me, :, :HEAD] = turn(r[:, :HEAD], cos, sin).astype(BF)
+        kv_out[me, :, HEAD:] = r[:, HEAD:].astype(BF)
+        gk.begin()
+        for h in range(0, GROUP, 2):
+            r = dot(h1, w_full[:, h * HEAD : (h + 2) * HEAD])
+            for g in range(2):
+                v = turn(r[:, g * HEAD : (g + 1) * HEAD], cos, sin) * (SCALE * LOG2E)
+                v = v.astype(BF)
+                at = slice((h + g) * HEAD, (h + g + 1) * HEAD)
+                qp[0, :, at] = v[:block]
+                qp[1, :, at] = v[block:]
+        q_refs = [
+            lambda k=k: (qp.at[k], q_out.at[rows_out[k][1]], sq.at[k], rq.at[rows_out[k][1]])
+            for k in range(2)
+        ]
+        o_refs = [
+            lambda k=k: (o_out.at[k], mix_out.at[net.y], so.at[k], ro.at[net.y]) for k in range(2)
+        ]
+        for k in range(2):
+            rows_out[k][0].send(q_refs[k])
+        mine_m.wait()
+        mine_w.wait()
+        chain.begin(moe_ready)
+        gg.begin_x()
+        acc[...] = jnp.zeros_like(acc)
+        top[...] = jnp.full_like(top, NEG)
+        total[...] = jnp.zeros_like(total)
+        gk.after_z()
+        for k in range(2):
+            rows_out[k][0].arrive(lambda: (q_out.at[k], sq.at[k], rq.at[k]))
+
+        low, high = mirror.blocks()
+        bases = (low * block, high * block)
+        xi = lax.rem(net.i + 2, INNER)
+        ci = net.i + 1 - 2 * net.core
+
+        def attend(t, j, masked):
+            start = pl.multiple_of(t * rows, rows)
+            k = jnp.concatenate(
+                [kv_out[t, :, :HEAD], seg_tile(start, rows, sg_ref[0:1, :], sg_ref[1:2, :])], axis=1
+            )
+            vt = kv_out[t, :, HEAD:].T
+            if masked:
+                key = start + lax.broadcasted_iota(jnp.int32, (rows, block), 0)
+                ok = key <= bases[j] + lax.broadcasted_iota(jnp.int32, (rows, block), 1)
+            scores = [
+                dot(
+                    k,
+                    jnp.concatenate(
+                        [q_out[j, :, h * HEAD : (h + 1) * HEAD], qs_ref[j]], axis=1
+                    ),
+                    NT,
+                )
+                for h in range(GROUP)
+            ]
+            for h in range(GROUP):
+                s = scores[h]
+                if masked:
+                    s = jnp.where(ok, s, NEG)
+                m0 = top[j, h : h + 1, :]
+                m1 = jnp.maximum(m0, jnp.max(s, axis=0, keepdims=True))
+                p = jnp.exp2(s - m1)
+                f = jnp.exp2(m0 - m1)
+                top[j, h : h + 1, :] = m1
+                total[j, h : h + 1, :] = total[j, h : h + 1, :] * f + jnp.sum(
+                    p, axis=0, keepdims=True
+                )
+                acc[j, h] = acc[j, h] * f + dot(vt, p.astype(BF))
+
+        polled = min((shards - depth) // 2, 2 * INNER - 1, chain.steps)
+
+        def tile(u, carry):
+            in_z = u < depth
+            in_x = u < 2 * depth
+            in_c = u < 3 * depth
+            dz = lax.rem(u, depth)
+            place = jnp.where(in_z, net.i, jnp.where(in_x, xi, jnp.where(in_c, ci, lax.rem(ci + 2, INNER))))
+            t = lax.rem(net.z - dz + depth, depth) * INNER + place
+
+            @pl.when((u >= depth) & in_x)
+            def _():
+                gk.one_x(dz)
+
+            @pl.when(u >= 2 * depth)
+            def _():
+                gk.one_c(u - 2 * depth, t)
+
+            @pl.when(u == 2 * depth)
+            def _():
+                gg.middle()
+                gw.after_z()
+
+            @pl.when(u == 3 * depth)
+            def _():
+                gw.after_x()
+                gg.end()
+
+            @pl.when((u >= depth) & (lax.rem(u - depth, 2) == 1) & (u - depth < 2 * polled))
+            def _():
+                chain.step(lax.div(u - depth, 2))
+
+            for j in (0, 1):
+                live = t * rows <= bases[j] + block - 1
+                free = t * rows + rows - 1 <= bases[j]
+
+                @pl.when(live & free)
+                def _():
+                    attend(t, j, False)
+
+                @pl.when(live & jnp.logical_not(free))
+                def _():
+                    attend(t, j, True)
+
+            return carry
+
+        lax.fori_loop(0, shards, tile, 0)
+        gk.sent_loop()
+        for j in range(2):
+            for h in range(GROUP):
+                o_out[j, :, h * HEAD : (h + 1) * HEAD] = (
+                    (acc[j, h] / total[j, h : h + 1, :]).T.astype(BF)
+                )
+        for k in range(2):
+            heads[k].send(o_refs[k])
+        chain.run(polled, polled + 1)
+        m_out[...] = top[...]
+        l_out[...] = total[...]
+        gw.last()
+        gg.last()
+        for k in range(2):
+            heads[k].arrive(lambda: (mix_out.at[k], so.at[k], ro.at[k]))
+        x1 = here(net.y)[...].astype(F32)
+        x1 = x1 + dot(mix_out[0], wf_out[:QCOLS, :]) + dot(mix_out[1], wf_out[QCOLS:, :])
+        x1_out[...] = x1
+        scale = lax.rsqrt(jnp.mean(x1 * x1, axis=-1, keepdims=True) + EPS)
+        h2_own[...] = (x1 * scale * gains[1:2, :]).astype(BF)
+        mine_h = pltpu.make_async_copy(h2_own, h2_out.at[gh.me], own.at[2])
+        gh.begin()
+        mine_h.start()
+        chain.run(polled + 1, 2 * INNER)
+        gh.middle()
+        chain.run(2 * INNER, 2 * INNER + 2)
+        gh.end()
+        chain.run(2 * INNER + 2, chain.steps)
+        n = 0
+        for di in range(INNER):
+            for dy in range(SEQ):
+                if di or dy:
+                    frm = lax.rem(net.i - di + INNER, INNER) * SEQ + lax.rem(net.y + dy, SEQ)
+                    arrived(ch_out.at[frm], sp.at[n], rp.at[n], net.yp)
+                    n += 1
+        mine_c.wait()
+        gh.last()
+        for k in range(2):
+            rows_out[k][0].sent(q_refs[k])
+            heads[k].sent(o_refs[k])
+        chain.finish()
+        sends.finish()
+        mine_g.wait()
+        mine_h.wait()
+
+    sds = jax.ShapeDtypeStruct
+    stat = sds((2, 8, block), F32)
+    heads_shape = sds((2, block, QCOLS), BF)
+    return pl.pallas_call(
+        kernel,
+        out_shape=(
+            sds((rows, WIDTH), BF),
+            sds((WIDTH, FIRST), BF),
+            sds((E,) + chosen.shape, F32),
+            sds((rows, WIDTH), BF),
+            heads_shape,
+            sds((shards, rows, 2 * HEAD), BF),
+            heads_shape,
+            stat,
+            stat,
+            heads_shape,
+            sds((block, WIDTH), F32),
+            sds((E, block, WIDTH), BF),
+            sds((WIDTH, WIDTH), BF),
+            sds((E, block, WIDTH), BF),
+            sds((shards,) + moe.shape[1:], BF),
+        ),
+        in_specs=[hbm()] * 4 + [vmem()] * 2 + [hbm()] * 2 + [vmem()] * 2,
+        out_specs=(vmem(), vmem(), hbm()) + (vmem(),) * 8 + (hbm(), vmem(), hbm(), hbm()),
+        scratch_shapes=[
+            pltpu.VMEM((2, block, QCOLS), BF),
+            pltpu.VMEM((2, GROUP, HEAD, block), F32),
+            pltpu.VMEM((2, 8, block), F32),
+            pltpu.VMEM((2, 8, block), F32),
+            pltpu.VMEM((block, WIDTH), BF),
+            pltpu.VMEM((8, WIDTH), F32),
+        ]
+        + dma_sems(7, 2, 2, 2, 2, 1, 1, E - 1, E - 1, INNER - 1, INNER - 1)
+        + ShardGather.sems(depth) * 2
+        + PlaneGather.sems() * 2
+        + Chain.sems(depth)
+        + ShardGather.sems(depth),
+        compiler_params=comm_params(7, 60 << 20),
+        name="front",
+    )(stream, pack, moe, chosen, cosine, sine, w_out, out_grad, qseg, starts)
 
 
 def rms_parts(x):
@@ -901,23 +1473,12 @@
         axis=1,
     )
     pack = jnp.concatenate(
-        [cut(w_query, QCOLS), cut(w_key, HEAD), cut(w_value, HEAD), extra, w_out], axis=1
+        [cut(w_query, QCOLS), cut(w_key, HEAD), cut(w_value, HEAD), extra], axis=1
     )
     moe_pack = jnp.concatenate([jnp.concatenate([w_gate, w_up], axis=2), w_down], axis=1)
     chosen_t = jnp.any(
         routes.T[:, None, :] == jnp.arange(E, dtype=jnp.int32)[None, :, None], axis=0
     ).astype(F32)
-    weights, moe_part, stream_pair, chosen_all = opening(pack, moe_pack, stream, chosen_t, depth)
-    grad_plane = lax.all_gather(out_grad, ("inner", "seq"), axis=0, tiled=False)
-    moe_w = lax.all_gather(moe_part, "outer", axis=0, tiled=True)
-    weights = weights.reshape(WIDTH, PACK)
-    extra_w = weights[:, QKV : QKV + EXTRA]
-    gains = extra_w[:, :2].astype(F32).T
-    gain_a, gain_f = gains[0:1], gains[1:2]
-    router_w = extra_w[:, 2 : 2 + E]
-    qkv_w = weights[:, :QKV]
-    out_w = weights[:, QKV + EXTRA :]
-
     pair_index = shard * SEQ * tokens + jnp.arange(SEQ * tokens, dtype=jnp.int32)
     position = pair_index - document_first(pair_index, doc_starts)
     freq = ROPE_BASE ** (-(jnp.arange(HEAD // 2, dtype=F32) * 2.0) / HEAD)
@@ -926,32 +1487,33 @@
     cosine = jnp.concatenate([cos_half, cos_half], axis=1)
     sine = jnp.concatenate([-sin_half, sin_half], axis=1)
 
-    pair = stream_pair.reshape(SEQ * tokens, WIDTH)
-    h1, qkv = project(pair, gain_a, qkv_w, cosine, sine)
-    even = lax.rem(shard, 2) == 0
-    q_pair = qkv[:, :QCOLS].reshape(SEQ, tokens, QCOLS)
-    q_low, q_high = pick(even, *(zig.move(q_pair[k], zig.rows[k]) for k in range(2)))
-    q = jnp.stack([q_low, q_high])
-    kv = gather_keys(qkv[:, QCOLS:], depth).reshape(shards * SEQ * tokens, 2 * HEAD)
-
     block_ids = jnp.stack([shard, 2 * shards - 1 - shard]).astype(jnp.int32)
     query_index = block_ids[:, None] * tokens + jnp.arange(tokens, dtype=jnp.int32)[None, :]
     lo = document_first(query_index, doc_starts).astype(jnp.int32)
     info = jnp.concatenate([block_ids, lo[:, 0], lo[:, -1], jnp.zeros((2,), jnp.int32)])
+    big = jnp.int32(1 << 30)
+    spare = jnp.full((HEAD - doc_starts.shape[0],), big)
+    first = jnp.concatenate([doc_starts, spare])
+    beyond = jnp.concatenate([doc_starts[1:], spare, big[None]])
+    starts = jnp.stack([first, beyond])
+    outside = (query_index[..., None] < first) | (query_index[..., None] >= beyond)
+    qseg = jnp.where(outside, NEG, 0.0).astype(BF)
     lo = lo[:, None, :]
-    ob, top, total = attend_forward(q, kv, lo, info)
-
+    (
+        pair, weights, chosen_all, h1, q, kv, ob, top, total, mixed, x1, h2_plane, out_w, grad_plane, moe_w,
+    ) = front(stream, pack, moe_pack, chosen_t, cosine, sine, w_out, out_grad, qseg, starts, depth)
+    extra_w = weights[:, QKV : QKV + EXTRA]
+    gains = extra_w[:, :2].astype(F32).T
+    gain_a, gain_f = gains[0:1], gains[1:2]
+    router_w = extra_w[:, 2 : 2 + E]
+    qkv_w = weights[:, :QKV]
+    kv = kv.reshape(shards * SEQ * tokens, 2 * HEAD)
+    even = lax.rem(shard, 2) == 0
     head_zero = y == 0
-    ob_a, ob_b = pick(head_zero, ob[0], ob[1])
     low_half = own_block < shards
-    half_0, half_1 = pick(
-        low_half, zig.move(ob_a, zig.heads[0]), zig.move(ob_b, zig.heads[1])
-    )
-    mixed = jnp.concatenate([half_0, half_1], axis=1)
-    x1 = stream.astype(F32) + dot(mixed, out_w)
+    mixed = jnp.concatenate([mixed[0], mixed[1]], axis=1)
     normed, scale = rms_parts(x1)
     h2 = (normed * gain_f).astype(BF)
-    h2_plane = gather_plane(h2, depth, 3)
 
     mixture_part, back_part, moe_grads = experts(
         h2_plane, grad_plane, chosen_all, router_w, moe_w, rows_in, rows_out, me

time: 890 us -> 783 us (0.88)
  starting transfers between devices: 112 us -> 44.9 us
  waiting for transfers between devices: 55.7 us -> 35.5 us
  local copies, waits for them, and re-layouts: 59.1 us -> 47.4 us
  matrix products: 117 us -> 108 us
    ppermute x8 -> x4, starting transfers between devices: 111 us -> 44.9 us  [move(): return lax.ppermute(x, AXES, [(b, a) for a, b in pairs] if back else pairs)]
    ppermute x8 -> x4, waiting for transfers between devices: 54.9 us -> 35.5 us  [move(): return lax.ppermute(x, AXES, [(b, a) for a, b in pairs] if back else pairs)]
    unnamed x123 -> x78, local copies, waits for them, and re-layouts: 15.3 us -> 6.34 us
    dot_general x19 -> x18, matrix products: 97.7 us -> 93.4 us  [dot(): return lax.dot_general(a, b, dims, preferred_element_type=F32)]
    pallas_call x5 -> x1, Pallas kernels: 224 us -> 220 us  [front(): pl.pallas_call(kernel, out_shape=(sds((rows, WIDTH), BF), sds((WIDTH, FIR...]
  transfers between devices with their start and end apart: 13 -> 7, of which waited for: 2 -> 1; matrix products, arithmetic and copies ran while one was open for 19% -> 15% of each run, Pallas kernels for 31% -> 17%
where the time goes in v2:
time: 783 us; the launch traced here: 773 us
  Pallas kernels  468 us (60%)
  matrix products  108 us (14%)
  other arithmetic  54 us (7%)
  local copies, waits for them, and re-layouts  47.4 us (6%)
  starting transfers between devices  44.9 us (6%)
  waiting for transfers between devices  35.5 us (5%)
  between operations  15.3 us (2%)
    pallas_call x1, Pallas kernels, front(): pl.pallas_call(kernel, out_shape=(sds((rows, WIDTH), BF), sds((WIDTH, FIR...  220 us
    pallas_call x1, Pallas kernels, closing(): pl.pallas_call(kernel, out_shape=(jax.ShapeDtypeStruct((rows, cols), F32)...  115 us
    dot_general x18, matrix products, dot(): return lax.dot_general(a, b, dims, preferred_element_type=F32)  93.4 us
    pallas_call x1, Pallas kernels, attend_backward(): pl.pallas_call(kernel, out_shape=(jax.ShapeDtypeStruct(q.shape, BF), jax....  49.5 us
    ppermute x4, starting transfers between devices, move(): return lax.ppermute(x, AXES, [(b, a) for a, b in pairs] if back else pairs)  44.9 us
    pallas_call x1, Pallas kernels, scatter_keys(): pl.pallas_call(kernel, out_shape=jax.ShapeDtypeStruct((rows, cols), F32),...  43.2 us
    pallas_call x1, Pallas kernels, scatter_plane(): pl.pallas_call(kernel, out_shape=jax.ShapeDtypeStruct((rows, cols), F32),...  40 us
    ppermute x4, waiting for transfers between devices, move(): return lax.ppermute(x, AXES, [(b, a) for a, b in pairs] if back else pairs)  35.5 us
  transfers between devices with their start and end apart: 7, of which 1 were waited for; matrix products, arithmetic and copies ran while one was open for 15% of the time, Pallas kernels for 17%

profile of v2, /device:TPU:0, one launch (start us, length us, event | category | flops | bytes accessed | tf_op | source)
XLA Modules:
  0.0 772.7 jit_solution(7669021009148593440)
XLA Ops:
  17.5 3.5 pad_maximum_fusion.2.mo_ref
  21.7 219.9 %front.1 = (bf16[512,1536]{1,0:T(8,128)(2,1)}, bf16[1536,1152]{1,0:T(8,128)(2,1)}, f32[8,8,256]{2,1,0:T(8,128)}, bf16[512,1536]{1,0:T(8,128)(2,1)}, bf16[2,256,7...) custom-call(bf16[256,1536]{1,0:T(8,128)(2,1)} %st_ref.1, ...), custom_call_target="tpu_custom_call" | custom-call | tf_op jit(solution)/shard_map/front/pallas_call | solution.py:1311
  242.9 5.1 fusion.55
  247.9 3.2 slice.116
  251.2 3.0 fusion.57
  254.3 4.3 convolution_convert_fusion.4
  258.7 1.4 convolution_convert_fusion.3
  260.1 2.0 copy-done.18
  262.1 3.9 fusion.59
  266.0 14.5 %multiply_convert_fusion.2 = (bf16[1536,768]{1,0:T(8,128)(2,1)S(1)}, f32[1536,768]{1,0:T(8,128)}, f32[1536,768]{1,0:T(8,128)}) fusion(f32[1536,768]{1,0:T(8,128)S(1)} %fusion.59, bf16[1536,1536]{1,0:T(8,128)(2,1)S(1)} %bitcast.92, bf16[1536,768]{1,0:T(8,128)(2,1)S(1)} %bitcast.106), kind=kOutput, calls=%fused_computation.17 | convolution fusion | flops 3701735424 | bytes 23592960 | tf_op jit(solution)/shard_map/dot_general | solution.py:39
  280.5 6.5 fusion.1
  288.0 11.1 %fusion.2 = (bf16[1536,1536]{1,0:T(8,128)(2,1)}, bf16[1536,1536]{1,0:T(8,128)(2,1)}) fusion(bf16[8,192,1536]{2,1,0:T(8,128)(2,1)} %copy-done.5, f32[1536]{0:T(1024)S(1)} %mul.278, f32[1536,1536]{1,0:T(8,128)} %get-tuple-element.143), kind=kLoop, calls=%fused_computation.5 | loop fusion | flops 11796480 | bytes 23599104 | tf_op jit(solution)/shard_map/convert_element_type | solution.py:1428
  299.1 6.8 convolution_convert_fusion.2
  306.0 3.3 fusion
  309.4 7.1 convolution_convert_fusion.6
  316.5 10.4 %multiply_convert_fusion.1 = (bf16[1536,768]{1,0:T(8,128)(2,1)}, bf16[1536,768]{1,0:T(8,128)(2,1)S(1)}) fusion(f32[1536,768]{1,0:T(8,128)} %get-tuple-element.111, f32[1536,768]{1,0:T(8,128)} %copy-done.29, f32[1536,768]{1,0:T(8,128)} %get-tuple-element.141, bf16[1536,1536]{1,0:T(8,128)(2,1)S(1)} %bitcast.97, bf16[768,1536]{1,0:T(8,128)(2,1)S(1)} %bitcast.105), kind=kOutput, calls=%fused_computation.15 | convolution fusion | flops 3645112320 | bytes 25952256 | tf_op jit(solution)/shard_map/dot_general | solution.py:39
  326.9 4.2 convolution_convert_fusion.8
  331.2 4.2 convolution_convert_fusion.7
  335.4 3.5 pad_maximum_fusion
  341.2 1.5 fusion.58
  343.3 10.0 %fusion.60 = f32[1536,1536]{1,0:T(8,128)} fusion(bf16[1536,768]{1,0:T(8,128)(2,1)} %copy-done.28, bf16[1536,768]{1,0:T(8,128)(2,1)} %bitcast.108), kind=kOutput, calls=%fused_computation.167 | convolution fusion | flops 3623878656 | bytes 14155776 | tf_op jit(solution)/shard_map/dot_general | solution.py:39
  353.3 6.5 add_convert_fusion
  359.9 1.9 convolution_convert_fusion.1
  361.8 3.4 pad_maximum_fusion.1.part_ref
  365.1 40.0 %scatter_plane.1 = f32[256,1664]{1,0:T(8,128)} custom-call(bf16[8,256,1664]{2,1,0:T(8,128)(2,1)} %pad_maximum_fusion.1.part_ref), custom_call_target="tpu_custom_call" | custom-call | tf_op jit(solution)/shard_map/scatter_plane/pallas_call | solution.py:419
  406.9 3.4 multiply_reduce_fusion
  410.4 1.3 convolution_convert_fusion.10
  411.7 3.3 multiply_add_fusion
  415.0 4.3 convolution_convert_fusion.9
  420.2 1.6 collective-permute-start
  421.9 2.0 collective-permute-start.1
  425.7 1.5 concatenate.102
  428.0 35.5 %collective-permute-done.1 = bf16[256,768]{1,0:T(8,128)(2,1)S(1)} collective-permute-done((bf16[256,768]{1,0:T(8,128)(2,1)}, bf16[256,768]{1,0:T(8,128)(2,1)S(1)}, u32[]{:S(2)}, u32[]{:S(2)}) %collective-permute-start.1) | collective-permute-done | bytes 393248 | tf_op jit(solution)/shard_map/ppermute | solution.py:1387
  464.4 49.5 %attend_backward.1 = (bf16[2,256,768]{2,1,0:T(8,128)(2,1)}, bf16[8192,256]{1,0:T(8,128)(2,1)}) custom-call(s32[8]{0:T(128)} %concatenate.84.info_ref, bf16[2,256,768]{2,1,0:T(8,128)(2,1)} %get-tuple-element.38.q_ref, bf16[8192,256]{1,0:T(8,128)(2,1)} %bitcast.116, s32[2,1,256]{2,1,0:T(1,128)} %broadcast_in_dim.68.lo_ref, ...), custom_call_target="tpu_custom_call" | custom-call | flops 24999999488 | bytes 12582912 | tf_op jit(solution)/shard_map/attend_backward/pallas_call | solution.py:803
  514.0 1.2 select_bitcast_fusion.1
  515.9 40.5 %collective-permute-start.3 = (bf16[256,768]{1,0:T(8,128)(2,1)S(1)}, bf16[256,768]{1,0:T(8,128)(2,1)S(1)}, u32[]{:S(2)}, u32[]{:S(2)}) collective-permute-start(bf16[256,768]{1,0:T(8,128)(2,1)S(1)} %get-tuple-element.129), channel_id=1, source_target_pairs={{2,0},{3,1},{6,2},{7,3},{10,4},{11,5},{14,6},{15,7},{18,8},{19,9},... | collective-permute-start | bytes 1179656 | tf_op jit(solution)/shard_map/ppermute | solution.py:1387
  556.5 43.2 %scatter_keys.1.dkv_ref = f32[512,256]{1,0:T(8,128)} custom-call(bf16[16,512,256]{2,1,0:T(8,128)(2,1)} %bitcast.99), custom_call_target="tpu_custom_call" | custom-call | tf_op jit(solution)/shard_map/scatter_keys/pallas_call | solution.py:509
  601.4 3.7 fusion.11
  605.2 1.7 copy-done.7
  607.9 3.5 convolution_convert_fusion
  611.4 1.5 concatenate.101
  612.8 5.0 convolution_convert_fusion.5
  618.6 13.9 %concatenate.92.part_ref = bf16[16,96,2688]{2,1,0:T(8,128)(2,1)} concatenate(bf16[16,96,1024]{2,1,0:T(8,128)(2,1)} %bitcast.100, bf16[16,96,1]{2,1,0:T(8,128)(2,1)} %concatenate.101, bf16[16,96,1]{2,1,0:T(8,128)(2,1)} %concatenate.102, bf16[16,96,8]{2,1,0:T(8,128)(2,1)} %bitcast.111, bf16[16,96,118]{2,1,0:T(8,128)(2,1)} %broadcast_in_dim.69, bf16[16,96,1536]{2,1,0:T(8,128)(2,1)} %bitcast.87), dimensions={2} | concatenate | bytes 16515072 | tf_op jit(solution)/shard_map/concatenate | solution.py:1580
  632.5 2.0 fusion.16
  634.5 2.6 fusion.20
  637.1 114.5 %closing.1 = (f32[96,2688]{1,0:T(8,128)}, bf16[96,2688]{1,0:T(8,128)(2,1)}, bf16[8,144,1536]{2,1,0:T(8,128)(2,1)}) custom-call(bf16[16,96,2688]{2,1,0:T(8,128)(2,1)} %concatenate.92.part_ref, bf16[4,144,1536]{2,1,0:T(8,128)(2,1)} %bitcast.110), custom_call_target="tpu_custom_call" | custom-call | tf_op jit(solution)/shard_map/closing/pallas_call | solution.py:554
  754.7 4.5 fusion.56
  759.1 1.7 slice.167
  (163 shorter events, 34.2 us)
Async XLA Ops:
  7.2 6.4 copy-start
  7.2 404.5 %reduce-scatter.3.cloned.1.call-start = ((), (), s32[]{:S(2)}) async-start(), calls=%async_computation.2 | async-start | bytes 7077888 | tf_op jit(solution)/shard_map/reduce_scatter | solution.py:1522
  11.3 9.7 %copy-start.23 = (s32[2,256]{1,0:T(2,128)}, s32[2,256]{1,0:T(2,128)S(1)}, u32[]{:S(2)}) copy-start(s32[2,256]{1,0:T(2,128)S(1)} %iota_add_fusion) | copy-start | bytes 6148
  241.6 9.5 %slice-start = ((s8[6291456]{0:T(1024)(128)(4,1)}), s8[4194304]{0:T(1024)(128)(4,1)S(1)}, s32[]{:S(2)}) async-start(s8[6291456]{0:T(1024)(128)(4,1)} %bitcast.84), calls=%async_computation.4 | async-start | bytes 8388608
  242.9 8.3 %slice-start.1 = ((s8[6291456]{0:T(1024)(128)(4,1)}), s8[2097152]{0:T(1024)(128)(4,1)S(1)}, s32[]{:S(2)}) async-start(s8[6291456]{0:T(1024)(128)(4,1)} %bitcast.84), calls=%async_computation.5 | async-start | bytes 4194304
  251.2 7.5 slice-start.2
  254.3 4.4 slice-start.3
  258.6 7.3 copy-start.9
  258.7 3.4 copy-start.18
  260.1 20.5 %copy-start.5 = (bf16[8,192,1536]{2,1,0:T(8,128)(2,1)}, bf16[8,192,1536]{2,1,0:T(8,128)(2,1)S(1)}, u32[]{:S(2)}) copy-start(bf16[8,192,1536]{2,1,0:T(8,128)(2,1)S(1)} %convolution_convert_fusion.3) | copy-start | bytes 14155780
  262.1 3.9 copy-start.16
  266.0 14.6 %copy-start.29 = (f32[1536,768]{1,0:T(8,128)}, f32[1536,768]{1,0:T(8,128)S(1)}, u32[]{:S(2)}) copy-start(f32[1536,768]{1,0:T(8,128)S(1)} %fusion.59) | copy-start | bytes 14155780
  266.0 14.5 %copy-start.15 = (bf16[16,48,1536]{2,1,0:T(8,128)(2,1)S(1)}, bf16[16,48,1536]{2,1,0:T(8,128)(2,1)}, u32[]{:S(2)}) copy-start(bf16[16,48,1536]{2,1,0:T(8,128)(2,1)} %slice.116) | copy-start | bytes 7077892
  280.5 6.5 copy-start.26
  306.0 331.2 %reduce-scatter.5.cloned.1.call-start = ((), (), s32[]{:S(2)}) async-start(), calls=%async_computation.3 | async-start | bytes 8847360 | tf_op jit(solution)/shard_map/reduce_scatter | solution.py:1523
  306.0 3.3 copy-start.27
  309.3 17.6 %slice-start.4 = ((s8[4718592]{0:T(1024)(128)(4,1)}), s8[4194304]{0:T(1024)(128)(4,1)S(1)}, s32[]{:S(2)}) async-start(s8[4718592]{0:T(1024)(128)(4,1)} %bitcast.93), calls=%async_computation.8 | async-start | bytes 8388608
  316.5 10.4 %slice-start.5 = ((s8[4718592]{0:T(1024)(128)(4,1)}), s8[524288]{0:T(1024)(128)(4,1)S(1)}, s32[]{:S(2)}) async-start(s8[4718592]{0:T(1024)(128)(4,1)} %bitcast.93), calls=%async_computation.9 | async-start | bytes 1048576
  326.9 4.3 copy-start.28
  326.9 4.3 copy-start.30
  338.9 2.1 copy-start.6
  343.3 10.1 %copy-start.17 = (bf16[16,96,768]{2,1,0:T(8,128)(2,1)S(1)}, bf16[16,96,768]{2,1,0:T(8,128)(2,1)}, u32[]{:S(2)}) copy-start(bf16[16,96,768]{2,1,0:T(8,128)(2,1)} %get-tuple-element.115) | copy-start | bytes 7077892
  343.3 10.0 %copy-start.31 = (bf16[1536,768]{1,0:T(8,128)(2,1)S(1)}, bf16[1536,768]{1,0:T(8,128)(2,1)}, u32[]{:S(2)}) copy-start(bf16[1536,768]{1,0:T(8,128)(2,1)} %get-tuple-element.112) | copy-start | bytes 7077892
  365.1 40.0 %copy-start.24 = (s32[2,256]{1,0:T(2,128)S(1)}, s32[2,256]{1,0:T(2,128)}, u32[]{:S(2)}) copy-start(s32[2,256]{1,0:T(2,128)} %copy-done.23) | copy-start | bytes 6148
  365.1 40.0 %copy-start.25 = (s32[10]{0:T(128)S(1)}, s32[10]{0:T(128)}, u32[]{:S(2)}) copy-start(s32[10]{0:T(128)} %param.15) | copy-start | bytes 124
  365.1 41.4 %copy-start.19 = (bf16[512,1536]{1,0:T(8,128)(2,1)S(1)}, bf16[512,1536]{1,0:T(8,128)(2,1)}, u32[]{:S(2)}) copy-start(bf16[512,1536]{1,0:T(8,128)(2,1)} %get-tuple-element.47) | copy-start | bytes 4718596
  415.0 192.9 %copy-start.10 = (f32[256,1536]{1,0:T(8,128)}, f32[256,1536]{1,0:T(8,128)S(1)}, u32[]{:S(2)}) copy-start(f32[256,1536]{1,0:T(8,128)S(1)} %get-tuple-element.124) | copy-start | bytes 4718596
  415.0 12.8 %copy-start.13 = (bf16[256,1536]{1,0:T(8,128)(2,1)S(1)}, bf16[256,1536]{1,0:T(8,128)(2,1)}, u32[]{:S(2)}) copy-start(bf16[256,1536]{1,0:T(8,128)(2,1)} %st_ref.1) | copy-start | bytes 2359300
  420.2 7.7 %collective-permute-start = (bf16[256,768]{1,0:T(8,128)(2,1)}, bf16[256,768]{1,0:T(8,128)(2,1)S(1)}, u32[]{:S(2)}, u32[]{:S(2)}) collective-permute-start(bf16[256,768]{1,0:T(8,128)(2,1)} %get-tuple-element.132), channel_id=1, source_target_pairs={{0,0},{31,1},{1,2},{30,3},{2,4},{29,5},{3,6},{28,7},{4,8},{27,9},{... | collective-permute-start | bytes 1179656 | tf_op jit(solution)/shard_map/ppermute | solution.py:1387
  421.9 41.5 %collective-permute-start.1 = (bf16[256,768]{1,0:T(8,128)(2,1)}, bf16[256,768]{1,0:T(8,128)(2,1)S(1)}, u32[]{:S(2)}, u32[]{:S(2)}) collective-permute-start(bf16[256,768]{1,0:T(8,128)(2,1)} %get-tuple-element.133), channel_id=1, source_target_pairs={{31,0},{0,1},{30,2},{1,3},{29,4},{2,5},{28,6},{3,7},{27,8},{4,9},{... | collective-permute-start | bytes 1179656 | tf_op jit(solution)/shard_map/ppermute | solution.py:1387
  464.4 92.0 %copy-start.22 = (bf16[2,256,768]{2,1,0:T(8,128)(2,1)S(1)}, bf16[2,256,768]{2,1,0:T(8,128)(2,1)}, u32[]{:S(2)}) copy-start(bf16[2,256,768]{2,1,0:T(8,128)(2,1)} %get-tuple-element.48) | copy-start | bytes 2359300
  514.0 85.9 %copy-start.2 = (f32[512,128]{1,0:T(8,128)S(1)}, f32[512,128]{1,0:T(8,128)}, u32[]{:S(2)}) copy-start(f32[512,128]{1,0:T(8,128)} %get-tuple-element.153.c_ref) | copy-start | bytes 786436
  514.0 85.9 %copy-start.3 = (f32[512,128]{1,0:T(8,128)S(1)}, f32[512,128]{1,0:T(8,128)}, u32[]{:S(2)}) copy-start(f32[512,128]{1,0:T(8,128)} %get-tuple-element.154.n_ref) | copy-start | bytes 786436
  515.2 84.5 %collective-permute-start.2 = (bf16[256,768]{1,0:T(8,128)(2,1)S(1)}, bf16[256,768]{1,0:T(8,128)(2,1)S(1)}, u32[]{:S(2)}, u32[]{:S(2)}) collective-permute-start(bf16[256,768]{1,0:T(8,128)(2,1)S(1)} %get-tuple-element.128), channel_id=1, source_target_pairs={{0,0},{1,1},{4,2},{5,3},{8,4},{9,5},{12,6},{13,7},{16,8},{17,9},{2... | collective-permute-start | bytes 1179656 | tf_op jit(solution)/shard_map/ppermute | solution.py:1387
  515.9 83.9 %collective-permute-start.3 = (bf16[256,768]{1,0:T(8,128)(2,1)S(1)}, bf16[256,768]{1,0:T(8,128)(2,1)S(1)}, u32[]{:S(2)}, u32[]{:S(2)}) collective-permute-start(bf16[256,768]{1,0:T(8,128)(2,1)S(1)} %get-tuple-element.129), channel_id=1, source_target_pairs={{2,0},{3,1},{6,2},{7,3},{10,4},{11,5},{14,6},{15,7},{18,8},{19,9},... | collective-permute-start | bytes 1179656 | tf_op jit(solution)/shard_map/ppermute | solution.py:1387
  556.5 44.9 %copy-start.20 = (bf16[512,1536]{1,0:T(8,128)(2,1)S(1)}, bf16[512,1536]{1,0:T(8,128)(2,1)}, u32[]{:S(2)}) copy-start(bf16[512,1536]{1,0:T(8,128)(2,1)} %get-tuple-element.47) | copy-start | bytes 4718596
  599.8 1.0 copy-start.4
  605.1 1.7 copy-start.7
  607.8 24.6 %collective-permute-start.4 = (bf16[256,1536]{1,0:T(8,128)(2,1)}, bf16[256,1536]{1,0:T(8,128)(2,1)}, u32[]{:S(2)}, u32[]{:S(2)}) collective-permute-start(bf16[256,1536]{1,0:T(8,128)(2,1)} %select_convert_fusion), channel_id=1, source_target_pairs={{0,1},{1,0},{2,3},{3,2},{4,5},{5,4},{6,7},{7,6},{8,9},{9,8},{10,11... | collective-permute-start | bytes 2359304 | tf_op jit(solution)/shard_map/ppermute | solution.py:1565
  618.6 13.9 %copy-start.8 = (f32[512,1536]{1,0:T(8,128)S(1)}, f32[512,1536]{1,0:T(8,128)}, u32[]{:S(2)}) copy-start(f32[512,1536]{1,0:T(8,128)} %copy-done.7) | copy-start | bytes 9437188
  632.5 2.1 copy-start.11
  632.5 2.1 copy-start.14
  754.6 4.5 copy-start.12
  754.6 6.2 copy-start.21
  754.7 10.7 %copy-start.1 = (bf16[96,1536]{1,0:T(8,128)(2,1)S(1)}, bf16[96,1536]{1,0:T(8,128)(2,1)}, u32[]{:S(2)}) copy-start(bf16[96,1536]{1,0:T(8,128)(2,1)} %param.18) | copy-start | bytes 884740
Sparse Core Ops, SparseCore 0:
  306.1 66.9 reduce-scatter.2
  375.5 138.1 reduce-scatter.4

commit v3 on v2

--- a/solution.py
+++ b/solution.py
@@ -213,143 +213,6 @@
     return pltpu.CompilerParams(
         collective_id=cid, has_side_effects=True, vmem_limit_bytes=limit
     )
-
-
-def opening(pack, moe, stream, chosen, depth):
-    rows = pack.shape[0]
-
-    def kernel(pack_ref, moe_ref, st_ref, ch_ref, pack_out, moe_out, st_out, ch_out, *sems):
-        net = Net(depth)
-        sends = Sends()
-        gather = ShardGather(net, sends, pack_ref, pack_out, sems[:6])
-        sm, rm, sy, ry, sp, rp, own = sems[6:]
-        locals_ = [
-            pltpu.make_async_copy(pack_ref, gather.slot(0, net.i), own.at[0]),
-            pltpu.make_async_copy(moe_ref.at[net.i * SEQ + net.y], moe_out.at[net.i], own.at[1]),
-            pltpu.make_async_copy(st_ref, st_out.at[net.y], own.at[2]),
-            pltpu.make_async_copy(ch_ref, ch_out.at[net.i * SEQ + net.y], own.at[3]),
-        ]
-        greet(net.zpeers() + net.plane())
-        gather.begin()
-        sends.start(st_ref, st_out.at[net.y], sy.at[0], ry.at[0], net.yp)
-        for n, device in enumerate(net.plane()):
-            sends.start(ch_ref, ch_out.at[net.i * SEQ + net.y], sp.at[n], rp.at[n], device)
-        for di in range(1, INNER):
-            other = lax.rem(net.i + di, INNER)
-            sends.start(
-                moe_ref.at[other * SEQ + net.y],
-                moe_out.at[net.i],
-                sm.at[di - 1],
-                rm.at[di - 1],
-                net.dev(i=other),
-            )
-        for copy in locals_:
-            copy.start()
-        gather.end()
-        arrived(st_out.at[1 - net.y], sy.at[0], ry.at[0], net.yp)
-        n = 0
-        for di in range(INNER):
-            for dy in range(SEQ):
-                if di or dy:
-                    frm = lax.rem(net.i - di + INNER, INNER) * SEQ + lax.rem(net.y + dy, SEQ)
-                    arrived(ch_out.at[frm], sp.at[n], rp.at[n], net.yp)
-                    n += 1
-        for di in range(1, INNER):
-            frm = lax.rem(net.i - di + INNER, INNER)
-            arrived(moe_out.at[frm], sm.at[di - 1], rm.at[di - 1], net.yp)
-        sends.finish()
-        for copy in locals_:
-            copy.wait()
-
-    return pl.pallas_call(
-        kernel,
-        out_shape=(
-            jax.ShapeDtypeStruct((depth * INNER,) + pack.shape, BF),
-            jax.ShapeDtypeStruct((INNER,) + moe.shape[1:], BF),
-            jax.ShapeDtypeStruct((SEQ,) + stream.shape, BF),
-            jax.ShapeDtypeStruct((E,) + chosen.shape, F32),
-        ),
-        in_specs=[hbm()] * 4,
-        out_specs=(hbm(),) * 4,
-        scratch_shapes=ShardGather.sems(depth) + dma_sems(3, 3, 1, 1, E - 1, E - 1, 4),
-        compiler_params=comm_params(1),
-        name="opening",
-    )(pack, moe, stream, chosen)
-
-
-def gather_keys(kv, depth):
-    def kernel(src, out, *sems):
-        net = Net(depth)
-        sends = Sends()
-        gather = ShardGather(net, sends, src, out, sems[:6])
-        own = pltpu.make_async_copy(src, gather.slot(0, net.i), sems[6].at[0])
-        greet(net.zpeers() + [net.xp, net.cp])
-        gather.begin()
-        own.start()
-        gather.end()
-        sends.finish()
-        own.wait()
-
-    return pl.pallas_call(
-        kernel,
-        out_shape=jax.ShapeDtypeStruct((depth * INNER,) + kv.shape, BF),
-        in_specs=[hbm()],
-        out_specs=hbm(),
-        scratch_shapes=ShardGather.sems(depth) + dma_sems(1),
-        compiler_params=comm_params(2),
-        name="gather_keys",
-    )(kv)
-
-
-def gather_plane(rows, depth, cid):
-    half = rows.shape[0] // 2
-
-    def kernel(src, out, sx, rx, sy, ry, sc, rc, own):
-        net = Net(depth)
-        sends = Sends()
-
-        def place(i, y):
-            return i * SEQ + y
-
-        xi = lax.rem(net.i + 2, INNER)
-        me, xb = place(net.i, net.y), place(xi, net.y)
-        yb, db = place(net.i, 1 - net.y), place(xi, 1 - net.y)
-        lo, hi = pl.ds(0, half), pl.ds(half, half)
-        mine = pltpu.make_async_copy(src, out.at[me], own.at[0])
-        greet([net.xp, net.yp, net.cp])
-        sends.start(src, out.at[me], sx.at[0], rx.at[0], net.xp)
-        sends.start(src, out.at[me], sy.at[0], ry.at[0], net.yp)
-        sends.start(src, out.at[me], sc.at[0], rc.at[0], net.cp)
-        mine.start()
-        arrived(out.at[yb], sy.at[0], ry.at[0], net.yp)
-        sends.start(out.at[yb, lo], out.at[yb, lo], sx.at[1], rx.at[1], net.xp)
-        sends.start(out.at[yb], out.at[yb], sc.at[1], rc.at[1], net.cp)
-        arrived(out.at[xb], sx.at[0], rx.at[0], net.xp)
-        sends.start(out.at[xb, hi], out.at[xb, hi], sy.at[1], ry.at[1], net.yp)
-        sends.start(out.at[xb], out.at[xb], sc.at[2], rc.at[2], net.cp)
-        arrived(out.at[db, lo], sx.at[1], rx.at[1], net.xp)
-        sends.start(out.at[db, lo], out.at[db, lo], sc.at[3], rc.at[3], net.cp)
-        arrived(out.at[db, hi], sy.at[1], ry.at[1], net.yp)
-        sends.start(out.at[db, hi], out.at[db, hi], sc.at[4], rc.at[4], net.cp)
-        ci = net.i + 1 - 2 * net.core
-        cx = lax.rem(ci + 2, INNER)
-        arrived(out.at[place(ci, net.y)], sc.at[0], rc.at[0], net.cp)
-        arrived(out.at[place(ci, 1 - net.y)], sc.at[1], rc.at[1], net.cp)
-        arrived(out.at[place(cx, net.y)], sc.at[2], rc.at[2], net.cp)
-        arrived(out.at[place(cx, 1 - net.y), lo], sc.at[3], rc.at[3], net.cp)
-        arrived(out.at[place(cx, 1 - net.y), hi], sc.at[4], rc.at[4], net.cp)
-        sends.finish()
-        mine.wait()
-
-    return pl.pallas_call(
-        kernel,
-        out_shape=jax.ShapeDtypeStruct((E,) + rows.shape, BF),
-        in_specs=[hbm()],
-        out_specs=hbm(),
-        scratch_shapes=dma_sems(2, 2, 2, 2, 5, 5, 1),
-        compiler_params=comm_params(cid),
-        name="gather_plane",
-    )(rows)
 
 
 def add_into(dst, sources, rows, chunk):
@@ -494,7 +357,7 @@
                 add_into(out, terms, self.rows, self.chunk)
 
 
-def scatter_keys(part, depth):
+def scatter_keys(part, depth, cid):
     rows, cols = part.shape[1:]
 
     def kernel(part_ref, out, *scratch):
@@ -512,203 +375,13 @@
         in_specs=[vmem()],
         out_specs=vmem(),
         scratch_shapes=ShardScatter.scratch(depth, rows, cols),
-        compiler_params=comm_params(5),
+        compiler_params=comm_params(cid),
         name="scatter_keys",
     )(part)
 
 
-def closing(part, moe, depth):
-    rows, cols = part.shape[1:]
-
-    def kernel(part_ref, moe_ref, own_out, pair_out, moe_out, low, sm, rm, sy, ry, ls, *scratch):
-        net = Net(depth)
-        sends = Sends()
-        me = net.i * SEQ + net.y
-        mine = pltpu.make_async_copy(moe_ref.at[net.i], moe_out.at[me], ls.at[0])
-        greet(net.zpeers() + net.plane())
-        work = ShardScatter(net, sends, part_ref, scratch)
-        work.begin()
-        n = 0
-        for di in range(INNER):
-            for dy in range(SEQ):
-                if di or dy:
-                    i = lax.rem(net.i + di, INNER)
-                    device = net.dev(i=i, y=lax.rem(net.y + dy, SEQ))
-                    sends.start(moe_ref.at[i], moe_out.at[me], sm.at[n], rm.at[n], device)
-                    n += 1
-        mine.start()
-        work.end(own_out)
-        low[...] = own_out[...].astype(BF)
-        sends.start(low, pair_out, sy.at[0], ry.at[0], net.yp)
-        n = 0
-        for di in range(INNER):
-            for dy in range(SEQ):
-                if di or dy:
-                    frm = lax.rem(net.i - di + INNER, INNER) * SEQ + lax.rem(net.y + dy, SEQ)
-                    arrived(moe_out.at[frm], sm.at[n], rm.at[n], net.yp)
-                    n += 1
-        arrived(pair_out, sy.at[0], ry.at[0], net.yp)
-        sends.finish()
-        mine.wait()
-
-    return pl.pallas_call(
-        kernel,
-        out_shape=(
-            jax.ShapeDtypeStruct((rows, cols), F32),
-            jax.ShapeDtypeStruct((rows, cols), BF),
-            jax.ShapeDtypeStruct((E,) + moe.shape[1:], BF),
-        ),
-        in_specs=[vmem(), hbm()],
-        out_specs=(vmem(), vmem(), hbm()),
-        scratch_shapes=[pltpu.VMEM((rows, cols), BF)]
-        + dma_sems(E - 1, E - 1, 1, 1, 1)
-        + ShardScatter.scratch(depth, rows, cols),
-        compiler_params=comm_params(6),
-        name="closing",
-    )(part, moe)
-
-
 def turn(values, cosine, sine):
     return values * cosine + pltpu.roll(values, HEAD // 2, 1) * sine
-
-
-def project(stream, gain, weights, cosine, sine):
-    rows = stream.shape[0]
-    wide = 2 * HEAD
-
-    def kernel(s_ref, g_ref, w_ref, c_ref, n_ref, h_ref, o_ref):
-        n = pl.program_id(0)
-
-        @pl.when(n == 0)
-        def _():
-            x = s_ref[...].astype(F32)
-            scale = lax.rsqrt(jnp.mean(x * x, axis=-1, keepdims=True) + EPS)
-            h_ref[...] = (x * scale * g_ref[...]).astype(BF)
-
-        r = dot(h_ref[...], w_ref[...])
-        first = turn(r[:, :HEAD], c_ref[...], n_ref[...])
-
-        @pl.when(n < 3)
-        def _():
-            o_ref[:, :HEAD] = (first * (SCALE * LOG2E)).astype(BF)
-            second = turn(r[:, HEAD:], c_ref[...], n_ref[...])
-            o_ref[:, HEAD:] = (second * (SCALE * LOG2E)).astype(BF)
-
-        @pl.when(n == 3)
-        def _():
-            o_ref[:, :HEAD] = first.astype(BF)
-            o_ref[:, HEAD:] = r[:, HEAD:].astype(BF)
-
-    fixed = lambda shape: pl.BlockSpec(shape, lambda n: (0, 0))
-    return pl.pallas_call(
-        kernel,
-        grid=(QKV // wide,),
-        in_specs=[
-            fixed((rows, WIDTH)),
-            fixed((1, WIDTH)),
-            pl.BlockSpec((WIDTH, wide), lambda n: (0, n)),
-            fixed((rows, HEAD)),
-            fixed((rows, HEAD)),
-        ],
-        out_specs=(fixed((rows, WIDTH)), pl.BlockSpec((rows, wide), lambda n: (0, n))),
-        out_shape=(
-            jax.ShapeDtypeStruct((rows, WIDTH), BF),
-            jax.ShapeDtypeStruct((rows, QKV), BF),
-        ),
-        compiler_params=pltpu.CompilerParams(vmem_limit_bytes=32 << 20),
-        name="project",
-    )(stream, gain, weights, cosine, sine)
-
-
-def unturn(dq, dkv, cosine, sine):
-    rows = dq.shape[0]
-
-    def kernel(dq_ref, dkv_ref, c_ref, n_ref, o_ref):
-        c, s = c_ref[...], -n_ref[...]
-        for h in range(GROUP):
-            at = slice(h * HEAD, (h + 1) * HEAD)
-            o_ref[:, at] = turn(dq_ref[:, at].astype(F32), c, s).astype(BF)
-        dk = dkv_ref[:, :HEAD].astype(BF).astype(F32)
-        o_ref[:, QCOLS : QCOLS + HEAD] = turn(dk, c, s).astype(BF)
-        o_ref[:, QCOLS + HEAD :] = dkv_ref[:, HEAD:].astype(BF)
-
-    return pl.pallas_call(
-        kernel,
-        in_specs=[vmem()] * 4,
-        out_specs=vmem(),
-        out_shape=jax.ShapeDtypeStruct((rows, QKV), BF),
-        compiler_params=pltpu.CompilerParams(vmem_limit_bytes=32 << 20),
-        name="unturn",
-    )(dq, dkv, cosine, sine)
-
-
-def attend_forward(q, kv, lo, info, tile=512):
-    block = q.shape[1]
-
-    def kernel(info_ref, q_ref, kv_ref, lo_ref, o_ref, m_ref, l_ref, acc, top, total):
-        for j in range(2):
-            base = info_ref[j] * block
-            first = info_ref[2 + j] // tile
-            last = (base + block - 1) // tile
-            acc[...] = jnp.zeros_like(acc)
-            top[...] = jnp.full_like(top, NEG)
-            total[...] = jnp.zeros_like(total)
-
-            def step(t, masked):
-                start = pl.multiple_of(t * tile, tile)
-                k = kv_ref[pl.ds(start, tile), :HEAD]
-                vt = kv_ref[pl.ds(start, tile), HEAD:].T
-                if masked:
-                    key = start + lax.broadcasted_iota(jnp.int32, (tile, block), 0)
-                    query = base + lax.broadcasted_iota(jnp.int32, (tile, block), 1)
-                    ok = (key <= query) & (key >= lo_ref[j])
-                for h in range(GROUP):
-                    s = dot(k, q_ref[j, :, h * HEAD : (h + 1) * HEAD], NT)
-                    if masked:
-                        s = jnp.where(ok, s, NEG)
-                    m0 = top[h : h + 1, :]
-                    m1 = jnp.maximum(m0, jnp.max(s, axis=0, keepdims=True))
-                    p = jnp.exp2(s - m1)
-                    f = jnp.exp2(m0 - m1)
-                    top[h : h + 1, :] = m1
-                    total[h : h + 1, :] = total[h : h + 1, :] * f + jnp.sum(
-                        p, axis=0, keepdims=True
-                    )
-                    acc[h] = acc[h] * f + dot(vt, p.astype(BF))
-
-            free_from = jnp.minimum((info_ref[4 + j] + tile - 1) // tile, last + 1)
-            free_to = jnp.maximum(base // tile, free_from)
-
-            def run(a, b, masked):
-                lax.fori_loop(a, b, lambda t, c: (step(t, masked), c)[1], 0)
-
-            run(first, free_from, True)
-            run(free_from, free_to, False)
-            run(jnp.maximum(free_to, first), last + 1, True)
-            for h in range(GROUP):
-                o_ref[j, :, h * HEAD : (h + 1) * HEAD] = (
-                    (acc[h] / total[h : h + 1, :]).T.astype(BF)
-                )
-            m_ref[j] = top[...]
-            l_ref[j] = total[...]
-
-    stat = jax.ShapeDtypeStruct((2, 8, block), F32)
-    return pl.pallas_call(
-        kernel,
-        out_shape=(jax.ShapeDtypeStruct(q.shape, BF), stat, stat),
-        in_specs=[smem()] + [vmem()] * 3,
-        out_specs=(vmem(),) * 3,
-        scratch_shapes=[
-            pltpu.VMEM((GROUP, HEAD, block), F32),
-            pltpu.VMEM((8, block), F32),
-            pltpu.VMEM((8, block), F32),
-        ],
-        compiler_params=pltpu.CompilerParams(vmem_limit_bytes=48 << 20),
-        cost_estimate=pl.CostEstimate(
-            flops=int(1e10), bytes_accessed=6 << 20, transcendentals=13 << 20
-        ),
-        name="attend_forward",
-    )(info, q, kv, lo)
 
 
 def attend_backward(q, kv, lo, info, m, l, dob, ob, tile=512):
@@ -1345,6 +1018,383 @@
         compiler_params=comm_params(7, 60 << 20),
         name="front",
     )(stream, pack, moe, chosen, cosine, sine, w_out, out_grad, qseg, starts)
+
+
+class Tally:
+    def __init__(self, net, part, rows, scratch):
+        self.net, self.part, self.rows = net, part, rows
+        self.bc, self.sx, self.bx, self.sz, self.bz = scratch[:5]
+        self.ssc, self.rsc, self.ssx, self.rsx, self.ssz, self.rsz = scratch[5:]
+        self.chunk = chunk_of(rows)
+
+    def number(self, dz, fx, core):
+        x = jnp.where(fx == 1, 1 - self.net.x, self.net.x)
+        return lax.rem(self.net.z + dz, self.net.depth) * INNER + x * 2 + core
+
+    def core_copy(self, dz, fx):
+        net, n = self.net, dz * 2 + fx
+        src = self.part.at[self.number(dz, fx, 1 - net.core)]
+        return remote(src, self.bc.at[n], self.ssc.at[n], self.rsc.at[n], net.cp)
+
+    def x_copy(self, dz):
+        return remote(
+            self.sx.at[dz], self.bx.at[dz], self.ssx.at[dz], self.rsx.at[dz], self.net.xp
+        )
+
+    def z_copy(self, dz):
+        n = dz - 1
+        device = self.net.dev(z=lax.rem(self.net.z + dz, self.net.depth))
+        return remote(self.sz.at[n], self.bz.at[n], self.ssz.at[n], self.rsz.at[n], device)
+
+    def terms(self, dz, fx):
+        n = dz * 2 + fx
+        arrived(self.bc.at[n], self.ssc.at[n], self.rsc.at[n], self.net.cp)
+        return [self.part.at[self.number(dz, fx, self.net.core)], self.bc.at[n]]
+
+    def x_stage(self, dz):
+        add_into(self.sx.at[dz], self.terms(dz, 1), self.rows, self.chunk)
+        self.x_copy(dz).start()
+
+    def x_terms(self, dz):
+        terms = self.terms(dz, 0)
+        arrived(self.bx.at[dz], self.ssx.at[dz], self.rsx.at[dz], self.net.xp)
+        return terms + [self.bx.at[dz]]
+
+    def z_stage(self, dz):
+        add_into(self.sz.at[dz - 1], self.x_terms(dz), self.rows, self.chunk)
+        self.z_copy(dz).start()
+
+    def final(self, out):
+        terms = self.x_terms(0)
+        for n in range(self.net.depth - 1):
+            arrived(self.bz.at[n], self.ssz.at[n], self.rsz.at[n], self.net.xp)
+            terms.append(self.bz.at[n])
+        add_into(out, terms, self.rows, self.chunk)
+
+    def finish(self):
+        for dz in range(self.net.depth):
+            for fx in range(2):
+                self.core_copy(dz, fx).wait_send()
+            self.x_copy(dz).wait_send()
+            if dz:
+                self.z_copy(dz).wait_send()
+
+    def far(self):
+        return [d for d in range(1, self.net.depth)] + [0]
+
+    def begin(self):
+        for dz in self.far():
+            for fx in (1, 0):
+                self.core_copy(dz, fx).start()
+
+    def far_stages(self):
+        for dz in self.far():
+            self.x_stage(dz)
+
+    def near_stages(self):
+        for dz in self.far()[:-1]:
+            self.z_stage(dz)
+
+
+def backward(q, kv, qseg, starts, m, l, ob, mixed, dx1, out_w, part_rows, depth):
+    block = q.shape[1]
+    rows = kv.shape[1]
+    shards = depth * INNER
+
+    def kernel(
+        q_ref, kv_ref, qs_ref, sg_ref, m_ref, l_ref, ob_ref, mix_ref, dx_ref, wf_ref,
+        dq_out, dkv_out, own_out,
+        dob, do_ref, da, dl, acc, dqs, dkv, wpart, so, ro, sq, rq, *scratch,
+    ):
+        net = Net(depth)
+        mirror = Mirror(net)
+        keys = Tally(net, dkv, rows, scratch[:11])
+        outs = Tally(net, wpart, part_rows, scratch[11:])
+        heads = [mirror.heads_out(k) for k in range(2)]
+        backs = [mirror.rows_back(k) for k in range(2)]
+        barrier = pltpu.get_barrier_semaphore()
+        for device in net.zpeers() + [net.xp, net.cp]:
+            pl.semaphore_signal(barrier, inc=1, device_id=device, device_id_type=MESH)
+        count = depth - 1 + 2
+        for route, _ in heads + backs:
+            count = count + route.hello()
+        do_refs = [
+            lambda k=k: (dob.at[k], do_ref.at[heads[k][1]], so.at[k], ro.at[heads[k][1]])
+            for k in range(2)
+        ]
+        dq_refs = [
+            lambda k=k: (dqs.at[k], dq_out.at[backs[k][1]], sq.at[k], rq.at[backs[k][1]])
+            for k in range(2)
+        ]
+        dx = dx_ref[...]
+        for k in range(2):
+            dob[k] = dot(dx, wf_ref[k * QCOLS : (k + 1) * QCOLS, :], NT).astype(BF)
+        pl.semaphore_wait(barrier, count)
+        for k in range(2):
+            heads[k][0].send(do_refs[k])
+        wide = QCOLS // 2
+        for n in range(4):
+            cols = slice((n % 2) * wide, (n % 2 + 1) * wide)
+            grad = dot(mix_ref[n // 2, :, cols].T, dx).astype(BF)
+            for b in range(wide // part_rows):
+                wpart[n * (wide // part_rows) + b] = grad[b * part_rows : (b + 1) * part_rows]
+        outs.begin()
+        acc[...] = jnp.zeros_like(acc)
+        for k in range(2):
+            heads[k][0].arrive(lambda: (do_ref.at[k], so.at[k], ro.at[k]))
+        for j in range(2):
+            for h in range(GROUP):
+                c = slice(h * HEAD, (h + 1) * HEAD)
+                d = do_ref[j, :, c].astype(F32)
+                o = ob_ref[j, :, c].astype(F32)
+                inv = 1.0 / l_ref[j, h : h + 1, :]
+                da[j, h] = (d.T * inv).T.astype(BF)
+                dl[j, h : h + 1, :] = -jnp.sum((d * o).T, axis=0, keepdims=True) * inv
+        low, high = mirror.blocks()
+        bases = (low * block, high * block)
+
+        def piece(t, j, masked):
+            start = pl.multiple_of(t * rows, rows)
+            k = kv_ref[t, :, :HEAD]
+            v = kv_ref[t, :, HEAD:]
+            kt = k.T
+            k_seg = jnp.concatenate(
+                [k, seg_tile(start, rows, sg_ref[0:1, :], sg_ref[1:2, :])], axis=1
+            )
+            if masked:
+                key = start + lax.broadcasted_iota(jnp.int32, (rows, block), 0)
+                ok = key <= bases[j] + lax.broadcasted_iota(jnp.int32, (rows, block), 1)
+            dk = dv = None
+            for h in range(GROUP):
+                qh = q_ref[j, :, h * HEAD : (h + 1) * HEAD]
+                s = dot(k_seg, jnp.concatenate([qh, qs_ref[j]], axis=1), NT)
+                s = s - m_ref[j, h : h + 1, :]
+                if masked:
+                    s = jnp.where(ok, s, NEG)
+                p = jnp.exp2(s)
+                dah = da[j, h]
+                dvh = dot(p.astype(BF), dah)
+                dp = dot(v, dah, NT) + dl[j, h : h + 1, :]
+                ds = (p * dp).astype(BF)
+                dkh = dot(ds, qh)
+                acc[j, h] += dot(kt, ds)
+                dk = dkh if dk is None else dk + dkh
+                dv = dvh if dv is None else dv + dvh
+            return dk * LN2, dv
+
+        def tile(u, carry):
+            g, r = lax.div(u, INNER), lax.rem(u, INNER)
+            dz = lax.rem(g + 1, depth)
+            fx = 1 - lax.div(r, 2)
+            other = lax.rem(r, 2) == 0
+            t = keys.number(dz, fx, jnp.where(other, 1 - net.core, net.core))
+
+            def put(j, masked):
+                dk, dv = piece(t, j, masked)
+                if j == 0:
+                    dk = dk + dkv[t, :, :HEAD].astype(F32)
+                    dv = dv + dkv[t, :, HEAD:].astype(F32)
+                dkv[t, :, :HEAD] = dk.astype(BF)
+                dkv[t, :, HEAD:] = dv.astype(BF)
+
+            for j in (1, 0):
+                live = t * rows <= bases[j] + block - 1
+                free = t * rows + rows - 1 <= bases[j]
+                if j == 1:
+
+                    @pl.when(jnp.logical_not(live))
+                    def _():
+                        dkv[t] = jnp.zeros((rows, 2 * HEAD), BF)
+
+                @pl.when(live & free)
+                def _():
+                    put(j, False)
+
+                @pl.when(live & jnp.logical_not(free))
+                def _():
+                    put(j, True)
+
+            @pl.when(other)
+            def _():
+                keys.core_copy(dz, fx).start()
+
+            @pl.when(r == INNER - 1)
+            def _():
+                keys.x_stage(dz)
+
+            @pl.when((r == INNER - 1) & (g > 0))
+            def _():
+                keys.z_stage(g)
+
+            @pl.when(u == 2)
+            def _():
+                outs.far_stages()
+
+            @pl.when(u == shards - INNER)
+            def _():
+                outs.near_stages()
+
+            return carry
+
+        lax.fori_loop(0, shards, tile, 0)
+        for j in range(2):
+            for h in range(GROUP):
+                dqs[j, :, h * HEAD : (h + 1) * HEAD] = (acc[j, h] * SCALE).T.astype(BF)
+        for k in range(2):
+            backs[k][0].send(dq_refs[k])
+        outs.final(own_out)
+        keys.final(dkv_out)
+        for k in range(2):
+            backs[k][0].arrive(lambda: (dq_out.at[k], sq.at[k], rq.at[k]))
+        for k in range(2):
+            heads[k][0].sent(do_refs[k])
+            backs[k][0].sent(dq_refs[k])
+        outs.finish()
+        keys.finish()
+
+    sds = jax.ShapeDtypeStruct
+    pair = (2, block, QCOLS)
+    return pl.pallas_call(
+        kernel,
+        out_shape=(
+            sds(pair, BF),
+            sds((rows, 2 * HEAD), F32),
+            sds((part_rows, WIDTH), F32),
+        ),
+        in_specs=[vmem()] * 10,
+        out_specs=(vmem(),) * 3,
+        scratch_shapes=[
+            pltpu.VMEM(pair, BF),
+            pltpu.VMEM(pair, BF),
+            pltpu.VMEM((2, GROUP, block, HEAD), BF),
+            pltpu.VMEM((2, 8, block), F32),
+            pltpu.VMEM((2, GROUP, HEAD, block), F32),
+            pltpu.VMEM(pair, BF),
+            pltpu.VMEM((shards, rows, 2 * HEAD), BF),
+            pltpu.VMEM((shards, part_rows, WIDTH), BF),
+        ]
+        + dma_sems(2, 2, 2, 2)
+        + ShardScatter.scratch(depth, rows, 2 * HEAD)
+        + ShardScatter.scratch(depth, part_rows, WIDTH),
+        compiler_params=comm_params(8, 60 << 20),
+        name="backward",
+    )(q, kv, qseg, starts, m, l, ob, mixed, dx1, out_w)
+
+
+def finish_layer(dq, dkv, cosine, sine, h1, weights, pair, small, dx1, gain_a, out_own, moe, depth):
+    block = dx1.shape[0]
+    rows = pair.shape[0]
+    shards = depth * INNER
+    part_rows = out_own.shape[0]
+    wide = 384
+
+    def kernel(
+        dq_ref, dkv_ref, c_ref, n_ref, h1_ref, w_ref, s_ref, sm_ref, dx_ref, ga_ref, oo_ref, moe_ref,
+        sg_out, own_out, pair_out, pair_wo, moe_out,
+        raw, part, give, take, low, low_wo, sm, rm, sy, ry, ls, *scratch,
+    ):
+        net = Net(depth)
+        sends = Sends()
+        me = net.i * SEQ + net.y
+        mine = pltpu.make_async_copy(moe_ref.at[net.i], moe_out.at[me], ls.at[0])
+        work = Tally(net, part, part_rows, scratch)
+        barrier = pltpu.get_barrier_semaphore()
+        for device in net.zpeers() + net.plane():
+            pl.semaphore_signal(barrier, inc=1, device_id=device, device_id_type=MESH)
+        cos, sin = c_ref[...], -n_ref[...]
+        for k in range(2):
+            at = slice(k * block, (k + 1) * block)
+            for h in range(GROUP):
+                cols = slice(h * HEAD, (h + 1) * HEAD)
+                v = dq_ref[k, :, cols].astype(F32)
+                raw[at, cols] = turn(v, cos[at], sin[at]).astype(BF)
+        dk = dkv_ref[:, :HEAD].astype(BF).astype(F32)
+        raw[:, QCOLS : QCOLS + HEAD] = turn(dk, cos, sin).astype(BF)
+        raw[:, QCOLS + HEAD :] = dkv_ref[:, HEAD:].astype(BF)
+        pl.semaphore_wait(barrier, depth - 1 + E - 1)
+        low_wo[...] = oo_ref[...].astype(BF)
+        sends.start(low_wo, pair_wo, sy.at[1], ry.at[1], net.yp)
+
+        def half(y):
+            at = pl.ds(pl.multiple_of(y * block, block), block)
+            x = s_ref[at, :].astype(F32)
+            scale = lax.rsqrt(jnp.mean(x * x, axis=-1, keepdims=True) + EPS)
+            grad = dot(raw[at, :], w_ref[:, :QKV], NT)
+            return x * scale, scale, grad
+
+        normed, _, grad = half(1 - net.y)
+        give[...] = grad.astype(BF)
+        sends.start(give, take, sy.at[2], ry.at[2], net.yp)
+        gain_part = jnp.sum(grad * normed, axis=0, keepdims=True)
+        n = 0
+        for di in range(INNER):
+            for dy in range(SEQ):
+                if di or dy:
+                    i = lax.rem(net.i + di, INNER)
+                    device = net.dev(i=i, y=lax.rem(net.y + dy, SEQ))
+                    sends.start(moe_ref.at[i], moe_out.at[me], sm.at[n], rm.at[n], device)
+                    n += 1
+        mine.start()
+        normed, scale, grad = half(net.y)
+        gain_part = gain_part + jnp.sum(grad * normed, axis=0, keepdims=True)
+        lanes = lax.broadcasted_iota(jnp.int32, (EXTRA, WIDTH), 0)
+        extra = jnp.where(lanes == 0, gain_part, sm_ref[...]).T.astype(BF)
+        per = wide // part_rows
+        for c in range(WIDTH // wide):
+            g = dot(h1_ref[:, c * wide : (c + 1) * wide].T, raw[...]).astype(BF)
+            for b in range(per):
+                part[c * per + b, :, :QKV] = g[b * part_rows : (b + 1) * part_rows]
+                part[c * per + b, :, QKV:] = extra[
+                    c * wide + b * part_rows : c * wide + (b + 1) * part_rows
+                ]
+        work.begin()
+        work.far_stages()
+        arrived(take, sy.at[2], ry.at[2], net.yp)
+        inner = (grad + take[...].astype(F32)) * ga_ref[...]
+        pull = scale * (inner - normed * jnp.mean(inner * normed, axis=-1, keepdims=True))
+        sg_out[...] = (dx_ref[...] + pull).astype(BF)
+        work.near_stages()
+        work.final(own_out)
+        low[...] = own_out[...].astype(BF)
+        sends.start(low, pair_out, sy.at[0], ry.at[0], net.yp)
+        n = 0
+        for di in range(INNER):
+            for dy in range(SEQ):
+                if di or dy:
+                    frm = lax.rem(net.i - di + INNER, INNER) * SEQ + lax.rem(net.y + dy, SEQ)
+                    arrived(moe_out.at[frm], sm.at[n], rm.at[n], net.yp)
+                    n += 1
+        arrived(pair_wo, sy.at[1], ry.at[1], net.yp)
+        arrived(pair_out, sy.at[0], ry.at[0], net.yp)
+        sends.finish()
+        work.finish()
+        mine.wait()
+
+    sds = jax.ShapeDtypeStruct
+    return pl.pallas_call(
+        kernel,
+        out_shape=(
+            sds((block, WIDTH), BF),
+            sds((part_rows, FIRST), F32),
+            sds((part_rows, FIRST), BF),
+            sds((part_rows, WIDTH), BF),
+            sds((E,) + moe.shape[1:], BF),
+        ),
+        in_specs=[vmem()] * 11 + [hbm()],
+        out_specs=(vmem(),) * 4 + (hbm(),),
+        scratch_shapes=[
+            pltpu.VMEM((rows, QKV), BF),
+            pltpu.VMEM((shards, part_rows, FIRST), BF),
+            pltpu.VMEM((block, WIDTH), BF),
+            pltpu.VMEM((block, WIDTH), BF),
+            pltpu.VMEM((part_rows, FIRST), BF),
+            pltpu.VMEM((part_rows, WIDTH), BF),
+        ]
+        + dma_sems(E - 1, E - 1, 3, 3, 1)
+        + ShardScatter.scratch(depth, part_rows, FIRST),
+        compiler_params=comm_params(9, 60 << 20),
+        name="finish_layer",
+    )(dq, dkv, cosine, sine, h1, weights, pair, small, dx1, gain_a, out_own, moe)
 
 
 def rms_parts(x):
@@ -1452,13 +1502,35 @@
     return mixture, back_tok, grads
 
 
+def back_apart(zig, q, kv, lo, info, top, total, ob, mixed, dx1, out_w, part_rows, depth):
+    z, i, y = (lax.axis_index(a) for a in AXES)
+    shards, rows = kv.shape[:2]
+    shard = z * INNER + i
+    even, head_zero = lax.rem(shard, 2) == 0, y == 0
+    dob = dot(dx1, out_w, NT).astype(BF)
+    out_part = dot(mixed, dx1, TN).astype(BF).reshape(shards, part_rows, WIDTH)
+    out_own = scatter_keys(out_part, depth, 10)
+    dob_a, dob_b = pick(shard * SEQ + y < shards, dob[:, :QCOLS], dob[:, QCOLS:])
+    dob_zig = jnp.stack(
+        pick(
+            head_zero,
+            zig.move(dob_a, zig.heads[0], True),
+            zig.move(dob_b, zig.heads[1], True),
+        )
+    )
+    flat = kv.reshape(shards * rows, 2 * HEAD)
+    dq, dkv_part = attend_backward(q, flat, lo, info, top, total, dob_zig, ob)
+    dq_a, dq_b = pick(even, dq[0], dq[1])
+    dq_pair = jnp.stack([zig.move(dq_a, zig.rows[0], True), zig.move(dq_b, zig.rows[1], True)])
+    return dq_pair, scatter_keys(dkv_part.reshape(kv.shape), depth, 5), out_own
+
+
 def local(depth, stream, doc_starts, routes, attn_gain, w_query, w_key, w_value, w_out, ffn_gain, w_router, w_gate, w_up, w_down, out_grad):
     tokens = stream.shape[0]
     rows_in, rows_out = w_gate.shape[1], w_down.shape[1]
     shards = depth * INNER
     z, i, y = (lax.axis_index(a) for a in AXES)
     shard = z * INNER + i
-    own_block = shard * SEQ + y
     me = i * SEQ + y
     zig = Zigzag(shards)
 
@@ -1507,10 +1579,8 @@
     gain_a, gain_f = gains[0:1], gains[1:2]
     router_w = extra_w[:, 2 : 2 + E]
     qkv_w = weights[:, :QKV]
-    kv = kv.reshape(shards * SEQ * tokens, 2 * HEAD)
-    even = lax.rem(shard, 2) == 0
     head_zero = y == 0
-    low_half = own_block < shards
+    mixed_pair = mixed
     mixed = jnp.concatenate([mixed[0], mixed[1]], axis=1)
     normed, scale = rms_parts(x1)
     h2 = (normed * gain_f).astype(BF)
@@ -1532,59 +1602,36 @@
     probs = jax.nn.softmax(dot(h2, router_w), axis=-1)
     dp = back[:, WIDTH : WIDTH + E] * chosen
     dz = (probs * (dp - jnp.sum(dp * probs, axis=-1, keepdims=True))).astype(BF)
-    router_part = dot(h2, dz, TN)
+    router_part = dot(dz, h2, TN)
     dh2 = back[:, :WIDTH] + dot(dz, router_w, NT)
     grad_f = out_grad.astype(F32)
     dx1 = grad_f + rms_pull(normed, scale, dh2, gain_f)
     gain_f_part = jnp.sum(dh2 * normed, axis=0)
     dx1_low = dx1.astype(BF)
-    out_part = dot(mixed, dx1_low, TN)
-    dob = dot(dx1_low, out_w, NT).astype(BF)
-
-    dob_a, dob_b = pick(low_half, dob[:, :QCOLS], dob[:, QCOLS:])
-    dob_low, dob_high = pick(
-        head_zero,
-        zig.move(dob_a, zig.heads[0], True),
-        zig.move(dob_b, zig.heads[1], True),
-    )
-    dob_zig = jnp.stack([dob_low, dob_high])
-    dq, dkv_part = attend_backward(q, kv, lo, info, top, total, dob_zig, ob)
-    dq_a, dq_b = pick(even, dq[0], dq[1])
-    dq_pair = jnp.concatenate(
-        [zig.move(dq_a, zig.rows[0], True), zig.move(dq_b, zig.rows[1], True)], axis=0
-    )
-    dkv = scatter_keys(dkv_part.reshape(shards, SEQ * tokens, 2 * HEAD), depth)
-    raw = unturn(dq_pair, dkv, cosine, sine)
-    qkv_part = dot(h1, raw, TN)
-    dh1 = dot(raw, qkv_w, NT)
-
-    normed_pair, scale_pair = rms_parts(pair.astype(F32))
-    gain_a_part = jnp.sum(dh1 * normed_pair, axis=0)
-    dh1 = dh1.reshape(SEQ, tokens, WIDTH)
-    mine, other = pick(head_zero, dh1[0], dh1[1])
-    theirs = lax.ppermute(other.astype(BF), "seq", [(0, 1), (1, 0)])
-    normed_s, scale_s = rms_parts(stream.astype(F32))
-    stream_grad = (
-        dx1 + rms_pull(normed_s, scale_s, mine + theirs.astype(F32), gain_a)
-    ).astype(BF)
-
+    if depth <= 4:
+        dq_pair, dkv, out_own = backward(
+            q, kv, qseg, starts, top, total, ob, mixed_pair, dx1_low, out_w, rows_in, depth
+        )
+    else:
+        dq_pair, dkv, out_own = back_apart(
+            zig, q, kv, lo, info, top, total, ob, mixed, dx1_low, out_w, rows_in, depth
+        )
     small = jnp.concatenate(
         [
-            gain_a_part[:, None],
-            gain_f_part[:, None],
+            jnp.zeros((1, WIDTH), F32),
+            gain_f_part[None, :],
             router_part,
-            jnp.zeros((WIDTH, EXTRA - 2 - E), F32),
+            jnp.zeros((EXTRA - 2 - E, WIDTH), F32),
         ],
-        axis=1,
+        axis=0,
     )
-    dense = jnp.concatenate([qkv_part, small, out_part], axis=1).astype(BF)
-    own, peer, moe_out = closing(dense.reshape(shards, rows_in, PACK), moe_own, depth)
+    stream_grad, own, peer, peer_out, moe_out = finish_layer(
+        dq_pair, dkv, cosine, sine, h1, weights, pair, small, dx1, gain_a, out_own, moe_own, depth
+    )
     peer = peer.astype(F32)
 
     def halves(a, b):
-        return jnp.concatenate(
-            pick(head_zero, own[:, a:b], peer[:, a:b]), axis=1
-        )
+        return jnp.concatenate(pick(head_zero, own[:, a:b], peer[:, a:b]), axis=1)
 
     both = own[:, QKV:] + peer[:, QKV:]
     moe_out = moe_out.astype(F32)
@@ -1595,7 +1642,7 @@
         halves(0, QCOLS),
         halves(QCOLS, QCOLS + HEAD),
         halves(QCOLS + HEAD, QKV),
-        both[:, EXTRA:],
+        out_own + peer_out.astype(F32),
         both[:, 1],
         both[:, 2 : 2 + E],
         moe_out[:, :rows_in, :FF],

time: 783 us -> 729 us (0.931)
  Pallas kernels: 468 us -> 537 us
  starting transfers between devices: 44.9 us -> 0.08 us
  waiting for transfers between devices: 35.5 us -> 0.06 us
  local copies, waits for them, and re-layouts: 47.4 us -> 31.2 us
  matrix products: 108 us -> 96.3 us
    pallas_call x4 -> x2, Pallas kernels: 208 us -> 278 us  [the longest x1 140 us: finish_layer(): pl.pallas_call(kernel, out_shape=(sds((block, WIDTH), BF), sds((part_rows...]
    ppermute x5 -> x0, starting transfers between devices: 44.9 us -> none  [the longest x4 44.9 us: move(): return lax.ppermute(x, AXES, [(b, a) for a, b in pairs] if back else pairs)]
    ppermute x5 -> x0, waiting for transfers between devices: 35.5 us -> none  [the longest x4 35.5 us: move(): return lax.ppermute(x, AXES, [(b, a) for a, b in pairs] if back else pairs)]
    concatenate x4 -> x2, local copies, waits for them, and re-layouts: 17.4 us -> 0.08 us  [local(): jnp.concatenate([jnp.zeros((1, WIDTH), F32), gain_f_part[None, :], router...]
    dot_general x18 -> x14, matrix products: 93.4 us -> 81.9 us  [dot(): return lax.dot_general(a, b, dims, preferred_element_type=F32)]
  transfers between devices with their start and end apart: 7 -> 2, of which waited for: 1 -> 0; matrix products, arithmetic and copies ran while one was open for 15% -> 10% of each run, Pallas kernels for 17% -> 24%
where the time goes in v3:
time: 729 us; the launch traced here: 726 us
  Pallas kernels  537 us (74%)
  matrix products  96.3 us (13%)
  other arithmetic  46.4 us (6%)
  local copies, waits for them, and re-layouts  31.2 us (4%)
  between operations  14.9 us (2%)
    pallas_call x1, Pallas kernels, front(): pl.pallas_call(kernel, out_shape=(sds((rows, WIDTH), BF), sds((WIDTH, FIR...  220 us
    pallas_call x1, Pallas kernels, finish_layer(): pl.pallas_call(kernel, out_shape=(sds((block, WIDTH), BF), sds((part_rows...  140 us
    pallas_call x1, Pallas kernels, backward(): pl.pallas_call(kernel, out_shape=(sds(pair, BF), sds((rows, 2 * HEAD), F3...  138 us
    dot_general x14, matrix products, dot(): return lax.dot_general(a, b, dims, preferred_element_type=F32)  81.9 us
    pallas_call x1, Pallas kernels, scatter_plane(): pl.pallas_call(kernel, out_shape=jax.ShapeDtypeStruct((rows, cols), F32),...  38.9 us
  transfers between devices with their start and end apart: 2, of which 0 were waited for; matrix products, arithmetic and copies ran while one was open for 10% of the time, Pallas kernels for 24%

profile of v3, /device:TPU:0, one launch (start us, length us, event | category | flops | bytes accessed | tf_op | source)
XLA Modules:
  0.0 725.8 jit_solution(8273196117274852444)
XLA Ops:
  7.3 0.8 copy.47
  8.8 0.8 copy.49
  12.6 1.0 fusion.30
  16.5 1.0 pad_maximum_fusion.4
  17.5 3.4 pad_maximum_fusion.2.mo_ref
  20.9 0.8 concatenate.54.pk_ref
  21.7 219.9 %front.1 = (bf16[512,1536]{1,0:T(8,128)(2,1)}, bf16[1536,1152]{1,0:T(8,128)(2,1)}, f32[8,8,256]{2,1,0:T(8,128)}, bf16[512,1536]{1,0:T(8,128)(2,1)}, bf16[2,256,7...) custom-call(bf16[256,1536]{1,0:T(8,128)(2,1)} %st_ref.1, ...), custom_call_target="tpu_custom_call" | custom-call | tf_op jit(solution)/shard_map/front/pallas_call | solution.py:984
  241.6 1.1 multiply_reduce_fusion.5
  242.9 5.1 fusion.36
  247.9 3.2 slice.78
  251.2 3.0 fusion.39
  254.3 4.3 convolution_convert_fusion.3
  258.7 1.4 convolution_convert_fusion.2
  260.1 2.0 copy-done.10
  262.1 3.9 fusion.42
  266.0 14.5 %multiply_convert_fusion.2 = (bf16[1536,768]{1,0:T(8,128)(2,1)S(1)}, f32[1536,768]{1,0:T(8,128)}, f32[1536,768]{1,0:T(8,128)}) fusion(f32[1536,768]{1,0:T(8,128)S(1)} %fusion.42, bf16[1536,1536]{1,0:T(8,128)(2,1)S(1)} %bitcast.73, bf16[1536,768]{1,0:T(8,128)(2,1)S(1)} %bitcast.87), kind=kOutput, calls=%fused_computation.16 | convolution fusion | flops 3701735424 | bytes 23592960 | tf_op jit(solution)/shard_map/dot_general | solution.py:39
  280.5 16.2 %fusion.1 = (f32[1536]{0:T(1024)S(1)}, f32[1536,1536]{1,0:T(8,128)}) fusion(bf16[8,192,1536]{2,1,0:T(8,128)(2,1)S(1)} %convolution_convert_fusion.2, bf16[1536,768]{1,0:T(8,128)(2,1)S(1)} %get-tuple-element.114, bf16[768,1536]{1,0:T(8,128)(2,1)S(1)} %bitcast.85), kind=kOutput, calls=%fused_computation.4 | convolution fusion | flops 3630955008 | bytes 18880512 | tf_op jit(solution)/shard_map/dot_general | solution.py:39
  296.8 0.8 select_reduce_fusion
  297.7 11.0 %fusion.2 = (bf16[1536,1536]{1,0:T(8,128)(2,1)}, bf16[1536,1536]{1,0:T(8,128)(2,1)}) fusion(bf16[8,192,1536]{2,1,0:T(8,128)(2,1)} %copy-done.2, f32[1536]{0:T(1024)S(1)} %mul.223, f32[1536,1536]{1,0:T(8,128)} %get-tuple-element.141), kind=kLoop, calls=%fused_computation.5 | loop fusion | flops 11796480 | bytes 23599104 | tf_op jit(solution)/shard_map/convert_element_type | solution.py:1478
  308.7 6.9 convolution_convert_fusion.1
  315.7 3.3 fusion
  319.0 8.6 %multiply_convert_fusion.1 = (bf16[1536,768]{1,0:T(8,128)(2,1)S(1)}, bf16[1536,768]{1,0:T(8,128)(2,1)S(1)}) fusion(f32[1536,768]{1,0:T(8,128)} %get-tuple-element.115, f32[1536,768]{1,0:T(8,128)} %copy-done.17, f32[1536,768]{1,0:T(8,128)} %get-tuple-element.139, bf16[1536,1536]{1,0:T(8,128)(2,1)S(1)} %bitcast.78, bf16[768,1536]{1,0:T(8,128)(2,1)S(1)} %bitcast.86), kind=kOutput, calls=%fused_computation.14 | convolution fusion | flops 3645112320 | bytes 25952256 | tf_op jit(solution)/shard_map/dot_general | solution.py:39
  327.7 4.2 convolution_convert_fusion.6
  332.0 4.2 convolution_convert_fusion.5
  336.2 4.2 convolution_convert_fusion.4
  340.4 3.3 pad_maximum_fusion
  343.8 6.5 copy.50
  352.2 1.5 fusion.40
  354.3 10.0 %fusion.43 = f32[1536,1536]{1,0:T(8,128)} fusion(bf16[1536,768]{1,0:T(8,128)(2,1)} %copy-done.16, bf16[1536,768]{1,0:T(8,128)(2,1)} %bitcast.89), kind=kOutput, calls=%fused_computation.125 | convolution fusion | flops 3623878656 | bytes 14155776 | tf_op jit(solution)/shard_map/dot_general | solution.py:39
  364.3 6.7 add_convert_fusion
  371.0 1.9 convolution_convert_fusion
  372.9 3.4 pad_maximum_fusion.1.part_ref
  376.3 38.9 %scatter_plane.1 = f32[256,1664]{1,0:T(8,128)} custom-call(bf16[8,256,1664]{2,1,0:T(8,128)(2,1)} %pad_maximum_fusion.1.part_ref), custom_call_target="tpu_custom_call" | custom-call | tf_op jit(solution)/shard_map/scatter_plane/pallas_call | solution.py:282
  415.3 1.2 multiply_reduce_fusion.3
  416.5 3.4 multiply_reduce_fusion
  420.0 1.3 fusion.41
  421.3 1.0 maximum_maximum_fusion.sm_ref
  422.3 3.9 fusion.34
  426.2 137.9 %backward.1 = (bf16[2,256,768]{2,1,0:T(8,128)(2,1)}, f32[512,256]{1,0:T(8,128)}, f32[96,1536]{1,0:T(8,128)}) custom-call(bf16[2,256,768]{2,1,0:T(8,128)(2,1)} %get-tuple-element.40.q_ref, bf16[16,512,256]{2,1,0:T(8,128)(2,1)} %get-tuple-element.41.kv_ref, bf16[2,256,128]{2,1,0:T(8,128)(2,1)} %select_convert_fusion.qs_ref, s32[2,128]{1,0:T(2,128)} %pad_add_fusion.sg_ref, ...), custom_call_target="tpu_custom_call" | custom-call | tf_op jit(solution)/shard_map/backward/pallas_call | solution.py:1257
  564.1 140.1 %finish_layer.1 = (bf16[256,1536]{1,0:T(8,128)(2,1)}, f32[96,1152]{1,0:T(8,128)}, bf16[96,1152]{1,0:T(8,128)(2,1)}, bf16[96,1536]{1,0:T(8,128)(2,1)}, bf16[8,144,1536]{2,1,0:T(8,128)(2,1)}) custom-call(bf16[2,256,768]{2,1,0:T(8,128)(2,1)} %get-tuple-element.48.dq_ref, f32[512,256]{1,0:T(8,128)} %get-tuple-element.49.dkv_ref, ...), custom_call_target="tpu_custom_call" | custom-call | tf_op jit(solution)/shard_map/finish_layer/pallas_call | solution.py:1374
  704.3 1.0 convert_element_type.155
  705.2 0.9 slice_select_fusion.4
  706.1 1.0 slice_select_fusion.1
  707.1 4.5 fusion.37
  711.6 1.7 slice.111
  714.1 0.9 convert_add_fusion.1
  716.9 0.9 pad_maximum_fusion.3
  717.8 0.9 copy.56
  (111 shorter events, 12.7 us)
Async XLA Ops:
  7.2 5.4 copy-start
  7.2 415.1 %reduce-scatter.3.cloned.1.call-start = ((), (), s32[]{:S(2)}) async-start(), calls=%async_computation.2 | async-start | bytes 7077888 | tf_op jit(solution)/shard_map/reduce_scatter | solution.py:1592
  241.6 9.5 %slice-start = ((s8[6291456]{0:T(1024)(128)(4,1)}), s8[4194304]{0:T(1024)(128)(4,1)S(1)}, s32[]{:S(2)}) async-start(s8[6291456]{0:T(1024)(128)(4,1)} %bitcast.66), calls=%async_computation.4 | async-start | bytes 8388608
  242.9 8.3 %slice-start.1 = ((s8[6291456]{0:T(1024)(128)(4,1)}), s8[2097152]{0:T(1024)(128)(4,1)S(1)}, s32[]{:S(2)}) async-start(s8[6291456]{0:T(1024)(128)(4,1)} %bitcast.66), calls=%async_computation.5 | async-start | bytes 4194304
  251.2 7.5 %slice-start.2 = ((s8[6291456]{0:T(1024)(128)(4,1)}), s8[2097152]{0:T(1024)(128)(4,1)S(1)}, s32[]{:S(2)}) async-start(s8[6291456]{0:T(1024)(128)(4,1)} %bitcast.69), calls=%async_computation.6 | async-start | bytes 4194304
  254.3 4.4 slice-start.3
  258.6 7.3 %copy-start.3 = (bf16[8,192,1536]{2,1,0:T(8,128)(2,1)}, bf16[8,192,1536]{2,1,0:T(8,128)(2,1)S(1)}, u32[]{:S(2)}) copy-start(bf16[8,192,1536]{2,1,0:T(8,128)(2,1)S(1)} %convolution_convert_fusion.3) | copy-start | bytes 14155780
  258.7 3.4 copy-start.10
  260.1 20.4 %copy-start.2 = (bf16[8,192,1536]{2,1,0:T(8,128)(2,1)}, bf16[8,192,1536]{2,1,0:T(8,128)(2,1)S(1)}, u32[]{:S(2)}) copy-start(bf16[8,192,1536]{2,1,0:T(8,128)(2,1)S(1)} %convolution_convert_fusion.2) | copy-start | bytes 14155780
  262.1 3.9 copy-start.8
  266.0 14.5 %copy-start.17 = (f32[1536,768]{1,0:T(8,128)}, f32[1536,768]{1,0:T(8,128)S(1)}, u32[]{:S(2)}) copy-start(f32[1536,768]{1,0:T(8,128)S(1)} %fusion.42) | copy-start | bytes 14155780
  266.0 14.5 %copy-start.7 = (bf16[16,48,1536]{2,1,0:T(8,128)(2,1)S(1)}, bf16[16,48,1536]{2,1,0:T(8,128)(2,1)}, u32[]{:S(2)}) copy-start(bf16[16,48,1536]{2,1,0:T(8,128)(2,1)} %slice.78) | copy-start | bytes 7077892
  280.5 16.3 %copy-start.14 = (bf16[1536,768]{1,0:T(8,128)(2,1)}, bf16[1536,768]{1,0:T(8,128)(2,1)S(1)}, u32[]{:S(2)}) copy-start(bf16[1536,768]{1,0:T(8,128)(2,1)S(1)} %get-tuple-element.114) | copy-start | bytes 7077892
  315.6 248.5 %reduce-scatter.5.cloned.1.call-start = ((), (), s32[]{:S(2)}) async-start(), calls=%async_computation.3 | async-start | bytes 8847360 | tf_op jit(solution)/shard_map/reduce_scatter | solution.py:1593
  315.7 12.0 %slice-start.4 = ((s8[4718592]{0:T(1024)(128)(4,1)}), s8[4194304]{0:T(1024)(128)(4,1)S(1)}, s32[]{:S(2)}) async-start(s8[4718592]{0:T(1024)(128)(4,1)} %bitcast.74), calls=%async_computation.8 | async-start | bytes 8388608
  319.0 8.7 %slice-start.5 = ((s8[4718592]{0:T(1024)(128)(4,1)}), s8[524288]{0:T(1024)(128)(4,1)S(1)}, s32[]{:S(2)}) async-start(s8[4718592]{0:T(1024)(128)(4,1)} %bitcast.74), calls=%async_computation.9 | async-start | bytes 1048576
  327.6 4.3 copy-start.16
  327.7 4.3 copy-start.18
  327.7 8.5 %slice-start.6 = ((s8[4718592]{0:T(1024)(128)(4,1)}), s8[4194304]{0:T(1024)(128)(4,1)S(1)}, s32[]{:S(2)}) async-start(s8[4718592]{0:T(1024)(128)(4,1)} %bitcast.79), calls=%async_computation.10 | async-start | bytes 8388608
  332.0 4.3 slice-start.7
  332.0 4.3 copy-start.15
  343.8 6.7 copy-start.5
  354.3 10.0 %copy-start.9 = (bf16[16,96,768]{2,1,0:T(8,128)(2,1)S(1)}, bf16[16,96,768]{2,1,0:T(8,128)(2,1)}, u32[]{:S(2)}) copy-start(bf16[16,96,768]{2,1,0:T(8,128)(2,1)} %get-tuple-element.119) | copy-start | bytes 7077892
  354.3 10.0 %copy-start.19 = (bf16[1536,768]{1,0:T(8,128)(2,1)S(1)}, bf16[1536,768]{1,0:T(8,128)(2,1)}, u32[]{:S(2)}) copy-start(bf16[1536,768]{1,0:T(8,128)(2,1)} %copy-done.18) | copy-start | bytes 7077892
  415.1 7.2 copy-start.6
  707.1 4.5 copy-start.4
  707.1 11.6 %copy-start.1 = (bf16[96,1536]{1,0:T(8,128)(2,1)S(1)}, bf16[96,1536]{1,0:T(8,128)(2,1)}, u32[]{:S(2)}) copy-start(bf16[96,1536]{1,0:T(8,128)(2,1)} %param.18) | copy-start | bytes 884740
  711.6 2.5 copy-start.11
  711.6 2.5 copy-start.13
  711.6 6.2 copy-start.12
Sparse Core Ops, SparseCore 0:
  315.7 66.9 reduce-scatter.2
  385.2 138.1 reduce-scatter.4

commit v4 on v3

--- a/solution.py
+++ b/solution.py
@@ -234,49 +234,85 @@
     return rows
 
 
+class PlaneScatter:
+    ORDER = ((1, 1), (1, 0), (0, 1), (0, 0))
+
+    @staticmethod
+    def scratch(rows, cols):
+        return (
+            [pltpu.VMEM((4, rows, cols), BF)] * 2
+            + [pltpu.VMEM((2, rows // 2, cols), BF)] * 4
+            + dma_sems(10, 10)
+        )
+
+    def __init__(self, net, sends, part, rows, scratch):
+        self.net, self.sends, self.part, self.rows = net, sends, part, rows
+        self.bc, self.mid, self.bx, self.by, self.second, self.b2, self.ss, self.rs = scratch
+        self.half = rows // 2
+        self.lo, self.hi = pl.ds(0, self.half), pl.ds(self.half, self.half)
+        self.chunk = chunk_of(self.half)
+
+    def place(self, fx, fy, core):
+        x = 1 - self.net.x if fx else self.net.x
+        y = 1 - self.net.y if fy else self.net.y
+        return (x * 2 + core) * SEQ + y
+
+    def send(self, src, dst, n, device):
+        self.sends.start(src, dst, self.ss.at[n], self.rs.at[n], device)
+
+    def take(self, dst, n):
+        arrived(dst, self.ss.at[n], self.rs.at[n], self.net.xp)
+
+    def begin(self):
+        net = self.net
+        for n, (fx, fy) in enumerate(self.ORDER):
+            self.send(self.part.at[self.place(fx, fy, 1 - net.core)], self.bc.at[n], n, net.cp)
+
+    def cores(self):
+        net, mid = self.net, self.mid
+        for n, (fx, fy) in enumerate(self.ORDER):
+            self.take(self.bc.at[n], n)
+            own = self.part.at[self.place(fx, fy, net.core)]
+            add_into(mid.at[n], [own, self.bc.at[n]], self.rows, self.chunk)
+            if n == 0:
+                self.send(mid.at[0, self.lo], self.bx.at[0], 4, net.xp)
+                self.send(mid.at[0, self.hi], self.by.at[0], 5, net.yp)
+            if n == 1:
+                self.send(mid.at[1, self.lo], self.bx.at[1], 6, net.xp)
+            if n == 2:
+                self.send(mid.at[2, self.hi], self.by.at[1], 7, net.yp)
+
+    def turn(self):
+        net, mid, second = self.net, self.mid, self.second
+        self.take(self.bx.at[0], 4)
+        add_into(second.at[0], [mid.at[2, self.lo], self.bx.at[0]], self.half, self.chunk)
+        self.send(second.at[0], self.b2.at[0], 8, net.yp)
+        self.take(self.by.at[0], 5)
+        add_into(second.at[1], [mid.at[1, self.hi], self.by.at[0]], self.half, self.chunk)
+        self.send(second.at[1], self.b2.at[1], 9, net.xp)
+
+    def final(self, out, more=()):
+        mid = self.mid
+        self.take(self.bx.at[1], 6)
+        self.take(self.by.at[1], 7)
+        for n, (at, got) in enumerate(((self.lo, self.bx), (self.hi, self.by))):
+            self.take(self.b2.at[n], 8 + n)
+            terms = [mid.at[3, at], got.at[1], self.b2.at[n]] + [m.at[at] for m in more]
+            add_into(out.at[at], terms, self.half, self.chunk)
+
+
 def scatter_plane(part, depth):
     rows, cols = part.shape[1:]
-    half = rows // 2
-
-    def kernel(part_ref, out, bc, mid, bx, by, second, b2, ssem, rsem):
+
+    def kernel(part_ref, out, *scratch):
         net = Net(depth)
         sends = Sends()
-
-        def place(fx, fy, core):
-            x = 1 - net.x if fx else net.x
-            y = 1 - net.y if fy else net.y
-            return (x * 2 + core) * SEQ + y
-
         greet([net.xp, net.yp, net.cp])
-        order = ((1, 1), (1, 0), (0, 1), (0, 0))
-        for n, (fx, fy) in enumerate(order):
-            sends.start(
-                part_ref.at[place(fx, fy, 1 - net.core)], bc.at[n], ssem.at[n], rsem.at[n], net.cp
-            )
-        ch = chunk_of(half)
-        lo, hi = pl.ds(0, half), pl.ds(half, half)
-        for n, (fx, fy) in enumerate(order):
-            arrived(bc.at[n], ssem.at[n], rsem.at[n], net.cp)
-            add_into(mid.at[n], [part_ref.at[place(fx, fy, net.core)], bc.at[n]], rows, ch)
-            if n == 0:
-                sends.start(mid.at[0, lo], bx.at[0], ssem.at[4], rsem.at[4], net.xp)
-                sends.start(mid.at[0, hi], by.at[0], ssem.at[5], rsem.at[5], net.yp)
-            if n == 1:
-                sends.start(mid.at[1, lo], bx.at[1], ssem.at[6], rsem.at[6], net.xp)
-            if n == 2:
-                sends.start(mid.at[2, hi], by.at[1], ssem.at[7], rsem.at[7], net.yp)
-        arrived(bx.at[0], ssem.at[4], rsem.at[4], net.xp)
-        add_into(second.at[0], [mid.at[2, lo], bx.at[0]], half, ch)
-        sends.start(second.at[0], b2.at[0], ssem.at[8], rsem.at[8], net.yp)
-        arrived(by.at[0], ssem.at[5], rsem.at[5], net.yp)
-        add_into(second.at[1], [mid.at[1, hi], by.at[0]], half, ch)
-        sends.start(second.at[1], b2.at[1], ssem.at[9], rsem.at[9], net.xp)
-        arrived(bx.at[1], ssem.at[6], rsem.at[6], net.xp)
-        arrived(by.at[1], ssem.at[7], rsem.at[7], net.yp)
-        arrived(b2.at[0], ssem.at[8], rsem.at[8], net.yp)
-        add_into(out.at[lo], [mid.at[3, lo], bx.at[1], b2.at[0]], half, ch)
-        arrived(b2.at[1], ssem.at[9], rsem.at[9], net.xp)
-        add_into(out.at[hi], [mid.at[3, hi], by.at[1], b2.at[1]], half, ch)
+        work = PlaneScatter(net, sends, part_ref, rows, scratch)
+        work.begin()
+        work.cores()
+        work.turn()
+        work.final(out)
         sends.finish()
 
     return pl.pallas_call(
@@ -284,9 +320,7 @@
         out_shape=jax.ShapeDtypeStruct((rows, cols), F32),
         in_specs=[vmem()],
         out_specs=vmem(),
-        scratch_shapes=[pltpu.VMEM((4, rows, cols), BF)] * 2
-        + [pltpu.VMEM((2, half, cols), BF)] * 4
-        + dma_sems(10, 10),
+        scratch_shapes=PlaneScatter.scratch(rows, cols),
         compiler_params=comm_params(4),
         name="scatter_plane",
     )(part)
@@ -1104,18 +1138,41 @@
     def kernel(
         q_ref, kv_ref, qs_ref, sg_ref, m_ref, l_ref, ob_ref, mix_ref, dx_ref, wf_ref,
         dq_out, dkv_out, own_out,
-        dob, do_ref, da, dl, acc, dqs, dkv, wpart, so, ro, sq, rq, *scratch,
+        dob, do_ref, da, dl, acc, dqs, dkv, wpart, wget, so, ro, sq, rq, sw, rw, *scratch,
     ):
         net = Net(depth)
         mirror = Mirror(net)
         keys = Tally(net, dkv, rows, scratch[:11])
-        outs = Tally(net, wpart, part_rows, scratch[11:])
+        mine = wpart.at[net.y]
+        outs = Tally(net, mine, part_rows, scratch[11:])
+        quarter = shards // 4
+
+        def pair_copy(n):
+            at = pl.ds(n * quarter, quarter)
+            return remote(
+                wpart.at[1 - net.y, at], wget.at[at], sw.at[n], rw.at[n], net.yp
+            )
+
+        def pair_sum():
+            for n in range(4):
+                at = pl.ds(n * quarter, quarter)
+                arrived(wget.at[at], sw.at[n], rw.at[n], net.yp)
+
+                def body(b, carry):
+                    add_into(
+                        wpart.at[net.y, b], [wpart.at[net.y, b], wget.at[b]], part_rows, outs.chunk
+                    )
+                    return carry
+
+                lax.fori_loop(n * quarter, (n + 1) * quarter, body, 0)
+            outs.begin()
+
         heads = [mirror.heads_out(k) for k in range(2)]
         backs = [mirror.rows_back(k) for k in range(2)]
         barrier = pltpu.get_barrier_semaphore()
-        for device in net.zpeers() + [net.xp, net.cp]:
+        for device in net.zpeers() + [net.xp, net.cp, net.yp]:
             pl.semaphore_signal(barrier, inc=1, device_id=device, device_id_type=MESH)
-        count = depth - 1 + 2
+        count = depth - 1 + 3
         for route, _ in heads + backs:
             count = count + route.hello()
         do_refs = [
@@ -1137,8 +1194,11 @@
             cols = slice((n % 2) * wide, (n % 2 + 1) * wide)
             grad = dot(mix_ref[n // 2, :, cols].T, dx).astype(BF)
             for b in range(wide // part_rows):
-                wpart[n * (wide // part_rows) + b] = grad[b * part_rows : (b + 1) * part_rows]
-        outs.begin()
+                for s in range(SEQ):
+                    wpart[s, n * (wide // part_rows) + b] = grad[
+                        b * part_rows : (b + 1) * part_rows, s * QCOLS : (s + 1) * QCOLS
+                    ]
+            pair_copy(n).start()
         acc[...] = jnp.zeros_like(acc)
         for k in range(2):
             heads[k][0].arrive(lambda: (do_ref.at[k], so.at[k], ro.at[k]))
@@ -1226,11 +1286,15 @@
             def _():
                 keys.z_stage(g)
 
-            @pl.when(u == 2)
+            @pl.when(u == shards - 7)
+            def _():
+                pair_sum()
+
+            @pl.when(u == shards - 4)
             def _():
                 outs.far_stages()
 
-            @pl.when(u == shards - INNER)
+            @pl.when(u == shards - 1)
             def _():
                 outs.near_stages()
 
@@ -1249,6 +1313,8 @@
         for k in range(2):
             heads[k][0].sent(do_refs[k])
             backs[k][0].sent(dq_refs[k])
+        for n in range(4):
+            pair_copy(n).wait_send()
         outs.finish()
         keys.finish()
 
@@ -1259,7 +1325,7 @@
         out_shape=(
             sds(pair, BF),
             sds((rows, 2 * HEAD), F32),
-            sds((part_rows, WIDTH), F32),
+            sds((part_rows, QCOLS), F32),
         ),
         in_specs=[vmem()] * 10,
         out_specs=(vmem(),) * 3,
@@ -1271,17 +1337,20 @@
             pltpu.VMEM((2, GROUP, HEAD, block), F32),
             pltpu.VMEM(pair, BF),
             pltpu.VMEM((shards, rows, 2 * HEAD), BF),
-            pltpu.VMEM((shards, part_rows, WIDTH), BF),
+            pltpu.VMEM((SEQ, shards, part_rows, QCOLS), BF),
+            pltpu.VMEM((shards, part_rows, QCOLS), BF),
         ]
-        + dma_sems(2, 2, 2, 2)
+        + dma_sems(2, 2, 2, 2, 4, 4)
         + ShardScatter.scratch(depth, rows, 2 * HEAD)
-        + ShardScatter.scratch(depth, part_rows, WIDTH),
+        + ShardScatter.scratch(depth, part_rows, QCOLS),
         compiler_params=comm_params(8, 60 << 20),
         name="backward",
     )(q, kv, qseg, starts, m, l, ob, mixed, dx1, out_w)
 
 
-def finish_layer(dq, dkv, cosine, sine, h1, weights, pair, small, dx1, gain_a, out_own, moe, depth):
+def finish_layer(
+    dq, dkv, cosine, sine, h1, weights, pair, small, dx1, gain_a, out_own, mixture, x1, moe, depth
+):
     block = dx1.shape[0]
     rows = pair.shape[0]
     shards = depth * INNER
@@ -1289,18 +1358,28 @@
     wide = 384
 
     def kernel(
-        dq_ref, dkv_ref, c_ref, n_ref, h1_ref, w_ref, s_ref, sm_ref, dx_ref, ga_ref, oo_ref, moe_ref,
-        sg_out, own_out, pair_out, pair_wo, moe_out,
+        dq_ref, dkv_ref, c_ref, n_ref, h1_ref, w_ref, s_ref, sm_ref, dx_ref, ga_ref, oo_ref, mx_ref, x1_ref, moe_ref,
+        res_out, sg_out, own_out, pair_out, pair_wo, moe_out,
         raw, part, give, take, low, low_wo, sm, rm, sy, ry, ls, *scratch,
     ):
         net = Net(depth)
         sends = Sends()
         me = net.i * SEQ + net.y
         mine = pltpu.make_async_copy(moe_ref.at[net.i], moe_out.at[me], ls.at[0])
-        work = Tally(net, part, part_rows, scratch)
+        work = Tally(net, part, part_rows, scratch[:11])
+        mix = PlaneScatter(net, sends, mx_ref, block, scratch[11:])
         barrier = pltpu.get_barrier_semaphore()
         for device in net.zpeers() + net.plane():
             pl.semaphore_signal(barrier, inc=1, device_id=device, device_id_type=MESH)
+        pl.semaphore_wait(barrier, depth - 1 + E - 1)
+        mix.begin()
+        for di in range(1, INNER):
+            i = lax.rem(net.i + di, INNER)
+            sends.start(
+                moe_ref.at[i], moe_out.at[me], sm.at[di], rm.at[di], net.dev(i=i)
+            )
+        sends.start(moe_ref.at[net.i], moe_out.at[me], sm.at[0], rm.at[0], net.yp)
+        mine.start()
         cos, sin = c_ref[...], -n_ref[...]
         for k in range(2):
             at = slice(k * block, (k + 1) * block)
@@ -1311,7 +1390,7 @@
         dk = dkv_ref[:, :HEAD].astype(BF).astype(F32)
         raw[:, QCOLS : QCOLS + HEAD] = turn(dk, cos, sin).astype(BF)
         raw[:, QCOLS + HEAD :] = dkv_ref[:, HEAD:].astype(BF)
-        pl.semaphore_wait(barrier, depth - 1 + E - 1)
+        mix.cores()
         low_wo[...] = oo_ref[...].astype(BF)
         sends.start(low_wo, pair_wo, sy.at[1], ry.at[1], net.yp)
 
@@ -1326,15 +1405,6 @@
         give[...] = grad.astype(BF)
         sends.start(give, take, sy.at[2], ry.at[2], net.yp)
         gain_part = jnp.sum(grad * normed, axis=0, keepdims=True)
-        n = 0
-        for di in range(INNER):
-            for dy in range(SEQ):
-                if di or dy:
-                    i = lax.rem(net.i + di, INNER)
-                    device = net.dev(i=i, y=lax.rem(net.y + dy, SEQ))
-                    sends.start(moe_ref.at[i], moe_out.at[me], sm.at[n], rm.at[n], device)
-                    n += 1
-        mine.start()
         normed, scale, grad = half(net.y)
         gain_part = gain_part + jnp.sum(grad * normed, axis=0, keepdims=True)
         lanes = lax.broadcasted_iota(jnp.int32, (EXTRA, WIDTH), 0)
@@ -1349,6 +1419,11 @@
                 ]
         work.begin()
         work.far_stages()
+        mix.turn()
+        for di in range(1, INNER):
+            got = moe_out.at[lax.rem(net.i - di + INNER, INNER) * SEQ + net.y]
+            arrived(got, sm.at[di], rm.at[di], net.yp)
+            sends.start(got, got, sm.at[INNER - 1 + di], rm.at[INNER - 1 + di], net.yp)
         arrived(take, sy.at[2], ry.at[2], net.yp)
         inner = (grad + take[...].astype(F32)) * ga_ref[...]
         pull = scale * (inner - normed * jnp.mean(inner * normed, axis=-1, keepdims=True))
@@ -1357,13 +1432,11 @@
         work.final(own_out)
         low[...] = own_out[...].astype(BF)
         sends.start(low, pair_out, sy.at[0], ry.at[0], net.yp)
-        n = 0
+        mix.final(res_out, [x1_ref])
         for di in range(INNER):
-            for dy in range(SEQ):
-                if di or dy:
-                    frm = lax.rem(net.i - di + INNER, INNER) * SEQ + lax.rem(net.y + dy, SEQ)
-                    arrived(moe_out.at[frm], sm.at[n], rm.at[n], net.yp)
-                    n += 1
+            n = INNER - 1 + di if di else 0
+            got = moe_out.at[lax.rem(net.i - di + INNER, INNER) * SEQ + 1 - net.y]
+            arrived(got, sm.at[n], rm.at[n], net.yp)
         arrived(pair_wo, sy.at[1], ry.at[1], net.yp)
         arrived(pair_out, sy.at[0], ry.at[0], net.yp)
         sends.finish()
@@ -1375,26 +1448,146 @@
         kernel,
         out_shape=(
             sds((block, WIDTH), BF),
+            sds((block, WIDTH), BF),
             sds((part_rows, FIRST), F32),
             sds((part_rows, FIRST), BF),
-            sds((part_rows, WIDTH), BF),
+            sds((part_rows, QCOLS), BF),
             sds((E,) + moe.shape[1:], BF),
         ),
-        in_specs=[vmem()] * 11 + [hbm()],
-        out_specs=(vmem(),) * 4 + (hbm(),),
+        in_specs=[vmem()] * 13 + [hbm()],
+        out_specs=(vmem(),) * 5 + (hbm(),),
         scratch_shapes=[
             pltpu.VMEM((rows, QKV), BF),
             pltpu.VMEM((shards, part_rows, FIRST), BF),
             pltpu.VMEM((block, WIDTH), BF),
             pltpu.VMEM((block, WIDTH), BF),
             pltpu.VMEM((part_rows, FIRST), BF),
-            pltpu.VMEM((part_rows, WIDTH), BF),
+            pltpu.VMEM((part_rows, QCOLS), BF),
         ]
-        + dma_sems(E - 1, E - 1, 3, 3, 1)
-        + ShardScatter.scratch(depth, part_rows, FIRST),
+        + dma_sems(2 * INNER - 1, 2 * INNER - 1, 3, 3, 1)
+        + ShardScatter.scratch(depth, part_rows, FIRST)
+        + PlaneScatter.scratch(block, WIDTH),
         compiler_params=comm_params(9, 60 << 20),
         name="finish_layer",
-    )(dq, dkv, cosine, sine, h1, weights, pair, small, dx1, gain_a, out_own, moe)
+    )(dq, dkv, cosine, sine, h1, weights, pair, small, dx1, gain_a, out_own, mixture, x1, moe)
+
+
+def run_expert(h2, out_grad, onehot, gate, lane, moe_w, rows_in, rows_out):
+    blocks, tokens = h2.shape[:2]
+    slots = onehot.shape[1]
+    shards = moe_w.shape[0]
+    pairs = 2
+    steps = blocks // pairs
+    wide = WIDTH + EXTRA
+
+    def kernel(
+        h_ref, g_ref, oh_ref, gt_ref, ln_ref, w_ref, mix_out, back_out, grads_out,
+        gu_w, dn_w, gu_acc, dn_acc, rows, slot_g, stage, wsem, gsem,
+    ):
+        step = pl.program_id(0)
+
+        def weight_copies():
+            for n in range(shards):
+                yield pltpu.make_async_copy(
+                    w_ref.at[n, pl.ds(0, rows_in)], gu_w.at[pl.ds(n * rows_in, rows_in)], wsem.at[n]
+                )
+                yield pltpu.make_async_copy(
+                    w_ref.at[n, pl.ds(rows_in, rows_out)],
+                    dn_w.at[pl.ds(n * rows_out, rows_out)],
+                    wsem.at[shards + n],
+                )
+
+        @pl.when(step == 0)
+        def _():
+            for copy in weight_copies():
+                copy.start()
+            gu_acc[...] = jnp.zeros_like(gu_acc)
+            dn_acc[...] = jnp.zeros_like(dn_acc)
+            for copy in weight_copies():
+                copy.wait()
+
+        for b in range(pairs):
+            at = slice(b * slots, (b + 1) * slots)
+            rows[at, :] = dot(oh_ref[b], h_ref[b]).astype(BF)
+            slot_g[at, :] = dot(oh_ref[b], g_ref[b]).astype(BF)
+        gate_col = gt_ref[...].reshape(pairs * slots, 1)
+        both = dot(rows[...], gu_w[...])
+        pre, up = both[:, :FF], both[:, FF:]
+        phi = 0.5 * (1.0 + lax.erf(pre * (0.5**0.5)))
+        slope = phi + pre * jnp.exp(-0.5 * pre * pre) * 0.3989422804014327
+        gelu = pre * phi
+        active = (gelu * up).astype(BF)
+        grad = slot_g[...]
+        out = dot(active, dn_w[...])
+        gate_grad = jnp.sum(grad.astype(F32) * out, axis=-1, keepdims=True)
+        mixed = (out * gate_col).astype(BF)
+        expert_grad = (grad.astype(F32) * gate_col).astype(BF)
+        active_grad = dot(expert_grad, dn_w[...], NT)
+        low = jnp.concatenate(
+            [(active_grad * up * slope).astype(BF), (active_grad * gelu).astype(BF)], axis=1
+        )
+        back = dot(low, gu_w[...], NT).astype(BF)
+        back = jnp.concatenate([back, (gate_grad * ln_ref[...]).astype(BF)], axis=1)
+        for b in range(pairs):
+            at = slice(b * slots, (b + 1) * slots)
+            spread = oh_ref[b].T
+            mix_out[b] = dot(spread, mixed[at]).astype(BF)
+            back_out[b] = dot(spread, back[at]).astype(BF)
+        gu_acc[...] += dot(rows[...].T, low)
+        dn_acc[...] += dot(active.T, expert_grad)
+
+        @pl.when(step == steps - 1)
+        def _():
+            def copy(n, slot):
+                return pltpu.make_async_copy(stage.at[slot], grads_out.at[n], gsem.at[slot])
+
+            for n in range(shards):
+                slot = n % 2
+                if n >= 2:
+                    copy(n - 2, slot).wait()
+                stage[slot, :rows_in, :] = gu_acc[n * rows_in : (n + 1) * rows_in, :].astype(BF)
+                stage[slot, rows_in:, :] = dn_acc[n * rows_out : (n + 1) * rows_out, :].astype(BF)
+                copy(n, slot).start()
+            for n in range(shards - 2, shards):
+                copy(n, n % 2).wait()
+
+    sds = jax.ShapeDtypeStruct
+    block = lambda *shape: pl.BlockSpec((pairs,) + shape, lambda n: (n,) + (0,) * len(shape))
+    return pl.pallas_call(
+        kernel,
+        grid=(steps,),
+        out_shape=(
+            sds((blocks, tokens, WIDTH), BF),
+            sds((blocks, tokens, wide), BF),
+            sds(moe_w.shape, BF),
+        ),
+        in_specs=[
+            block(tokens, WIDTH),
+            block(tokens, WIDTH),
+            block(slots, tokens),
+            block(slots, 1),
+            pl.BlockSpec((1, EXTRA), lambda n: (0, 0)),
+            hbm(),
+        ],
+        out_specs=(block(tokens, WIDTH), block(tokens, wide), hbm()),
+        scratch_shapes=[
+            pltpu.VMEM((WIDTH, 2 * FF), BF),
+            pltpu.VMEM((FF, WIDTH), BF),
+            pltpu.VMEM((WIDTH, 2 * FF), F32),
+            pltpu.VMEM((FF, WIDTH), F32),
+            pltpu.VMEM((pairs * slots, WIDTH), BF),
+            pltpu.VMEM((pairs * slots, WIDTH), BF),
+            pltpu.VMEM((2, rows_in + rows_out, WIDTH), BF),
+        ]
+        + dma_sems(2 * shards, 2),
+        compiler_params=pltpu.CompilerParams(
+            vmem_limit_bytes=60 << 20, dimension_semantics=("arbitrary",)
+        ),
+        cost_estimate=pl.CostEstimate(
+            flops=int(3.8e10), bytes_accessed=40 << 20, transcendentals=4 << 20
+        ),
+        name="run_expert",
+    )(h2, out_grad, onehot, gate, lane, moe_w)
 
 
 def rms_parts(x):
@@ -1455,7 +1648,13 @@
     ) & (named[:, None, :] > 0.5)
     onehot = pick_slot.astype(BF)
     slots = blocks * MOST
-    gate = jnp.sum(jnp.where(pick_slot, gate_tok[:, None, :], 0.0), axis=-1).reshape(slots, 1)
+    gate = jnp.sum(jnp.where(pick_slot, gate_tok[:, None, :], 0.0), axis=-1)
+    if rows_in % 16 == 0 and rows_out % 16 == 0:
+        lane = (jnp.arange(EXTRA) == me).astype(F32)[None, :]
+        return run_expert(
+            h2, out_grad, onehot, gate[:, :, None], lane, moe_w, rows_in, rows_out
+        )
+    gate = gate.reshape(slots, 1)
     spread = lambda v: lax.dot_general(
         onehot, v, (((2,), (1,)), ((0,), (0,))), preferred_element_type=F32
     )
@@ -1508,8 +1707,10 @@
     shard = z * INNER + i
     even, head_zero = lax.rem(shard, 2) == 0, y == 0
     dob = dot(dx1, out_w, NT).astype(BF)
-    out_part = dot(mixed, dx1, TN).astype(BF).reshape(shards, part_rows, WIDTH)
-    out_own = scatter_keys(out_part, depth, 10)
+    out_part = dot(mixed, dx1, TN).astype(BF)
+    keep, give = pick(head_zero, out_part[:, :QCOLS], out_part[:, QCOLS:])
+    keep = keep.astype(F32) + lax.ppermute(give, "seq", [(0, 1), (1, 0)]).astype(F32)
+    out_own = scatter_keys(keep.astype(BF).reshape(shards, part_rows, QCOLS), depth, 10)
     dob_a, dob_b = pick(shard * SEQ + y < shards, dob[:, :QCOLS], dob[:, QCOLS:])
     dob_zig = jnp.stack(
         pick(
@@ -1589,14 +1790,12 @@
         h2_plane, grad_plane, chosen_all, router_w, moe_w, rows_in, rows_out, me
     )
     back = scatter_plane(back_part, depth)
-    mixture = lax.psum_scatter(mixture_part, ("inner", "seq"), scatter_dimension=0, tiled=False)
     moe_own = lax.psum_scatter(
         moe_grads.reshape(depth, INNER, rows_in + rows_out, WIDTH),
         "outer",
         scatter_dimension=0,
         tiled=False,
     )
-    result = (x1 + mixture.astype(F32)).astype(BF)
 
     chosen = chosen_t.T
     probs = jax.nn.softmax(dot(h2, router_w), axis=-1)
@@ -1625,8 +1824,22 @@
         ],
         axis=0,
     )
-    stream_grad, own, peer, peer_out, moe_out = finish_layer(
-        dq_pair, dkv, cosine, sine, h1, weights, pair, small, dx1, gain_a, out_own, moe_own, depth
+    result, stream_grad, own, peer, peer_out, moe_out = finish_layer(
+        dq_pair,
+        dkv,
+        cosine,
+        sine,
+        h1,
+        weights,
+        pair,
+        small,
+        dx1,
+        gain_a,
+        out_own,
+        mixture_part,
+        x1,
+        moe_own,
+        depth,
     )
     peer = peer.astype(F32)
 
@@ -1642,7 +1855,7 @@
         halves(0, QCOLS),
         halves(QCOLS, QCOLS + HEAD),
         halves(QCOLS + HEAD, QKV),
-        out_own + peer_out.astype(F32),
+        jnp.concatenate(pick(head_zero, out_own, peer_out.astype(F32)), axis=1),
         both[:, 1],
         both[:, 2 : 2 + E],
         moe_out[:, :rows_in, :FF],

time: 729 us -> 675 us (0.926)
  matrix products: 96.3 us -> 10 us
  Pallas kernels: 537 us -> 597 us
  other arithmetic: 46.4 us -> 23.9 us
  local copies, waits for them, and re-layouts: 31.2 us -> 22.2 us
    dot_general x14 -> x5, matrix products: 81.9 us -> 10 us  [dot(): return lax.dot_general(a, b, dims, preferred_element_type=F32)]
    pallas_call x1 -> x2, Pallas kernels: 140 us -> 210 us  [the longest x1 150 us: finish_layer(): pl.pallas_call(kernel, out_shape=(sds((block, WIDTH), BF), sds((block, WI...]
    dot_general x4 -> x0, matrix products: 14.5 us -> none  [the longest x2 8.74 us: experts(): lax.dot_general(onehot, v, (((1,), (1,)), ((0,), (0,))), preferred_elemen...]
    convert_element_type x4 -> x2, other arithmetic: 14.7 us -> 1.66 us  [the longest x1 1.14 us: experts(): onehot = pick_slot.astype(BF)]
    pallas_call x1, Pallas kernels: 138 us -> 128 us  [backward(): pl.pallas_call(kernel, out_shape=(sds(pair, BF), sds((rows, 2 * HEAD), F3...]
    slice x2 -> x0, local copies, waits for them, and re-layouts: 8.28 us -> none  [the longest x1 5.05 us: experts(): gate_w = moe_w[:, :rows_in, :FF].reshape(WIDTH, FF)]
  transfers between devices with their start and end apart: 2 -> 1, of which waited for: 0 -> 0; matrix products, arithmetic and copies ran while one was open for 10% -> 3% of each run, Pallas kernels for 24% -> 25%
where the time goes in v4:
time: 675 us; the launch traced here: 668 us
  Pallas kernels  597 us (88%)
  other arithmetic  23.9 us (4%)
  local copies, waits for them, and re-layouts  22.2 us (3%)
  between operations  14.6 us (2%)
  matrix products  10 us (1%)
    pallas_call x1, Pallas kernels, front(): pl.pallas_call(kernel, out_shape=(sds((rows, WIDTH), BF), sds((WIDTH, FIR...  220 us
    pallas_call x1, Pallas kernels, finish_layer(): pl.pallas_call(kernel, out_shape=(sds((block, WIDTH), BF), sds((block, WI...  150 us
    pallas_call x1, Pallas kernels, backward(): pl.pallas_call(kernel, out_shape=(sds(pair, BF), sds((rows, 2 * HEAD), F3...  128 us
    pallas_call x1, Pallas kernels, run_expert(): pl.pallas_call(kernel, grid=(steps,), out_shape=(sds((blocks, tokens, WID...  59.9 us
    pallas_call x1, Pallas kernels, scatter_plane(): pl.pallas_call(kernel, out_shape=jax.ShapeDtypeStruct((rows, cols), F32),...  39.1 us
  transfers between devices with their start and end apart: 1, of which 0 were waited for; matrix products, arithmetic and copies ran while one was open for 3% of the time, Pallas kernels for 25%

profile of v4, /device:TPU:0, one launch (start us, length us, event | category | flops | bytes accessed | tf_op | source)
XLA Modules:
  0.0 667.7 jit_solution(2169395722911580942)
XLA Ops:
  7.3 0.9 copy.49
  8.1 0.8 copy.50
  8.9 0.8 copy.51
  9.7 0.7 fusion.11
  10.4 0.6 convert_element_type.63.ch_ref
  11.0 0.7 slice.66
  11.7 0.7 select_reduce_fusion.1
  12.7 1.0 fusion.9
  13.7 0.7 pad_bitcast_fusion
  14.4 0.8 select_convert_fusion.qs_ref
  15.2 0.6 pad_add_fusion.sg_ref
  15.8 0.8 constant_dynamic-slice_fusion
  16.5 3.2 pad_maximum_fusion.mo_ref
  19.7 1.0 pad_maximum_fusion.3
  20.7 0.8 concatenate.40.pk_ref
  21.5 219.9 %front.1 = (bf16[512,1536]{1,0:T(8,128)(2,1)}, bf16[1536,1152]{1,0:T(8,128)(2,1)}, f32[8,8,256]{2,1,0:T(8,128)}, bf16[512,1536]{1,0:T(8,128)(2,1)}, bf16[2,256,7...) custom-call(bf16[256,1536]{1,0:T(8,128)(2,1)} %st_ref.1, ...), custom_call_target="tpu_custom_call" | custom-call | tf_op jit(solution)/shard_map/front/pallas_call | solution.py:1018
  241.4 0.9 multiply_reduce_fusion.5
  242.5 0.5 compare_convert_fusion.ln_ref
  243.0 4.6 fusion.16
  247.8 1.1 fusion.1.oh_ref
  248.9 0.4 select_reduce_fusion
  249.4 1.2 copy.52.gt_ref
  250.6 59.9 %run_expert.1 = (bf16[8,256,1536]{2,1,0:T(8,128)(2,1)}, bf16[8,256,1664]{2,1,0:T(8,128)(2,1)}, bf16[16,144,1536]{2,1,0:T(8,128)(2,1)}) custom-call(bf16[8,256,1536]{2,1,0:T(8,128)(2,1)} %get-tuple-element.46.h_ref, bf16[8,256,1536]{2,1,0:T(8,128)(2,1)} %get-tuple-element.47.g_ref, bf16[8,192,256]{2,1,0:T(8,128)(2,1)} %fusion.1.oh_ref, ...), custom_call_target="tpu_custom_call" | custom-call | flops 38000001024 | bytes 41943040 | tf_op jit(solution)/shard_map/run_expert/pallas_call | solution.py:1556
  310.5 5.9 copy.53
  316.6 39.1 %scatter_plane.1 = f32[256,1664]{1,0:T(8,128)} custom-call(bf16[8,256,1664]{2,1,0:T(8,128)(2,1)} %get-tuple-element.51.part_ref), custom_call_target="tpu_custom_call" | custom-call | tf_op jit(solution)/shard_map/scatter_plane/pallas_call | solution.py:318
  355.9 0.7 convert_bitcast_fusion
  356.7 0.6 fusion.15
  357.5 1.5 fusion.17
  359.3 1.1 multiply_reduce_fusion.3
  360.4 2.4 multiply_reduce_fusion
  363.0 1.9 fusion.13
  364.9 128.1 %backward.1 = (bf16[2,256,768]{2,1,0:T(8,128)(2,1)}, f32[512,256]{1,0:T(8,128)}, f32[96,768]{1,0:T(8,128)}) custom-call(bf16[2,256,768]{2,1,0:T(8,128)(2,1)} %get-tuple-element.39.q_ref, bf16[16,512,256]{2,1,0:T(8,128)(2,1)} %get-tuple-element.40.kv_ref, bf16[2,256,128]{2,1,0:T(8,128)(2,1)} %select_convert_fusion.qs_ref, s32[2,128]{1,0:T(2,128)} %pad_add_fusion.sg_ref, ...), custom_call_target="tpu_custom_call" | custom-call | tf_op jit(solution)/shard_map/backward/pallas_call | solution.py:1323
  493.0 1.3 fusion.18
  494.3 1.0 maximum_maximum_fusion.sm_ref
  495.3 149.9 %finish_layer.1 = (bf16[256,1536]{1,0:T(8,128)(2,1)}, bf16[256,1536]{1,0:T(8,128)(2,1)}, f32[96,1152]{1,0:T(8,128)}, bf16[96,1152]{1,0:T(8,128)(2,1)}, bf16[96,7...) custom-call(bf16[2,256,768]{2,1,0:T(8,128)(2,1)} %get-tuple-element.53.dq_ref, f32[512,256]{1,0:T(8,128)} %get-tuple-element.54.dkv_ref, ...), custom_call_target="tpu_custom_call" | custom-call | tf_op jit(solution)/shard_map/finish_layer/pallas_call | solution.py:1447
  645.2 1.0 convert_element_type.74
  646.2 0.9 slice_select_fusion.4
  647.1 1.0 slice_select_fusion.1
  648.1 0.7 slice_reduce_fusion
  648.8 4.5 fusion.14
  653.3 1.7 slice.99
  655.1 0.7 copy.57
  655.7 0.9 pad_maximum_fusion.1
  656.6 0.6 pad_maximum_fusion.5
  657.3 0.6 pad_maximum_fusion.6
  657.9 0.9 pad_maximum_fusion.2
  658.8 0.9 copy.60
  659.7 0.9 copy.61
  (51 shorter events, 1.7 us)
Async XLA Ops:
  7.2 5.5 copy-start
  7.2 9.3 %copy-start.5 = (bf16[8,48,1536]{2,1,0:T(8,128)(2,1)S(1)}, bf16[8,48,1536]{2,1,0:T(8,128)(2,1)}, u32[]{:S(2)}) copy-start(bf16[8,48,1536]{2,1,0:T(8,128)(2,1)} %param.26) | copy-start | bytes 3538948
  7.2 488.1 %reduce-scatter.2.cloned.1.call-start = ((), (), s32[]{:S(2)}) async-start(), calls=%async_computation.1 | async-start | bytes 8847360 | tf_op jit(solution)/shard_map/reduce_scatter | solution.py:1793
  316.6 39.1 %copy-start.2 = (f32[256,1536]{1,0:T(8,128)S(1)}, f32[256,1536]{1,0:T(8,128)}, u32[]{:S(2)}) copy-start(f32[256,1536]{1,0:T(8,128)} %get-tuple-element.45.x1_ref) | copy-start | bytes 4718596
  360.4 2.6 copy-start.4
  648.8 4.5 copy-start.3
  653.3 1.7 copy-start.6
  653.3 1.7 copy-start.9
  655.1 3.7 copy-start.8
  656.6 3.0 copy-start.7
  658.8 1.8 copy-start.1
Sparse Core Ops, SparseCore 0:
  310.6 143.3 reduce-scatter.1

commit v5 on v4

--- a/solution.py
+++ b/solution.py
@@ -258,7 +258,7 @@
         return (x * 2 + core) * SEQ + y
 
     def send(self, src, dst, n, device):
-        self.sends.start(src, dst, self.ss.at[n], self.rs.at[n], device)
+        self.sends.later(lambda: (src(), dst(), self.ss.at[n], self.rs.at[n], device))
 
     def take(self, dst, n):
         arrived(dst, self.ss.at[n], self.rs.at[n], self.net.xp)
@@ -266,7 +266,8 @@
     def begin(self):
         net = self.net
         for n, (fx, fy) in enumerate(self.ORDER):
-            self.send(self.part.at[self.place(fx, fy, 1 - net.core)], self.bc.at[n], n, net.cp)
+            src = lambda fx=fx, fy=fy: self.part.at[self.place(fx, fy, 1 - net.core)]
+            self.send(src, lambda n=n: self.bc.at[n], n, net.cp)
 
     def cores(self):
         net, mid = self.net, self.mid
@@ -275,21 +276,21 @@
             own = self.part.at[self.place(fx, fy, net.core)]
             add_into(mid.at[n], [own, self.bc.at[n]], self.rows, self.chunk)
             if n == 0:
-                self.send(mid.at[0, self.lo], self.bx.at[0], 4, net.xp)
-                self.send(mid.at[0, self.hi], self.by.at[0], 5, net.yp)
+                self.send(lambda: mid.at[0, self.lo], lambda: self.bx.at[0], 4, net.xp)
+                self.send(lambda: mid.at[0, self.hi], lambda: self.by.at[0], 5, net.yp)
             if n == 1:
-                self.send(mid.at[1, self.lo], self.bx.at[1], 6, net.xp)
+                self.send(lambda: mid.at[1, self.lo], lambda: self.bx.at[1], 6, net.xp)
             if n == 2:
-                self.send(mid.at[2, self.hi], self.by.at[1], 7, net.yp)
+                self.send(lambda: mid.at[2, self.hi], lambda: self.by.at[1], 7, net.yp)
 
     def turn(self):
         net, mid, second = self.net, self.mid, self.second
         self.take(self.bx.at[0], 4)
         add_into(second.at[0], [mid.at[2, self.lo], self.bx.at[0]], self.half, self.chunk)
-        self.send(second.at[0], self.b2.at[0], 8, net.yp)
+        self.send(lambda: second.at[0], lambda: self.b2.at[0], 8, net.yp)
         self.take(self.by.at[0], 5)
         add_into(second.at[1], [mid.at[1, self.hi], self.by.at[0]], self.half, self.chunk)
-        self.send(second.at[1], self.b2.at[1], 9, net.xp)
+        self.send(lambda: second.at[1], lambda: self.b2.at[1], 9, net.xp)
 
     def final(self, out, more=()):
         mid = self.mid
@@ -1130,21 +1131,23 @@
             self.z_stage(dz)
 
 
-def backward(q, kv, qseg, starts, m, l, ob, mixed, dx1, out_w, part_rows, depth):
+def backward(q, kv, qseg, starts, m, l, ob, mixed, dx1, out_w, mixture, part_rows, depth):
     block = q.shape[1]
     rows = kv.shape[1]
     shards = depth * INNER
 
     def kernel(
-        q_ref, kv_ref, qs_ref, sg_ref, m_ref, l_ref, ob_ref, mix_ref, dx_ref, wf_ref,
-        dq_out, dkv_out, own_out,
+        q_ref, kv_ref, qs_ref, sg_ref, m_ref, l_ref, ob_ref, mix_ref, dx_ref, wf_ref, mx_ref,
+        dq_out, dkv_out, own_out, sum_out,
         dob, do_ref, da, dl, acc, dqs, dkv, wpart, wget, so, ro, sq, rq, sw, rw, *scratch,
     ):
         net = Net(depth)
         mirror = Mirror(net)
         keys = Tally(net, dkv, rows, scratch[:11])
         mine = wpart.at[net.y]
-        outs = Tally(net, mine, part_rows, scratch[11:])
+        outs = Tally(net, mine, part_rows, scratch[11:22])
+        sends = Sends()
+        plane = PlaneScatter(net, sends, mx_ref, block, scratch[22:])
         quarter = shards // 4
 
         def pair_copy(n):
@@ -1189,6 +1192,7 @@
         pl.semaphore_wait(barrier, count)
         for k in range(2):
             heads[k][0].send(do_refs[k])
+        plane.begin()
         wide = QCOLS // 2
         for n in range(4):
             cols = slice((n % 2) * wide, (n % 2 + 1) * wide)
@@ -1200,6 +1204,7 @@
                     ]
             pair_copy(n).start()
         acc[...] = jnp.zeros_like(acc)
+        plane.cores()
         for k in range(2):
             heads[k][0].arrive(lambda: (do_ref.at[k], so.at[k], ro.at[k]))
         for j in range(2):
@@ -1286,6 +1291,10 @@
             def _():
                 keys.z_stage(g)
 
+            @pl.when(u == shards // 2 - 2)
+            def _():
+                plane.turn()
+
             @pl.when(u == shards - 7)
             def _():
                 pair_sum()
@@ -1306,6 +1315,7 @@
                 dqs[j, :, h * HEAD : (h + 1) * HEAD] = (acc[j, h] * SCALE).T.astype(BF)
         for k in range(2):
             backs[k][0].send(dq_refs[k])
+        plane.final(sum_out)
         outs.final(own_out)
         keys.final(dkv_out)
         for k in range(2):
@@ -1315,6 +1325,7 @@
             backs[k][0].sent(dq_refs[k])
         for n in range(4):
             pair_copy(n).wait_send()
+        sends.finish()
         outs.finish()
         keys.finish()
 
@@ -1326,9 +1337,10 @@
             sds(pair, BF),
             sds((rows, 2 * HEAD), F32),
             sds((part_rows, QCOLS), F32),
+            sds((block, WIDTH), BF),
         ),
-        in_specs=[vmem()] * 10,
-        out_specs=(vmem(),) * 3,
+        in_specs=[vmem()] * 11,
+        out_specs=(vmem(),) * 4,
         scratch_shapes=[
             pltpu.VMEM(pair, BF),
             pltpu.VMEM(pair, BF),
@@ -1342,14 +1354,15 @@
         ]
         + dma_sems(2, 2, 2, 2, 4, 4)
         + ShardScatter.scratch(depth, rows, 2 * HEAD)
-        + ShardScatter.scratch(depth, part_rows, QCOLS),
+        + ShardScatter.scratch(depth, part_rows, QCOLS)
+        + PlaneScatter.scratch(block, WIDTH),
         compiler_params=comm_params(8, 60 << 20),
         name="backward",
-    )(q, kv, qseg, starts, m, l, ob, mixed, dx1, out_w)
+    )(q, kv, qseg, starts, m, l, ob, mixed, dx1, out_w, mixture)
 
 
 def finish_layer(
-    dq, dkv, cosine, sine, h1, weights, pair, small, dx1, gain_a, out_own, mixture, x1, moe, depth
+    dq, dkv, cosine, sine, h1, weights, pair, small, dx1, gain_a, out_own, moe, depth
 ):
     block = dx1.shape[0]
     rows = pair.shape[0]
@@ -1358,21 +1371,19 @@
     wide = 384
 
     def kernel(
-        dq_ref, dkv_ref, c_ref, n_ref, h1_ref, w_ref, s_ref, sm_ref, dx_ref, ga_ref, oo_ref, mx_ref, x1_ref, moe_ref,
-        res_out, sg_out, own_out, pair_out, pair_wo, moe_out,
+        dq_ref, dkv_ref, c_ref, n_ref, h1_ref, w_ref, s_ref, sm_ref, dx_ref, ga_ref, oo_ref, moe_ref,
+        sg_out, own_out, pair_out, pair_wo, moe_out,
         raw, part, give, take, low, low_wo, sm, rm, sy, ry, ls, *scratch,
     ):
         net = Net(depth)
         sends = Sends()
         me = net.i * SEQ + net.y
         mine = pltpu.make_async_copy(moe_ref.at[net.i], moe_out.at[me], ls.at[0])
-        work = Tally(net, part, part_rows, scratch[:11])
-        mix = PlaneScatter(net, sends, mx_ref, block, scratch[11:])
+        work = Tally(net, part, part_rows, scratch)
         barrier = pltpu.get_barrier_semaphore()
         for device in net.zpeers() + net.plane():
             pl.semaphore_signal(barrier, inc=1, device_id=device, device_id_type=MESH)
         pl.semaphore_wait(barrier, depth - 1 + E - 1)
-        mix.begin()
         for di in range(1, INNER):
             i = lax.rem(net.i + di, INNER)
             sends.start(
@@ -1390,7 +1401,6 @@
         dk = dkv_ref[:, :HEAD].astype(BF).astype(F32)
         raw[:, QCOLS : QCOLS + HEAD] = turn(dk, cos, sin).astype(BF)
         raw[:, QCOLS + HEAD :] = dkv_ref[:, HEAD:].astype(BF)
-        mix.cores()
         low_wo[...] = oo_ref[...].astype(BF)
         sends.start(low_wo, pair_wo, sy.at[1], ry.at[1], net.yp)
 
@@ -1419,7 +1429,6 @@
                 ]
         work.begin()
         work.far_stages()
-        mix.turn()
         for di in range(1, INNER):
             got = moe_out.at[lax.rem(net.i - di + INNER, INNER) * SEQ + net.y]
             arrived(got, sm.at[di], rm.at[di], net.yp)
@@ -1432,7 +1441,6 @@
         work.final(own_out)
         low[...] = own_out[...].astype(BF)
         sends.start(low, pair_out, sy.at[0], ry.at[0], net.yp)
-        mix.final(res_out, [x1_ref])
         for di in range(INNER):
             n = INNER - 1 + di if di else 0
             got = moe_out.at[lax.rem(net.i - di + INNER, INNER) * SEQ + 1 - net.y]
@@ -1448,14 +1456,13 @@
         kernel,
         out_shape=(
             sds((block, WIDTH), BF),
-            sds((block, WIDTH), BF),
             sds((part_rows, FIRST), F32),
             sds((part_rows, FIRST), BF),
             sds((part_rows, QCOLS), BF),
             sds((E,) + moe.shape[1:], BF),
         ),
-        in_specs=[vmem()] * 13 + [hbm()],
-        out_specs=(vmem(),) * 5 + (hbm(),),
+        in_specs=[vmem()] * 11 + [hbm()],
+        out_specs=(vmem(),) * 4 + (hbm(),),
         scratch_shapes=[
             pltpu.VMEM((rows, QKV), BF),
             pltpu.VMEM((shards, part_rows, FIRST), BF),
@@ -1465,11 +1472,10 @@
             pltpu.VMEM((part_rows, QCOLS), BF),
         ]
         + dma_sems(2 * INNER - 1, 2 * INNER - 1, 3, 3, 1)
-        + ShardScatter.scratch(depth, part_rows, FIRST)
-        + PlaneScatter.scratch(block, WIDTH),
+        + ShardScatter.scratch(depth, part_rows, FIRST),
         compiler_params=comm_params(9, 60 << 20),
         name="finish_layer",
-    )(dq, dkv, cosine, sine, h1, weights, pair, small, dx1, gain_a, out_own, mixture, x1, moe)
+    )(dq, dkv, cosine, sine, h1, weights, pair, small, dx1, gain_a, out_own, moe)
 
 
 def run_expert(h2, out_grad, onehot, gate, lane, moe_w, rows_in, rows_out):
@@ -1775,7 +1781,7 @@
     (
         pair, weights, chosen_all, h1, q, kv, ob, top, total, mixed, x1, h2_plane, out_w, grad_plane, moe_w,
     ) = front(stream, pack, moe_pack, chosen_t, cosine, sine, w_out, out_grad, qseg, starts, depth)
-    extra_w = weights[:, QKV : QKV + EXTRA]
+    extra_w = lax.optimization_barrier(weights[:, QKV : QKV + EXTRA])
     gains = extra_w[:, :2].astype(F32).T
     gain_a, gain_f = gains[0:1], gains[1:2]
     router_w = extra_w[:, 2 : 2 + E]
@@ -1808,13 +1814,15 @@
     gain_f_part = jnp.sum(dh2 * normed, axis=0)
     dx1_low = dx1.astype(BF)
     if depth <= 4:
-        dq_pair, dkv, out_own = backward(
-            q, kv, qseg, starts, top, total, ob, mixed_pair, dx1_low, out_w, rows_in, depth
+        dq_pair, dkv, out_own, mixture = backward(
+            q, kv, qseg, starts, top, total, ob, mixed_pair, dx1_low, out_w, mixture_part, rows_in, depth
         )
     else:
         dq_pair, dkv, out_own = back_apart(
             zig, q, kv, lo, info, top, total, ob, mixed, dx1_low, out_w, rows_in, depth
         )
+        mixture = lax.psum_scatter(mixture_part, ("inner", "seq"), scatter_dimension=0, tiled=False)
+    result = (x1 + mixture.astype(F32)).astype(BF)
     small = jnp.concatenate(
         [
             jnp.zeros((1, WIDTH), F32),
@@ -1824,7 +1832,7 @@
         ],
         axis=0,
     )
-    result, stream_grad, own, peer, peer_out, moe_out = finish_layer(
+    stream_grad, own, peer, peer_out, moe_out = finish_layer(
         dq_pair,
         dkv,
         cosine,
@@ -1836,8 +1844,6 @@
         dx1,
         gain_a,
         out_own,
-        mixture_part,
-        x1,
         moe_own,
         depth,
     )

time: 675 us -> 655 us (0.970)
  Pallas kernels: 597 us -> 577 us
    pallas_call x1, Pallas kernels: 150 us -> 115 us  [finish_layer(): pl.pallas_call(kernel, out_shape=(sds((block, WIDTH), BF), sds((part_rows...]
    pallas_call x1, Pallas kernels: 128 us -> 143 us  [backward(): pl.pallas_call(kernel, out_shape=(sds(pair, BF), sds((rows, 2 * HEAD), F3...]
  transfers between devices with their start and end apart: 1 -> 1, of which waited for: 0 -> 0; matrix products, arithmetic and copies ran while one was open for 3% -> 2% of each run, Pallas kernels for 25% -> 28%
where the time goes in v5:
time: 655 us; the launch traced here: 647 us
  Pallas kernels  577 us (88%)
  other arithmetic  24.2 us (4%)
  local copies, waits for them, and re-layouts  22.3 us (3%)
  between operations  14.6 us (2%)
  matrix products  8.57 us (1%)
    pallas_call x1, Pallas kernels, front(): pl.pallas_call(kernel, out_shape=(sds((rows, WIDTH), BF), sds((WIDTH, FIR...  220 us
    pallas_call x1, Pallas kernels, backward(): pl.pallas_call(kernel, out_shape=(sds(pair, BF), sds((rows, 2 * HEAD), F3...  143 us
    pallas_call x1, Pallas kernels, finish_layer(): pl.pallas_call(kernel, out_shape=(sds((block, WIDTH), BF), sds((part_rows...  115 us
    pallas_call x1, Pallas kernels, run_expert(): pl.pallas_call(kernel, grid=(steps,), out_shape=(sds((blocks, tokens, WID...  60 us
    pallas_call x1, Pallas kernels, scatter_plane(): pl.pallas_call(kernel, out_shape=jax.ShapeDtypeStruct((rows, cols), F32),...  39 us
  transfers between devices with their start and end apart: 1, of which 0 were waited for; matrix products, arithmetic and copies ran while one was open for 2% of the time, Pallas kernels for 28%

profile of v5, /device:TPU:0, one launch (start us, length us, event | category | flops | bytes accessed | tf_op | source)
XLA Modules:
  0.0 646.9 jit_solution(17126550671371069663)
XLA Ops:
  7.3 0.9 copy.49
  8.1 0.8 copy.50
  8.9 0.8 copy.51
  9.7 0.7 fusion.6
  10.4 0.6 convert_element_type.69.ch_ref
  11.0 0.7 slice.66
  11.7 0.7 select_reduce_fusion.1
  12.7 1.0 fusion.4
  13.7 0.7 pad_bitcast_fusion
  14.4 0.8 select_convert_fusion.qs_ref
  15.2 0.6 pad_add_fusion.sg_ref
  15.8 0.8 constant_dynamic-slice_fusion
  16.5 3.2 pad_maximum_fusion.mo_ref
  19.7 1.0 pad_maximum_fusion.3
  20.7 0.8 concatenate.40.pk_ref
  21.5 219.9 %front.1 = (bf16[512,1536]{1,0:T(8,128)(2,1)}, bf16[1536,1152]{1,0:T(8,128)(2,1)}, f32[8,8,256]{2,1,0:T(8,128)}, bf16[512,1536]{1,0:T(8,128)(2,1)}, bf16[2,256,7...) custom-call(bf16[256,1536]{1,0:T(8,128)(2,1)} %st_ref.1, ...), custom_call_target="tpu_custom_call" | custom-call | tf_op jit(solution)/shard_map/front/pallas_call | solution.py:1019
  241.4 0.9 multiply_reduce_fusion.5
  242.5 0.5 compare_convert_fusion.ln_ref
  243.0 5.8 copy.52
  248.8 1.0 slice.88
  249.8 4.5 fusion.16
  254.5 1.1 fusion.1.oh_ref
  255.7 0.4 select_reduce_fusion
  256.1 1.2 copy.53.gt_ref
  257.3 60.0 %run_expert.1 = (bf16[8,256,1536]{2,1,0:T(8,128)(2,1)}, bf16[8,256,1664]{2,1,0:T(8,128)(2,1)}, bf16[16,144,1536]{2,1,0:T(8,128)(2,1)}) custom-call(bf16[8,256,1536]{2,1,0:T(8,128)(2,1)} %get-tuple-element.46.h_ref, bf16[8,256,1536]{2,1,0:T(8,128)(2,1)} %get-tuple-element.47.g_ref, bf16[8,192,256]{2,1,0:T(8,128)(2,1)} %fusion.1.oh_ref, ...), custom_call_target="tpu_custom_call" | custom-call | flops 38000001024 | bytes 41943040 | tf_op jit(solution)/shard_map/run_expert/pallas_call | solution.py:1562
  317.5 39.0 %scatter_plane.1 = f32[256,1664]{1,0:T(8,128)} custom-call(bf16[8,256,1664]{2,1,0:T(8,128)(2,1)} %get-tuple-element.51.part_ref), custom_call_target="tpu_custom_call" | custom-call | tf_op jit(solution)/shard_map/scatter_plane/pallas_call | solution.py:319
  356.7 0.6 fusion.15
  357.6 0.3 fusion.17
  358.2 1.1 multiply_reduce_fusion.3
  359.4 2.2 multiply_reduce_fusion
  361.7 1.9 fusion.13
  363.6 143.4 %backward.1 = (bf16[2,256,768]{2,1,0:T(8,128)(2,1)}, f32[512,256]{1,0:T(8,128)}, f32[96,768]{1,0:T(8,128)}, bf16[256,1536]{1,0:T(8,128)(2,1)}) custom-call(bf16[2,256,768]{2,1,0:T(8,128)(2,1)} %get-tuple-element.40.q_ref, bf16[16,512,256]{2,1,0:T(8,128)(2,1)} %get-tuple-element.41.kv_ref, bf16[2,256,128]{2,1,0:T(8,128)(2,1)} %select_convert_fusion.qs_ref, ...), custom_call_target="tpu_custom_call" | custom-call | tf_op jit(solution)/shard_map/backward/pallas_call | solution.py:1334
  507.0 1.4 fusion.18
  508.4 1.0 maximum_maximum_fusion.sm_ref
  509.4 1.1 add_convert_fusion
  510.5 114.9 %finish_layer.1 = (bf16[256,1536]{1,0:T(8,128)(2,1)}, f32[96,1152]{1,0:T(8,128)}, bf16[96,1152]{1,0:T(8,128)(2,1)}, bf16[96,768]{1,0:T(8,128)(2,1)}, bf16[8,144,1536]{2,1,0:T(8,128)(2,1)}) custom-call(bf16[2,256,768]{2,1,0:T(8,128)(2,1)} %get-tuple-element.55.dq_ref, f32[512,256]{1,0:T(8,128)} %get-tuple-element.56.dkv_ref, ...), custom_call_target="tpu_custom_call" | custom-call | tf_op jit(solution)/shard_map/finish_layer/pallas_call | solution.py:1455
  625.4 1.0 convert_element_type.82
  626.4 0.9 slice_select_fusion.4
  627.2 1.0 slice_select_fusion.1
  628.2 0.7 slice_reduce_fusion
  629.0 4.5 fusion.14
  633.5 1.7 slice.102
  635.3 0.7 copy.57
  635.9 0.9 pad_maximum_fusion.1
  636.8 0.6 pad_maximum_fusion.5
  637.4 0.6 pad_maximum_fusion.6
  638.1 0.9 pad_maximum_fusion.2
  639.0 0.9 copy.59
  (52 shorter events, 1.7 us)
Async XLA Ops:
  7.2 5.5 copy-start
  7.2 9.3 %copy-start.6 = (bf16[8,48,1536]{2,1,0:T(8,128)(2,1)S(1)}, bf16[8,48,1536]{2,1,0:T(8,128)(2,1)}, u32[]{:S(2)}) copy-start(bf16[8,48,1536]{2,1,0:T(8,128)(2,1)} %param.26) | copy-start | bytes 3538948
  7.2 503.3 %reduce-scatter.2.cloned.1.call-start = ((), (), s32[]{:S(2)}) async-start(), calls=%async_computation.1 | async-start | bytes 8847360 | tf_op jit(solution)/shard_map/reduce_scatter | solution.py:1799
  317.5 39.1 %copy-start.2 = (f32[256,1536]{1,0:T(8,128)S(1)}, f32[256,1536]{1,0:T(8,128)}, u32[]{:S(2)}) copy-start(f32[256,1536]{1,0:T(8,128)} %get-tuple-element.39) | copy-start | bytes 4718596
  359.3 2.3 copy-start.4
  507.0 2.4 copy-start.8
  629.0 4.5 copy-start.3
  633.5 1.7 copy-start.5
  633.5 1.7 copy-start.9
  635.3 3.7 copy-start.7
  636.8 3.0 copy-start.1
Sparse Core Ops, SparseCore 0:
  317.4 145.9 reduce-scatter.1

commit v6 on v5

--- a/solution.py
+++ b/solution.py
@@ -1509,13 +1509,17 @@
                 copy.start()
             gu_acc[...] = jnp.zeros_like(gu_acc)
             dn_acc[...] = jnp.zeros_like(dn_acc)
-            for copy in weight_copies():
-                copy.wait()
 
         for b in range(pairs):
             at = slice(b * slots, (b + 1) * slots)
             rows[at, :] = dot(oh_ref[b], h_ref[b]).astype(BF)
             slot_g[at, :] = dot(oh_ref[b], g_ref[b]).astype(BF)
+
+        @pl.when(step == 0)
+        def _():
+            for copy in weight_copies():
+                copy.wait()
+
         gate_col = gt_ref[...].reshape(pairs * slots, 1)
         both = dot(rows[...], gu_w[...])
         pre, up = both[:, :FF], both[:, FF:]

time: 655 us -> 655 us (level)
  no operation moved by 1% of the time
where the time goes in v6:
time: 655 us; the launch traced here: 647 us
  Pallas kernels  577 us (88%)
  other arithmetic  24.2 us (4%)
  local copies, waits for them, and re-layouts  22.3 us (3%)
  between operations  14.6 us (2%)
  matrix products  8.57 us (1%)
    pallas_call x1, Pallas kernels, front(): pl.pallas_call(kernel, out_shape=(sds((rows, WIDTH), BF), sds((WIDTH, FIR...  220 us
    pallas_call x1, Pallas kernels, backward(): pl.pallas_call(kernel, out_shape=(sds(pair, BF), sds((rows, 2 * HEAD), F3...  143 us
    pallas_call x1, Pallas kernels, finish_layer(): pl.pallas_call(kernel, out_shape=(sds((block, WIDTH), BF), sds((part_rows...  115 us
    pallas_call x1, Pallas kernels, run_expert(): pl.pallas_call(kernel, grid=(steps,), out_shape=(sds((blocks, tokens, WID...  60.1 us
    pallas_call x1, Pallas kernels, scatter_plane(): pl.pallas_call(kernel, out_shape=jax.ShapeDtypeStruct((rows, cols), F32),...  39 us
  transfers between devices with their start and end apart: 1, of which 0 were waited for; matrix products, arithmetic and copies ran while one was open for 2% of the time, Pallas kernels for 28%

profile of v6, /device:TPU:0, one launch (start us, length us, event | category | flops | bytes accessed | tf_op | source)
XLA Modules:
  0.0 647.1 jit_solution(11678459928176101546)
XLA Ops:
  7.3 0.9 copy.49
  8.1 0.8 copy.50
  8.9 0.8 copy.51
  9.7 0.7 fusion.6
  10.4 0.6 convert_element_type.69.ch_ref
  11.0 0.7 slice.66
  11.7 0.7 select_reduce_fusion.1
  12.7 1.0 fusion.4
  13.7 0.7 pad_bitcast_fusion
  14.4 0.8 select_convert_fusion.qs_ref
  15.2 0.6 pad_add_fusion.sg_ref
  15.8 0.8 constant_dynamic-slice_fusion
  16.5 3.2 pad_maximum_fusion.mo_ref
  19.7 1.0 pad_maximum_fusion.3
  20.7 0.8 concatenate.40.pk_ref
  21.5 219.9 %front.1 = (bf16[512,1536]{1,0:T(8,128)(2,1)}, bf16[1536,1152]{1,0:T(8,128)(2,1)}, f32[8,8,256]{2,1,0:T(8,128)}, bf16[512,1536]{1,0:T(8,128)(2,1)}, bf16[2,256,7...) custom-call(bf16[256,1536]{1,0:T(8,128)(2,1)} %st_ref.1, ...), custom_call_target="tpu_custom_call" | custom-call | tf_op jit(solution)/shard_map/front/pallas_call | solution.py:1019
  241.4 0.9 multiply_reduce_fusion.5
  242.5 0.5 compare_convert_fusion.ln_ref
  243.0 5.8 copy.52
  248.8 1.0 slice.88
  249.8 4.5 fusion.16
  254.5 1.1 fusion.1.oh_ref
  255.7 0.4 select_reduce_fusion
  256.1 1.2 copy.53.gt_ref
  257.3 60.1 %run_expert.1 = (bf16[8,256,1536]{2,1,0:T(8,128)(2,1)}, bf16[8,256,1664]{2,1,0:T(8,128)(2,1)}, bf16[16,144,1536]{2,1,0:T(8,128)(2,1)}) custom-call(bf16[8,256,1536]{2,1,0:T(8,128)(2,1)} %get-tuple-element.46.h_ref, bf16[8,256,1536]{2,1,0:T(8,128)(2,1)} %get-tuple-element.47.g_ref, bf16[8,192,256]{2,1,0:T(8,128)(2,1)} %fusion.1.oh_ref, ...), custom_call_target="tpu_custom_call" | custom-call | flops 38000001024 | bytes 41943040 | tf_op jit(solution)/shard_map/run_expert/pallas_call | solution.py:1566
  317.6 39.0 %scatter_plane.1 = f32[256,1664]{1,0:T(8,128)} custom-call(bf16[8,256,1664]{2,1,0:T(8,128)(2,1)} %get-tuple-element.51.part_ref), custom_call_target="tpu_custom_call" | custom-call | tf_op jit(solution)/shard_map/scatter_plane/pallas_call | solution.py:319
  356.9 0.6 fusion.15
  357.7 0.3 fusion.17
  358.4 1.1 multiply_reduce_fusion.3
  359.5 2.2 multiply_reduce_fusion
  361.8 1.9 fusion.13
  363.7 143.4 %backward.1 = (bf16[2,256,768]{2,1,0:T(8,128)(2,1)}, f32[512,256]{1,0:T(8,128)}, f32[96,768]{1,0:T(8,128)}, bf16[256,1536]{1,0:T(8,128)(2,1)}) custom-call(bf16[2,256,768]{2,1,0:T(8,128)(2,1)} %get-tuple-element.40.q_ref, bf16[16,512,256]{2,1,0:T(8,128)(2,1)} %get-tuple-element.41.kv_ref, bf16[2,256,128]{2,1,0:T(8,128)(2,1)} %select_convert_fusion.qs_ref, ...), custom_call_target="tpu_custom_call" | custom-call | tf_op jit(solution)/shard_map/backward/pallas_call | solution.py:1334
  507.2 1.4 fusion.18
  508.6 1.0 maximum_maximum_fusion.sm_ref
  509.6 1.1 add_convert_fusion
  510.7 114.9 %finish_layer.1 = (bf16[256,1536]{1,0:T(8,128)(2,1)}, f32[96,1152]{1,0:T(8,128)}, bf16[96,1152]{1,0:T(8,128)(2,1)}, bf16[96,768]{1,0:T(8,128)(2,1)}, bf16[8,144,1536]{2,1,0:T(8,128)(2,1)}) custom-call(bf16[2,256,768]{2,1,0:T(8,128)(2,1)} %get-tuple-element.55.dq_ref, f32[512,256]{1,0:T(8,128)} %get-tuple-element.56.dkv_ref, ...), custom_call_target="tpu_custom_call" | custom-call | tf_op jit(solution)/shard_map/finish_layer/pallas_call | solution.py:1455
  625.5 1.0 convert_element_type.82
  626.5 0.9 slice_select_fusion.4
  627.4 1.0 slice_select_fusion.1
  628.4 0.7 slice_reduce_fusion
  629.2 4.5 fusion.14
  633.7 1.7 slice.102
  635.4 0.7 copy.57
  636.1 0.9 pad_maximum_fusion.1
  636.9 0.6 pad_maximum_fusion.5
  637.6 0.6 pad_maximum_fusion.6
  638.2 0.9 pad_maximum_fusion.2
  639.1 0.9 copy.59
  (52 shorter events, 1.7 us)
Async XLA Ops:
  7.2 5.5 copy-start
  7.2 9.3 %copy-start.6 = (bf16[8,48,1536]{2,1,0:T(8,128)(2,1)S(1)}, bf16[8,48,1536]{2,1,0:T(8,128)(2,1)}, u32[]{:S(2)}) copy-start(bf16[8,48,1536]{2,1,0:T(8,128)(2,1)} %param.26) | copy-start | bytes 3538948
  7.2 503.5 %reduce-scatter.2.cloned.1.call-start = ((), (), s32[]{:S(2)}) async-start(), calls=%async_computation.1 | async-start | bytes 8847360 | tf_op jit(solution)/shard_map/reduce_scatter | solution.py:1803
  317.6 39.0 %copy-start.2 = (f32[256,1536]{1,0:T(8,128)S(1)}, f32[256,1536]{1,0:T(8,128)}, u32[]{:S(2)}) copy-start(f32[256,1536]{1,0:T(8,128)} %get-tuple-element.39) | copy-start | bytes 4718596
  359.5 2.3 copy-start.4
  507.2 2.4 copy-start.8
  629.2 4.5 copy-start.3
  633.7 1.7 copy-start.5
  633.7 1.7 copy-start.9
  635.4 3.7 copy-start.7
  636.9 3.0 copy-start.1
Sparse Core Ops, SparseCore 0:
  317.6 145.9 reduce-scatter.1
